TPU v7x, 32 devices: a whole 2x2x4 slice. The times are simulated.
32 devices in a mesh: shard: 2 (over y), ctx: 4 (over x, core), tp: 4 (over z).
Axes of the slice: x: 2, y: 2, z: 4, core: 2. Of those that a mesh axis runs over, the one named last changes fastest.
Arguments:
- inputs: bfloat16 [2, 4096, 1024], P('shard', 'ctx'), may hold values from -6 to 6
- cotangent: bfloat16 [2, 4096, 1024], P('shard', 'ctx'), may hold values from -6 to 6
- segments: int32 [2, 4096], P('shard'), may hold values from 0 to 4095, as said below
- adapter_index: int32 [2], P('shard'), may hold values from 0 to 7
- query_weight: bfloat16 [1024, 1024], P('shard', 'tp'), may hold values from -0.1875 to 0.1875
- key_value_weight: bfloat16 [2, 1024, 512], P(None, 'shard', 'tp'), may hold values from -0.1875 to 0.1875
- output_weight: bfloat16 [1024, 1024], P('tp', 'shard'), may hold values from -1 to 1
- gate_up_weight: bfloat16 [2, 1024, 4608], P(None, 'shard', 'tp'), may hold values from -0.1875 to 0.1875
- down_weight: bfloat16 [4608, 1024], P('tp', 'shard'), may hold values from -0.09375 to 0.09375
- norm_attn: float32 [1024], replicated, may hold values from 0.5 to 1.5
- norm_ffn: float32 [1024], replicated, may hold values from 0.5 to 1.5
- q_gain: float32 [64], replicated, may hold values from 0.8 to 2
- k_gain: float32 [64], replicated, may hold values from 0.8 to 2
- input_adapter_lower: bfloat16 [8, 1024, 80], replicated, may hold values from -0.1875 to 0.1875
- query_adapter_upper: bfloat16 [8, 16, 1024], P(None, None, 'tp'), may hold values from -0.75 to 0.75
- key_value_adapter_upper: bfloat16 [8, 2, 16, 512], P(None, None, None, 'tp'), may hold values from -0.75 to 0.75
- gate_up_adapter_upper: bfloat16 [8, 2, 16, 4608], P(None, None, None, 'tp'), may hold values from -0.75 to 0.75
- output_adapter_lower: bfloat16 [8, 1024, 16], P(None, 'tp'), may hold values from -1 to 1
- output_adapter_upper: bfloat16 [8, 16, 1024], replicated, may hold values from -0.75 to 0.75
- down_adapter_lower: bfloat16 [8, 4608, 16], P(None, 'tp'), may hold values from -0.09375 to 0.09375
- down_adapter_upper: bfloat16 [8, 16, 1024], replicated, may hold values from -0.75 to 0.75
Outputs:
- outputs: bfloat16 [2, 4096, 1024], P('shard', 'ctx')
- grad_inputs: float32 [2, 4096, 1024], P('shard', 'ctx')
- grad_adapt_in: float32 [8, 1024, 80], P(None, ('shard', 'ctx'))
- grad_b_query: float32 [8, 16, 1024], P(None, None, 'tp')
- grad_b_keyval: float32 [8, 2, 16, 512], P(None, None, None, 'tp')
- grad_b_gateup: float32 [8, 2, 16, 4608], P(None, None, None, 'tp')
- grad_a_out: float32 [8, 1024, 16], P(None, 'tp')
- grad_b_out: float32 [8, 16, 1024], replicated
- grad_a_down: float32 [8, 4608, 16], P(None, 'tp')
- grad_b_down: float32 [8, 16, 1024], replicated
Inputs may be any that keep to these rules, and one draw needn't show every extreme that they name: `segments`: A token's segment number is the position in its packed sequence where its document starts, so numbers never fall along a sequence and begin at 0; the last token is a document of its own; in every sequence one document starts among the first 1024 positions and ends among the last 1024.
All inputs are finite; a program needn't handle non-finite values.
Results may differ from a plain program's by a relative error of at most 0.024.
Values may be sent and summed in bfloat16 or wider, within the bound.
No kernel may reach another device: no remote copies, remote signals or barrier semaphores. Data moves between devices by JAX's collectives and lax.ppermute only.
A program may use at most 192 MiB of HBM per device.

v0:
```python
import jax
import jax.numpy as jnp
from jax import lax
from jax.sharding import PartitionSpec as P

HD = 64
ADAPTER_RANK = 16
ADAPT = 8


EPS = 1e-05
ADAPTER_SCALING = 2.0
THETA = 1000000.0
NEG = -1e30
HIGHEST = lax.Precision.HIGHEST


def in_blocks(shard, dim, devices):
    before, after = (shard.shape[:dim], shard.shape[dim + 1 :])
    return jnp.moveaxis(shard.reshape(*before, devices, -1, *after), dim, 0)


def sent_and_summed(shard, axis, dim):
    devices = lax.axis_size(axis)
    pieces = lax.all_to_all(in_blocks(shard, dim, devices), axis, 0, 0, tiled=True)
    return jnp.sum(pieces.astype(jnp.float32), axis=0)


def rmsnorm(value, gain):
    return value * lax.rsqrt(jnp.mean(value * value, axis=-1, keepdims=True) + EPS) * gain


def rotate(value, cosines, sines):
    half_dim = value.shape[-1] // 2
    first = value[..., :half_dim]
    second = value[..., half_dim:]
    return jnp.concatenate(
        [first * cosines - second * sines, second * cosines + first * sines], axis=-1
    )


def matrix_product(left, right):
    return jnp.dot(left, right, preferred_element_type=jnp.float32)


def interior_rows(left, right):
    return lax.dot_general(
        left, right, (((0,), (0,)), ((), ())), preferred_element_type=jnp.float32
    )


def interior_columns(left, right):
    return lax.dot_general(
        left, right, (((1,), (1,)), ((), ())), preferred_element_type=jnp.float32
    )


def exact_rows(left, right):
    return lax.dot_general(
        left.astype(jnp.float32), right, (((0,), (0,)), ((), ())), precision=HIGHEST
    )


def precise_columns(left, right):
    return lax.dot_general(
        left, right.astype(jnp.float32), (((1,), (1,)), ((), ())), precision=HIGHEST
    )


def select_adapter(table, adapter_slot):
    return lax.dynamic_index_in_dim(table, adapter_slot, 0, keepdims=False)


def body(
    inputs,
    cotangent,
    segments,
    adapter_index,
    query_weight,
    key_value_weight,
    output_weight,
    gate_up_weight,
    down_weight,
    norm_attn,
    norm_ffn,
    q_gain,
    k_gain,
    input_adapter_lower,
    query_adapter_upper,
    key_value_adapter_upper,
    gate_up_adapter_upper,
    output_adapter_lower,
    output_adapter_upper,
    down_adapter_lower,
    down_adapter_upper,
):
    dense_query, dense_key_value, full_out, dense_gate_up, full_down = (
        lax.all_gather(query_weight, "shard", axis=0, tiled=True),
        lax.all_gather(key_value_weight, "shard", axis=1, tiled=True),
        lax.all_gather(output_weight, "shard", axis=1, tiled=True),
        lax.all_gather(gate_up_weight, "shard", axis=1, tiled=True),
        lax.all_gather(down_weight, "shard", axis=1, tiled=True),
    )
    adapter_slot = adapter_index[0]
    adapter_input = select_adapter(input_adapter_lower, adapter_slot)
    adapter_query = select_adapter(query_adapter_upper, adapter_slot)
    adapter_key_value = select_adapter(key_value_adapter_upper, adapter_slot)
    adapter_gate_up = select_adapter(gate_up_adapter_upper, adapter_slot)
    adapter_output_lower = select_adapter(output_adapter_lower, adapter_slot)
    adapter_output_upper = select_adapter(output_adapter_upper, adapter_slot)
    adapter_down_lower = select_adapter(down_adapter_lower, adapter_slot)
    adapter_down_upper = select_adapter(down_adapter_upper, adapter_slot)
    layer_input = inputs[0].astype(jnp.float32)
    tok_rows = layer_input.shape[0]
    ctx_place = lax.axis_index("ctx")
    ctx_count = lax.axis_size("ctx")
    segment = segments[0]
    query_place = ctx_place * tok_rows + jnp.arange(tok_rows, dtype=jnp.int32)
    query_segment = lax.dynamic_slice_in_dim(segment, ctx_place * tok_rows, tok_rows)
    head_count = dense_query.shape[1] // HD
    kv_count = dense_key_value.shape[2] // HD
    group = head_count // kv_count
    scale = HD ** (-0.5)
    half_dim = HD // 2
    inverse = THETA ** (-(jnp.arange(half_dim, dtype=jnp.float32) * 2.0 / HD))
    angles = query_place.astype(jnp.float32)[:, None] * inverse[None, :]
    cosines = jnp.cos(angles)[:, None, :]
    sines = jnp.sin(angles)[:, None, :]
    normalized = rmsnorm(layer_input, norm_attn).astype(jnp.bfloat16)
    narrow_product = matrix_product(normalized, adapter_input[:, : 3 * ADAPTER_RANK]).astype(
        jnp.bfloat16
    )
    query_projected = matrix_product(normalized, dense_query) + ADAPTER_SCALING * matrix_product(
        narrow_product[:, :ADAPTER_RANK], adapter_query
    )
    key_projected = matrix_product(
        normalized, dense_key_value[0]
    ) + ADAPTER_SCALING * matrix_product(
        narrow_product[:, ADAPTER_RANK : 2 * ADAPTER_RANK], adapter_key_value[0]
    )
    value_projected = matrix_product(
        normalized, dense_key_value[1]
    ) + ADAPTER_SCALING * matrix_product(
        narrow_product[:, 2 * ADAPTER_RANK : 3 * ADAPTER_RANK], adapter_key_value[1]
    )

    def shape_heads(query_in, key_in):
        query_out = rotate(
            rmsnorm(query_in.reshape(tok_rows, head_count, HD), q_gain), cosines, sines
        )
        key_out = rotate(rmsnorm(key_in.reshape(tok_rows, kv_count, HD), k_gain), cosines, sines)
        return (query_out, key_out)

    query_heads, key_heads = shape_heads(query_projected, key_projected)
    query_use = query_heads.astype(jnp.bfloat16).reshape(tok_rows, kv_count, group, HD)
    key_use = key_heads.astype(jnp.bfloat16).reshape(tok_rows, kv_count * HD)
    value_use = value_projected.astype(jnp.bfloat16)
    keys_all, values_all = (
        lax.all_gather(key_use, "ctx", axis=0, tiled=True),
        lax.all_gather(value_use, "ctx", axis=0, tiled=True),
    )

    def block_scores(key_block, start):
        block_keys = key_block.reshape(tok_rows, kv_count, HD)
        scores = (
            jnp.einsum("tkgd,skd->kgts", query_use, block_keys, preferred_element_type=jnp.float32)
            * scale
        )
        key_place = start + jnp.arange(tok_rows, dtype=jnp.int32)
        key_segment = lax.dynamic_slice_in_dim(segment, start, tok_rows)
        allowed = (key_place[None, :] <= query_place[:, None]) & (
            key_segment[None, :] == query_segment[:, None]
        )
        return (jnp.where(allowed, scores, NEG), allowed)

    def stats_step(block, carry):
        row_top, row_total = carry
        start = block * tok_rows
        scores, allowed = block_scores(lax.dynamic_slice_in_dim(keys_all, start, tok_rows), start)
        new_top = jnp.maximum(row_top, jnp.max(scores, axis=-1))
        spread = jnp.where(allowed, jnp.exp(scores - new_top[..., None]), 0.0)
        return (new_top, row_total * jnp.exp(row_top - new_top) + jnp.sum(spread, axis=-1))

    stat_shape = (kv_count, group, tok_rows)
    row_top, row_total = lax.fori_loop(
        0,
        ctx_place + 1,
        stats_step,
        (jnp.full(stat_shape, NEG, jnp.float32), jnp.zeros(stat_shape, jnp.float32)),
    )
    log_total = row_top + jnp.log(row_total)

    def value_step(block, acc):
        start = block * tok_rows
        scores, allowed = block_scores(lax.dynamic_slice_in_dim(keys_all, start, tok_rows), start)
        probs = jnp.where(allowed, jnp.exp(scores - log_total[..., None]), 0.0).astype(jnp.bfloat16)
        value_block = lax.dynamic_slice_in_dim(values_all, start, tok_rows).reshape(
            tok_rows, kv_count, HD
        )
        return acc + jnp.einsum(
            "kgts,skd->tkgd", probs, value_block, preferred_element_type=jnp.float32
        )

    attention_mixed = lax.fori_loop(
        0, ctx_place + 1, value_step, jnp.zeros((tok_rows, kv_count, group, HD), jnp.float32)
    )
    attention_mixed = attention_mixed.reshape(tok_rows, head_count * HD)
    mixed_narrow = attention_mixed.astype(jnp.bfloat16)
    out_term = matrix_product(mixed_narrow, full_out)
    compressed_contribution = matrix_product(mixed_narrow, adapter_output_lower)
    output_projection_sum, compressed = (
        lax.psum(out_term.astype(jnp.bfloat16), "tp").astype(jnp.float32),
        lax.psum(compressed_contribution.astype(jnp.bfloat16), "tp").astype(jnp.float32),
    )
    compressed_narrow = compressed.astype(jnp.bfloat16)
    hidden_state = layer_input + (
        output_projection_sum
        + ADAPTER_SCALING * matrix_product(compressed_narrow, adapter_output_upper)
    )
    normalized_second = rmsnorm(hidden_state, norm_ffn).astype(jnp.bfloat16)
    narrow_product_second = matrix_product(
        normalized_second, adapter_input[:, 3 * ADAPTER_RANK :]
    ).astype(jnp.bfloat16)
    gate_values = matrix_product(
        normalized_second, dense_gate_up[0]
    ) + ADAPTER_SCALING * matrix_product(
        narrow_product_second[:, :ADAPTER_RANK], adapter_gate_up[0]
    )
    up_projected = matrix_product(
        normalized_second, dense_gate_up[1]
    ) + ADAPTER_SCALING * matrix_product(
        narrow_product_second[:, ADAPTER_RANK:], adapter_gate_up[1]
    )
    active_slots = (jax.nn.silu(gate_values) * up_projected).astype(jnp.bfloat16)
    down_term = matrix_product(active_slots, full_down)
    compressed_second_contribution = matrix_product(active_slots, adapter_down_lower)
    down_projection_sum, compressed_second = (
        lax.psum(down_term.astype(jnp.bfloat16), "tp").astype(jnp.float32),
        lax.psum(compressed_second_contribution.astype(jnp.bfloat16), "tp").astype(jnp.float32),
    )
    compressed_second_narrow = compressed_second.astype(jnp.bfloat16)
    final_output = hidden_state + (
        down_projection_sum
        + ADAPTER_SCALING * matrix_product(compressed_second_narrow, adapter_down_upper)
    )
    back_query, back_keyval, output_reverse, back_gateup, down_reverse = (
        lax.all_gather(query_weight, "shard", axis=0, tiled=True),
        lax.all_gather(key_value_weight, "shard", axis=1, tiled=True),
        lax.all_gather(output_weight, "shard", axis=1, tiled=True),
        lax.all_gather(gate_up_weight, "shard", axis=1, tiled=True),
        lax.all_gather(down_weight, "shard", axis=1, tiled=True),
    )
    grad_top = cotangent[0].astype(jnp.float32)
    gradient_upper_narrow = grad_top.astype(jnp.bfloat16)
    gradient_compressed_second = ADAPTER_SCALING * interior_columns(
        gradient_upper_narrow, adapter_down_upper
    )
    gradient_active_slots = interior_columns(gradient_upper_narrow, down_reverse) + precise_columns(
        gradient_compressed_second, adapter_down_lower
    )
    grad_down_a = exact_rows(active_slots, gradient_compressed_second)
    unused_silu, silu_back = jax.vjp(
        lambda gate_in, up_in: jax.nn.silu(gate_in) * up_in, gate_values, up_projected
    )
    grad_gate, grad_up = silu_back(gradient_active_slots)
    gate_reverse = grad_gate.astype(jnp.bfloat16)
    up_reverse = grad_up.astype(jnp.bfloat16)
    gradient_gate_up_upper = ADAPTER_SCALING * jnp.stack(
        [
            interior_rows(narrow_product_second[:, :ADAPTER_RANK], gate_reverse),
            interior_rows(narrow_product_second[:, ADAPTER_RANK:], up_reverse),
        ]
    )
    ffn_part = interior_columns(gate_reverse, back_gateup[0]) + interior_columns(
        up_reverse, back_gateup[1]
    )
    feedforward_narrow = ADAPTER_SCALING * jnp.concatenate(
        [
            interior_columns(gate_reverse, adapter_gate_up[0]),
            interior_columns(up_reverse, adapter_gate_up[1]),
        ],
        axis=1,
    )
    feedforward_combined, feedforward_narrow_sum = (
        lax.psum(ffn_part.astype(jnp.bfloat16), "tp").astype(jnp.float32),
        lax.psum(feedforward_narrow.astype(jnp.bfloat16), "tp").astype(jnp.float32),
    )
    gradient_normalized_second = feedforward_combined + precise_columns(
        feedforward_narrow_sum, adapter_input[:, 3 * ADAPTER_RANK :]
    )
    unused_norm_two, norm_two_back = jax.vjp(lambda value: rmsnorm(value, norm_ffn), hidden_state)
    grad_hidden = grad_top + norm_two_back(gradient_normalized_second)[0]
    grad_hidden_low = grad_hidden.astype(jnp.bfloat16)
    result_low = final_output.astype(jnp.bfloat16)
    gradient_hidden_every, result_all, compressed_second_every = (
        grad_hidden_low,
        result_low,
        compressed_second_narrow,
    )
    gradient_down_upper = ADAPTER_SCALING * interior_rows(
        compressed_second_every, gradient_upper_narrow
    )
    gradient_output_upper = ADAPTER_SCALING * interior_rows(
        compressed_narrow, gradient_hidden_every
    )
    gradient_compressed = ADAPTER_SCALING * interior_columns(
        gradient_hidden_every, adapter_output_upper
    )
    grad_out_a = exact_rows(mixed_narrow, gradient_compressed)
    grad_mixed = (
        interior_columns(gradient_hidden_every, output_reverse)
        + precise_columns(gradient_compressed, adapter_output_lower)
    ).astype(jnp.bfloat16)
    grad_mixed = grad_mixed.reshape(tok_rows, kv_count, group, HD)
    delta = jnp.einsum(
        "tkgd,tkgd->kgt",
        grad_mixed.astype(jnp.float32),
        attention_mixed.reshape(tok_rows, kv_count, group, HD),
    )
    back_keys, back_values = (keys_all, values_all)

    def grad_step(block, carry):
        grad_query, grad_keys, grad_values = carry
        start = block * tok_rows
        key_block = lax.dynamic_slice_in_dim(back_keys, start, tok_rows)
        value_block = lax.dynamic_slice_in_dim(back_values, start, tok_rows).reshape(
            tok_rows, kv_count, HD
        )
        scores, allowed = block_scores(key_block, start)
        probs = jnp.where(allowed, jnp.exp(scores - log_total[..., None]), 0.0)
        grad_probs = jnp.einsum(
            "tkgd,skd->kgts", grad_mixed, value_block, preferred_element_type=jnp.float32
        )
        grad_scores = (probs * (grad_probs - delta[..., None])).astype(jnp.bfloat16)
        block_keys = key_block.reshape(tok_rows, kv_count, HD)
        grad_query = (
            grad_query
            + jnp.einsum(
                "kgts,skd->tkgd", grad_scores, block_keys, preferred_element_type=jnp.float32
            )
            * scale
        )
        key_term = (
            jnp.einsum("kgts,tkgd->skd", grad_scores, query_use, preferred_element_type=jnp.float32)
            * scale
        )
        value_term = jnp.einsum(
            "kgts,tkgd->skd",
            probs.astype(jnp.bfloat16),
            grad_mixed,
            preferred_element_type=jnp.float32,
        )
        grad_keys = lax.dynamic_update_slice_in_dim(
            grad_keys, key_term.reshape(tok_rows, kv_count * HD), start, 0
        )
        grad_values = lax.dynamic_update_slice_in_dim(
            grad_values, value_term.reshape(tok_rows, kv_count * HD), start, 0
        )
        return (grad_query, grad_keys, grad_values)

    whole_shape = (tok_rows * ctx_count, kv_count * HD)
    grad_query, grad_keys, grad_values = lax.fori_loop(
        0,
        ctx_place + 1,
        grad_step,
        (
            jnp.zeros((tok_rows, kv_count, group, HD), jnp.float32),
            jnp.zeros(whole_shape, jnp.float32),
            jnp.zeros(whole_shape, jnp.float32),
        ),
    )
    grad_key_mine, grad_value_mine = (
        lax.psum_scatter(
            grad_keys.astype(jnp.bfloat16), "ctx", scatter_dimension=0, tiled=True
        ).astype(jnp.float32),
        lax.psum_scatter(
            grad_values.astype(jnp.bfloat16), "ctx", scatter_dimension=0, tiled=True
        ).astype(jnp.float32),
    )
    key_round = grad_key_mine.astype(jnp.bfloat16)
    value_reverse = grad_value_mine.astype(jnp.bfloat16)
    query_round = grad_query.astype(jnp.bfloat16)
    unused_heads, heads_back = jax.vjp(shape_heads, query_projected, key_projected)
    grad_query_proj, grad_key_proj = heads_back(
        (
            query_round.astype(jnp.float32).reshape(tok_rows, head_count, HD),
            key_round.astype(jnp.float32).reshape(tok_rows, kv_count, HD),
        )
    )
    query_reverse = grad_query_proj.astype(jnp.bfloat16)
    key_reverse = grad_key_proj.astype(jnp.bfloat16)
    gradient_query_upper = ADAPTER_SCALING * interior_rows(
        narrow_product[:, :ADAPTER_RANK], query_reverse
    )
    gradient_key_value_upper = ADAPTER_SCALING * jnp.stack(
        [
            interior_rows(narrow_product[:, ADAPTER_RANK : 2 * ADAPTER_RANK], key_reverse),
            interior_rows(narrow_product[:, 2 * ADAPTER_RANK : 3 * ADAPTER_RANK], value_reverse),
        ]
    )
    attn_part = (
        interior_columns(query_reverse, back_query)
        + interior_columns(key_reverse, back_keyval[0])
        + interior_columns(value_reverse, back_keyval[1])
    )
    attention_narrow = ADAPTER_SCALING * jnp.concatenate(
        [
            interior_columns(query_reverse, adapter_query),
            interior_columns(key_reverse, adapter_key_value[0]),
            interior_columns(value_reverse, adapter_key_value[1]),
        ],
        axis=1,
    )
    attention_combined, attention_narrow_sum = (
        lax.psum(attn_part.astype(jnp.bfloat16), "tp").astype(jnp.float32),
        lax.psum(attention_narrow.astype(jnp.bfloat16), "tp").astype(jnp.float32),
    )
    gradient_normalized = attention_combined + precise_columns(
        attention_narrow_sum, adapter_input[:, : 3 * ADAPTER_RANK]
    )
    unused_norm, norm_back = jax.vjp(lambda value: rmsnorm(value, norm_attn), layer_input)
    grad_layer_in = grad_hidden + norm_back(gradient_normalized)[0]
    grad_in_attn = exact_rows(normalized, attention_narrow_sum)
    grad_in_ffn = exact_rows(normalized_second, feedforward_narrow_sum)
    slot_mask = (jnp.arange(ADAPT, dtype=jnp.int32) == adapter_slot).astype(jnp.float32)

    def place(grad):
        return slot_mask.reshape((ADAPT,) + (1,) * grad.ndim) * grad[None]

    owned = sent_and_summed(
        place(jnp.concatenate([grad_in_attn, grad_in_ffn], axis=1)).astype(jnp.bfloat16),
        ("shard", "ctx"),
        1,
    )
    summed = lax.psum(
        (
            place(gradient_query_upper),
            place(gradient_key_value_upper),
            place(gradient_gate_up_upper),
            place(grad_out_a),
            place(gradient_output_upper),
            place(grad_down_a),
            place(gradient_down_upper),
        ),
        ("shard", "ctx"),
    )
    return (
        result_all[None],
        grad_layer_in[None],
        owned,
        summed[0],
        summed[1],
        summed[2],
        summed[3],
        summed[4],
        summed[5],
        summed[6],
    )


def solution(mesh):
    return jax.shard_map(
        body,
        mesh=mesh,
        in_specs=(
            P("shard", "ctx", None),
            P("shard", "ctx", None),
            P("shard", None),
            P("shard"),
            P("shard", "tp"),
            P(None, "shard", "tp"),
            P("tp", "shard"),
            P(None, "shard", "tp"),
            P("tp", "shard"),
            P(),
            P(),
            P(),
            P(),
            P(),
            P(None, None, "tp"),
            P(None, None, None, "tp"),
            P(None, None, None, "tp"),
            P(None, "tp", None),
            P(),
            P(None, "tp", None),
            P(),
        ),
        out_specs=(
            P("shard", "ctx", None),
            P("shard", "ctx", None),
            P(None, ("shard", "ctx"), None),
            P(None, None, "tp"),
            P(None, None, None, "tp"),
            P(None, None, None, "tp"),
            P(None, "tp", None),
            P(),
            P(None, "tp", None),
            P(),
        ),
        check_vma=False,
    )
```

profile of v0, /device:TPU:0, one launch (start us, length us, event | category | flops | bytes accessed | tf_op | source)
XLA Modules:
  0.0 901.2 jit_solution(12048959421370773161)
XLA Ops:
  8.1 2.2 fusion.51
  10.9 11.9 %all_gather.26 = bf16[2,1024,128]{2,1,0:T(8,128)(2,1)} all-gather(bf16[2,512,128]{2,1,0:T(8,128)(2,1)} %param.32), channel_id=1, replica_groups=mesh['shard'=2,'ctx'=4,'tp'=4] {'shard'}, dimensions={1}, use_global_device_ids=true | all-gather | bytes 786432 | tf_op jit(solution)/shard_map/all_gather | solution.py:99
  22.9 2.5 convolution_convert_fusion.2
  26.2 1.8 fusion.75
  32.3 1.7 fusion.76
  34.8 8.4 all_gather.29
  43.2 8.0 all_gather.30
  56.2 9.7 %while.39 = (s32[]{:T(128)}, f32[2,2,1024]{2,1,0:T(2,128)S(1)}, f32[2,2,1024]{2,1,0:T(2,128)S(1)}, s32[]{:T(128)}, s32[4096]{0:T(1024)S(1)}, /*index=5*/s32[1024...) while((s32[]{:T(128)}, f32[2,2,1024]{2,1,0:T(2,128)S(1)}, ...), condition=%wide.region_6.7_spmd.clone, body=%wide.region_3.6_spmd.clone.sunk | while | flops 573581312 | bytes 38256824 | solution.py:185
  58.7 3.0 fusion.252
  61.8 4.2 select_reduce_fusion.2
  67.6 2.3 copy.69
  71.0 12.2 %while.40 = (s32[]{:T(128)}, f32[1024,2,2,64]{0,3,2,1:T(8,128)}, s32[]{:T(128)}, bf16[4096,128]{0,1:T(8,128)(2,1)}, s32[4096]{0:T(1024)S(1)}, /*index=5*/s32[102...) while((s32[]{:T(128)}, f32[1024,2,2,64]{0,3,2,1:T(8,128)}, ...), condition=%wide.region_8.9_spmd.clone, body=%wide.region_7.8_spmd.clone.sunk | while | flops 1098123264 | bytes 6340803 | solution.py:204
  72.1 2.0 compare_and_fusion.7
  74.0 8.8 fusion.257
  84.5 3.3 convolution_convert_fusion.1
  88.5 2.3 fusion.77
  91.7 18.9 %psum.106 = bf16[1024,16]{0,1:T(8,128)(2,1)S(1)} all-reduce(bf16[1024,16]{0,1:T(8,128)(2,1)S(1)} %convolution_convert_fusion.4), channel_id=1, replica_groups=mesh['shard'=2,'ctx'=4,'tp'=4] {'tp'}, use_global_device_ids=true, to_apply=%region_10.11 | all-reduce | flops 16384 | bytes 65536 | tf_op jit(solution)/shard_map/psum | solution.py:213
  110.6 5.2 fusion.65
  115.8 5.2 convolution_add_fusion
  121.0 114.5 %all-reduce.12.cloned.1.call-done = bf16[1024,1024]{1,0:T(8,128)(2,1)} async-done(((bf16[1024,1024]{1,0:T(8,128)(2,1)}), bf16[1024,1024]{1,0:T(8,128)(2,1)}) %all-reduce.12.cloned.1.call-update) | async-done | bytes 2097168 | tf_op jit(solution)/shard_map/psum | solution.py:212
  235.5 2.8 multiply_reduce_fusion.1
  238.4 2.0 copy-done.2
  241.5 57.1 %all-gather.9.cloned.1.call-done = bf16[2,1024,1152]{2,1,0:T(8,128)(2,1)} async-done(((bf16[2,512,1152]{2,1,0:T(8,128)(2,1)}), bf16[2,1024,1152]{2,1,0:T(8,128)(2,1)}) %all-gather.9.cloned.1.call-update) | async-done | bytes 4718608 | tf_op jit(solution)/shard_map/all_gather | solution.py:101
  298.7 4.5 fusion.70
  303.2 1.7 fusion.45
  305.6 2.9 fusion.68
  308.5 5.2 fusion.49
  317.4 2.9 fusion.67
  320.3 4.1 add_convert_fusion.1
  325.1 89.0 %all-reduce.18.cloned.1.call-done = (bf16[1024,32]{0,1:T(8,128)(2,1)}, bf16[1024,1024]{1,0:T(8,128)(2,1)}) async-done(((bf16[1024,32]{0,1:T(8,128)(2,1)}, bf16[1024,1024]{1,0:T(8,128)(2,1)}), (bf16[1024,32]{0,1:T(8,128)(2,1)}, bf16[1024,1024]{1,0:T(8,128)(2,1)})) %all-reduce.18.cloned.1.call-update) | async-done | bytes 2162704 | tf_op jit(solution)/shard_map/psum | solution.py:286
  414.1 4.0 multiply_reduce_fusion
  421.0 1.6 convolution_multiply_fusion.7
  423.6 2.2 fusion.84
  428.1 37.6 %while.41 = (s32[]{:T(128)}, f32[1024,2,2,64]{0,3,2,1:T(8,128)S(1)}, bf16[4096,128]{0,1:T(8,128)(2,1)}, bf16[4096,128]{0,1:T(8,128)(2,1)}, s32[]{:T(128)}, /*ind...) while((s32[]{:T(128)}, ...), condition=%wide.region_18.19_spmd.clone, body=%wide.region_17.18_spmd.clone.sunk | while | flops 2738620416 | bytes 86327528 | solution.py:362
  431.5 8.2 fusion.268
  439.7 10.9 %fusion.271 = bf16[2,1024,64,1]{1,2,3,0:T(8,128)(2,1)S(1)} fusion(bf16[1024,2,2,64]{0,3,2,1:T(8,128)(2,1)} %get-tuple-element.808, f32[2,1024,1024,2]{2,1,3,0:T(8,128)} %fusion.268, f32[2,2,1024]{2,1,0:T(2,128)S(1)} %get-tuple-element.806, pred[1024,1024]{0,1:T(8,128)(4,1)S(1)} %compare_and_fusion.8), kind=kOutput, calls=%fused_computation.37.clone.1 | convolution fusion | flops 557842432 | bytes 18628608 | tf_op jit(solution)/shard_map/while/body/kgts,tkgd->skd/dot_general | solution.py:347
  450.7 9.5 %fusion.269 = bf16[2,2,1024,1024]{2,3,1,0:T(8,128)(2,1)S(1)} fusion(f32[2,1024,1024,2]{2,1,3,0:T(8,128)} %fusion.268, f32[2,2,1024]{2,1,0:T(2,128)S(1)} %get-tuple-element.809, f32[2,2,1024]{2,1,0:T(2,128)S(1)} %get-tuple-element.806, pred[1024,1024]{0,1:T(8,128)(4,1)S(1)} %compare_and_fusion.8, bf16[1024,2,64,1]{0,2,3,1:T(8,128)(2,1)S(1)} %bitcast.379, ...), kind=kOutput, calls=%fused_computation.31.clone.1 | convolution fusion | flops 566231040 | bytes 27033600 | tf_op jit(solution)/shard_map/while/body/tkgd,skd->kgts/dot_general | solution.py:331
  460.2 2.7 fusion.272
  462.9 1.7 fusion.270
  465.8 2.9 convolution_bitcast_fusion.2
  468.7 3.0 convolution_convert_fusion.5
  471.7 4.1 convolution_convert_fusion
  478.8 2.8 fusion.166
  481.6 119.2 %reduce-scatter.3.cloned.1.call-done = bf16[1024,128]{0,1:T(8,128)(2,1)} async-done(((bf16[4096,128]{0,1:T(8,128)(2,1)}), bf16[1024,128]{0,1:T(8,128)(2,1)}) %reduce-scatter.3.cloned.1.call-update) | async-done | bytes 262160 | tf_op jit(solution)/shard_map/reduce_scatter | solution.py:373
  603.1 2.8 fusion.90
  605.9 22.5 %reduce-scatter.5.cloned.1.call-done = bf16[1024,128]{0,1:T(8,128)(2,1)} async-done(((bf16[4096,128]{0,1:T(8,128)(2,1)}), bf16[1024,128]{0,1:T(8,128)(2,1)}) %reduce-scatter.5.cloned.1.call-update) | async-done | bytes 262160 | tf_op jit(solution)/shard_map/reduce_scatter | solution.py:376
  630.2 5.6 add_convert_fusion
  636.6 2.8 convolution_bitcast_fusion.1
  639.4 21.6 %psum.108 = bf16[1024,16]{0,1:T(8,128)(2,1)} all-reduce(bf16[1024,16]{0,1:T(8,128)(2,1)} %convolution_convert_fusion.5), channel_id=1, replica_groups=mesh['shard'=2,'ctx'=4,'tp'=4] {'tp'}, use_global_device_ids=true, to_apply=%region_13.14 | all-reduce | flops 16384 | bytes 65536 | tf_op jit(solution)/shard_map/psum | solution.py:239
  663.5 2.8 fusion.168
  673.8 121.9 %all-reduce.16.cloned.1.call-done = (bf16[1024,1024]{1,0:T(8,128)(2,1)}, bf16[1024,48]{0,1:T(8,128)(2,1)}, bf16[1024,1024]{1,0:T(8,128)(2,1)}) async-done(((bf16[1024,1024]{1,0:T(8,128)(2,1)}, bf16[1024,48]{0,1:T(8,128)(2,1)}, bf16[1024,1024]{1,0:T(8,128)(2,1)}), (bf16[1024,1024]{1,0:T(8,128)(2,1)}, bf16[1024,48]{0,1:T(8,128)(2,1)}, bf16[1024,1024]{1,0:T(8,128)(2,1)})) %all-reduce.16.cloned.1.call-update) | async-done | bytes 4292624 | tf_op jit(solution)/shard_map/psum | solution.py:238
  795.7 1.7 fusion.160
  798.7 4.6 all-to-all-start
  803.4 2.9 fusion.54
  807.5 3.1 fusion.71
  810.6 2.8 fusion.59
  813.4 20.2 %all-to-all-done = bf16[8,8,128,80]{2,3,1,0:T(8,128)(2,1)} async-done(((bf16[8,8,128,80]{2,3,1,0:T(8,128)(2,1)}), bf16[8,8,128,80]{2,3,1,0:T(8,128)(2,1)}, u32[]{:S(2)}, u32[]{:S(2)}) %all-to-all-start) | async-done | bytes 1310752 | tf_op jit(solution)/shard_map/all_to_all | solution.py:25
  833.6 2.3 convert_reduce_fusion
  835.9 47.3 %all-reduce.14.cloned.1.call-done = (f32[8,16,256]{2,1,0:T(8,128)}, f32[8,2,16,128]{3,2,1,0:T(8,128)}, f32[8,2,16,1152]{3,2,1,0:T(8,128)}, f32[8,256,16]{1,2,0:T...) async-done(((f32[8,16,256]{2,1,0:T(8,128)}, f32[8,2,16,128]{3,2,1,0:T(8,128)}, f32[8,2,16,1152]{3,2,1,0:T(8,128)}, ...) | async-done | bytes 3211280 | tf_op jit(solution)/shard_map/psum | solution.py:435
  883.1 1.7 copy.143
  884.8 1.6 copy.144
  886.4 2.4 copy.145
  888.7 1.6 copy.146
  890.3 1.9 copy.147
  (281 shorter events, 58.4 us)
Async XLA Ops:
  7.2 15.7 %copy-start = (bf16[8,1024,80]{1,2,0:T(8,128)(2,1)S(1)}, bf16[8,1024,80]{1,2,0:T(8,128)(2,1)}, u32[]{:S(2)}) copy-start(bf16[8,1024,80]{1,2,0:T(8,128)(2,1)} %param.40) | copy-start | bytes 3932164
  7.2 18.2 %copy-start.8 = (bf16[1,1024,1024]{2,1,0:T(8,128)(2,1)S(1)}, bf16[1,1024,1024]{2,1,0:T(8,128)(2,1)}, u32[]{:S(2)}) copy-start(bf16[1,1024,1024]{2,1,0:T(8,128)(2,1)} %param.27) | copy-start | bytes 6291460
  7.2 18.2 %copy-start.72 = (f32[1024]{0:T(1024)S(1)}, f32[1024]{0:T(1024)}, u32[]{:S(2)}) copy-start(f32[1024]{0:T(1024)} %param.36) | copy-start | bytes 12292
  7.2 49.0 %all-gather.7.cloned.1.call-start = ((), (), s32[]{:S(2)}) async-start(), calls=%async_computation.4 | async-start | bytes 1310720 | tf_op jit(solution)/shard_map/all_gather | solution.py:159
  10.9 40.3 %copy-start.74 = (f32[1024]{0:T(1024)}, f32[1024]{0:T(1024)S(1)}, u32[]{:S(2)}) copy-start(f32[1024]{0:T(1024)S(1)} %fusion.134) | copy-start | bytes 12292
  25.4 26.8 %copy-start.52 = (bf16[1024,48]{0,1:T(8,128)(2,1)}, bf16[1024,48]{0,1:T(8,128)(2,1)S(1)}, u32[]{:S(2)}) copy-start(bf16[1024,48]{0,1:T(8,128)(2,1)S(1)} %convolution_convert_fusion.2) | copy-start | bytes 294916
  25.4 5.1 copy-start.76
  25.4 6.1 copy-start.35
  29.2 4.8 copy-start.16
  30.5 23.6 %copy-start.29 = (f32[1024,32]{0,1:T(8,128)}, f32[1024,32]{0,1:T(8,128)S(1)}, u32[]{:S(2)}) copy-start(f32[1024,32]{0,1:T(8,128)S(1)} %get-tuple-element.442) | copy-start | bytes 393220
  30.5 23.6 %copy-start.31 = (f32[1024,32]{0,1:T(8,128)}, f32[1024,32]{0,1:T(8,128)S(1)}, u32[]{:S(2)}) copy-start(f32[1024,32]{0,1:T(8,128)S(1)} %get-tuple-element.443) | copy-start | bytes 393220
  31.5 36.1 %all-gather.5.cloned.1.call-start = ((), (), s32[]{:S(2)}) async-start(), calls=%async_computation.3 | async-start | bytes 1310720 | tf_op jit(solution)/shard_map/all_gather | solution.py:160
  34.0 76.6 %all-gather.11.cloned.1.call-start = ((), (), s32[]{:S(2)}) async-start(), calls=%async_computation.7 | async-start | bytes 3538944 | tf_op jit(solution)/shard_map/all_gather | solution.py:102
  34.7 200.7 %all-reduce.12.cloned.1.call-start = ((), (), s32[]{:S(2)}) async-start(), calls=%async_computation.5 | async-start | bytes 4194304 | tf_op jit(solution)/shard_map/psum | solution.py:212
  34.8 19.1 %copy-start.78 = (f32[64]{0:T(128)S(1)}, f32[64]{0:T(128)}, u32[]{:S(2)}) copy-start(f32[64]{0:T(128)} %param.38) | copy-start | bytes 772
  43.2 8.1 copy-start.37
  84.5 6.2 copy-start.23
  87.8 210.8 %all-gather.9.cloned.1.call-start = ((), (), s32[]{:S(2)}) async-start(), calls=%async_computation.6 | async-start | bytes 7077888 | tf_op jit(solution)/shard_map/all_gather | solution.py:101
  88.4 325.7 %all-reduce.18.cloned.1.call-start = ((), (), s32[]{:S(2)}) async-start(), calls=%async_computation.12 | async-start | bytes 4325376 | tf_op jit(solution)/shard_map/psum | solution.py:286
  90.7 25.1 %copy-start.43 = (f32[16,1024]{1,0:T(8,128)}, f32[16,1024]{1,0:T(8,128)S(1)}, u32[]{:S(2)}) copy-start(f32[16,1024]{1,0:T(8,128)S(1)} %fusion.77) | copy-start | bytes 196612
  110.6 124.9 %copy-start.54 = (bf16[1024,16]{0,1:T(8,128)(2,1)}, bf16[1024,16]{0,1:T(8,128)(2,1)S(1)}, u32[]{:S(2)}) copy-start(bf16[1024,16]{0,1:T(8,128)(2,1)S(1)} %psum.106) | copy-start | bytes 98308
  121.0 119.4 %copy-start.68 = (f32[1024]{0:T(1024)S(1)}, f32[1024]{0:T(1024)}, u32[]{:S(2)}) copy-start(f32[1024]{0:T(1024)} %param.37) | copy-start | bytes 12292
  240.8 64.2 %copy-start.12 = (bf16[1024,1024]{1,0:T(8,128)(2,1)}, bf16[1024,1024]{1,0:T(8,128)(2,1)S(1)}, u32[]{:S(2)}) copy-start(bf16[1024,1024]{1,0:T(8,128)(2,1)S(1)} %multiply_convert_fusion.2) | copy-start | bytes 6291460
  241.5 66.9 %copy-start.49 = (bf16[1024,32]{0,1:T(8,128)(2,1)}, bf16[1024,32]{0,1:T(8,128)(2,1)S(1)}, u32[]{:S(2)}) copy-start(bf16[1024,32]{0,1:T(8,128)(2,1)S(1)} %convolution_convert_fusion.3) | copy-start | bytes 196612
  303.2 5.2 slice-start
  313.7 6.6 copy-start.19
  313.7 6.6 copy-start.20
  324.4 276.4 %reduce-scatter.3.cloned.1.call-start = ((), (), s32[]{:S(2)}) async-start(), calls=%async_computation.8 | async-start | bytes 1310720 | tf_op jit(solution)/shard_map/reduce_scatter | solution.py:373
  414.1 4.7 copy-start.10
  414.1 5.4 copy-start.25
  428.1 37.7 %copy-start.50 = (bf16[1024,32]{0,1:T(8,128)(2,1)S(1)}, bf16[1024,32]{0,1:T(8,128)(2,1)}, u32[]{:S(2)}) copy-start(bf16[1024,32]{0,1:T(8,128)(2,1)} %copy-done.49) | copy-start | bytes 196612
  465.7 162.7 %reduce-scatter.5.cloned.1.call-start = ((), (), s32[]{:S(2)}) async-start(), calls=%async_computation.9 | async-start | bytes 1310720 | tf_op jit(solution)/shard_map/reduce_scatter | solution.py:376
  465.8 5.9 copy-start.18
  465.8 5.9 copy-start.81
  471.7 4.2 copy-start.30
  471.7 4.2 copy-start.32
  477.4 318.3 %all-reduce.16.cloned.1.call-start = ((), (), s32[]{:S(2)}) async-start(), calls=%async_computation.11 | async-start | bytes 8585216 | tf_op jit(solution)/shard_map/psum | solution.py:238
  477.7 124.2 %copy-start.17 = (f32[1024,128]{0,1:T(8,128)S(1)}, f32[1024,128]{0,1:T(8,128)}, u32[]{:S(2)}) copy-start(f32[1024,128]{0,1:T(8,128)} %copy-done.16) | copy-start | bytes 1572868
  477.7 124.2 %copy-start.77 = (f32[64]{0:T(128)S(1)}, f32[64]{0:T(128)}, u32[]{:S(2)}) copy-start(f32[64]{0:T(128)} %param.39) | copy-start | bytes 772
  478.8 123.3 %copy-start.67 = (f32[1024,2]{0,1:T(2,128)S(1)}, f32[1024,2]{0,1:T(2,128)}, u32[]{:S(2)}) copy-start(f32[1024,2]{0,1:T(2,128)} %copy-done.66) | copy-start | bytes 24580
  478.8 123.3 %copy-start.65 = (f32[1024,2]{0,1:T(2,128)S(1)}, f32[1024,2]{0,1:T(2,128)}, u32[]{:S(2)}) copy-start(f32[1024,2]{0,1:T(2,128)} %copy-done.64) | copy-start | bytes 24580
  478.8 124.3 %copy-start.36 = (bf16[2,1024,128]{2,1,0:T(8,128)(2,1)S(1)}, bf16[2,1024,128]{2,1,0:T(8,128)(2,1)}, u32[]{:S(2)}) copy-start(bf16[2,1024,128]{2,1,0:T(8,128)(2,1)} %all_gather.26) | copy-start | bytes 1572868
  635.8 26.3 %copy-start.11 = (bf16[1,1024,1024]{2,1,0:T(8,128)(2,1)S(1)}, bf16[1,1024,1024]{2,1,0:T(8,128)(2,1)}, u32[]{:S(2)}) copy-start(bf16[1,1024,1024]{2,1,0:T(8,128)(2,1)} %param.28) | copy-start | bytes 6291460
  635.8 27.7 %copy-start.44 = (f32[16,1024]{1,0:T(8,128)S(1)}, f32[16,1024]{1,0:T(8,128)}, u32[]{:S(2)}) copy-start(f32[16,1024]{1,0:T(8,128)} %copy-done.43) | copy-start | bytes 196612
  635.8 30.4 %copy-start.71 = (f32[8]{0:T(128)S(1)}, f32[8]{0:T(128)}, u32[]{:S(2)}) copy-start(f32[8]{0:T(128)} %compare_convert_fusion) | copy-start | bytes 100
  635.8 32.5 %copy-start.24 = (bf16[1024,2,2,64]{0,3,2,1:T(8,128)(2,1)S(1)}, bf16[1024,2,2,64]{0,3,2,1:T(8,128)(2,1)}, u32[]{:S(2)}) copy-start(bf16[1024,2,2,64]{0,3,2,1:T(8,128)(2,1)} %copy-done.23) | copy-start | bytes 1572868
  635.8 32.5 %copy-start.46 = (f32[1024,16]{0,1:T(8,128)S(1)}, f32[1024,16]{0,1:T(8,128)}, u32[]{:S(2)}) copy-start(f32[1024,16]{0,1:T(8,128)} %copy-done.45) | copy-start | bytes 196612
  635.8 247.3 %all-reduce.14.cloned.1.call-start = ((), (), s32[]{:S(2)}) async-start(), calls=%async_computation.10 | async-start | bytes 6422528 | tf_op jit(solution)/shard_map/psum | solution.py:435
  639.4 30.3 %copy-start.27 = (bf16[1024,4,64]{0,2,1:T(8,128)(2,1)S(1)}, bf16[1024,4,64]{0,2,1:T(8,128)(2,1)}, u32[]{:S(2)}) copy-start(bf16[1024,4,64]{0,2,1:T(8,128)(2,1)} %copy-done.26) | copy-start | bytes 1572868
  660.9 8.7 copy-start.53
  660.9 9.7 %copy-start.6 = (f32[1024,1024]{1,0:T(8,128)S(1)}, f32[1024,1024]{1,0:T(8,128)}, u32[]{:S(2)}) copy-start(f32[1024,1024]{1,0:T(8,128)} %copy-done.5) | copy-start | bytes 12582916
  660.9 9.7 %copy-start.55 = (bf16[1024,16]{0,1:T(8,128)(2,1)S(1)}, bf16[1024,16]{0,1:T(8,128)(2,1)}, u32[]{:S(2)}) copy-start(bf16[1024,16]{0,1:T(8,128)(2,1)} %copy-done.54) | copy-start | bytes 98308
  667.2 5.0 copy-start.13
  667.2 5.0 copy-start.57
  671.0 124.7 %copy-start.9 = (bf16[1,1024,1024]{2,1,0:T(8,128)(2,1)S(1)}, bf16[1,1024,1024]{2,1,0:T(8,128)(2,1)}, u32[]{:S(2)}) copy-start(bf16[1,1024,1024]{2,1,0:T(8,128)(2,1)} %param.27) | copy-start | bytes 6291460
  671.0 124.7 %copy-start.73 = (f32[1024]{0:T(1024)S(1)}, f32[1024]{0:T(1024)}, u32[]{:S(2)}) copy-start(f32[1024]{0:T(1024)} %param.36) | copy-start | bytes 12292
  671.0 124.7 %copy-start.75 = (f32[1024]{0:T(1024)S(1)}, f32[1024]{0:T(1024)}, u32[]{:S(2)}) copy-start(f32[1024]{0:T(1024)} %copy-done.74) | copy-start | bytes 12292
  795.7 7.7 copy-start.42
  795.7 7.7 copy-start.63
  798.7 34.9 %all-to-all-start = ((bf16[8,8,128,80]{2,3,1,0:T(8,128)(2,1)}), bf16[8,8,128,80]{2,3,1,0:T(8,128)(2,1)}, u32[]{:S(2)}, u32[]{:S(2)}) async-start(bf16[8,8,128,80]{2,3,1,0:T(8,128)(2,1)} %multiply_convert_fusion.3), calls=%async_computation.2 | async-start | bytes 2621440 | tf_op jit(solution)/shard_map/all_to_all | solution.py:25
  803.4 4.1 copy-start.39
  810.6 83.2 %copy-start.1 = (bf16[8,1024,80]{1,2,0:T(8,128)(2,1)S(1)}, bf16[8,1024,80]{1,2,0:T(8,128)(2,1)}, u32[]{:S(2)}) copy-start(bf16[8,1024,80]{1,2,0:T(8,128)(2,1)} %param.40) | copy-start | bytes 3932164
  883.1 9.1 %copy-start.47 = (f32[8,1152,16]{1,2,0:T(8,128)S(1)}, f32[8,1152,16]{1,2,0:T(8,128)}, u32[]{:S(2)}) copy-start(f32[8,1152,16]{1,2,0:T(8,128)} %get-tuple-element.823) | copy-start | bytes 1769476
  883.1 9.9 %copy-start.48 = (f32[8,16,1024]{2,1,0:T(8,128)S(1)}, f32[8,16,1024]{2,1,0:T(8,128)}, u32[]{:S(2)}) copy-start(f32[8,16,1024]{2,1,0:T(8,128)} %get-tuple-element.824) | copy-start | bytes 1572868
  (31 other events, 68.0 us)
Sparse Core Ops, SparseCore 0:
  31.6 17.0 all-gather.6
  50.8 16.7 all-gather.4
  69.1 36.0 all-gather.10
  108.0 127.4 all-reduce.11
  237.0 61.6 all-gather.8
  324.6 89.4 all-reduce.17
  465.9 134.8 reduce-scatter.2
  603.5 24.8 reduce-scatter.4
  635.9 159.6 all-reduce.15
  800.8 82.2 all-reduce.13
where the time goes:
time: 908 us; the launch traced here: 901 us
  waiting for transfers between devices  595 us (66%)
  matrix products  148 us (16%)
  blocking collectives  68.8 us (8%)
  other arithmetic  35 us (4%)
  local copies, waits for them, and re-layouts  31.6 us (3%)
  between operations  16.6 us (2%)
    psum x1, waiting for transfers between devices, body(): lax.psum(down_term.astype(jnp.bfloat16), 'tp').astype(jnp.float32)  122 us
    reduce_scatter x1, waiting for transfers between devices, body(): lax.psum_scatter(grad_keys.astype(jnp.bfloat16), 'ctx', scatter_dimension...  119 us
    psum x1, waiting for transfers between devices, body(): lax.psum(out_term.astype(jnp.bfloat16), 'tp').astype(jnp.float32)  114 us
    psum x1, waiting for transfers between devices, body(): lax.psum(feedforward_narrow.astype(jnp.bfloat16), 'tp').astype(jnp.float32)  89 us
    all_gather x1, waiting for transfers between devices, body(): lax.all_gather(gate_up_weight, 'shard', axis=1, tiled=True)  57.1 us
    psum x1, waiting for transfers between devices, body(): lax.psum((place(gradient_query_upper), place(gradient_key_value_upper), p...  47.3 us
    dot_general x18, matrix products, matrix_product(): return jnp.dot(left, right, preferred_element_type=jnp.float32)  41.7 us
    dot_general x14, matrix products, interior_columns(): lax.dot_general(left, right, (((1,), (1,)), ((), ())), preferred_element_...  33.9 us
  transfers between devices with their start and end apart: 11, of which 9 were waited for; matrix products, arithmetic and copies ran while one was open for 11% of the time, Pallas kernels for 0%

commit v1 on v0

v1 whole, which is shorter than its diff:
```python
import functools

import jax
import jax.numpy as jnp
from jax import lax
from jax.experimental import pallas as pl
from jax.experimental.pallas import tpu as pltpu
from jax.sharding import PartitionSpec as P

HD = 64
RANK = 16
ADAPT = 8
EPS = 1e-05
ADAPTER_SCALING = 2.0
THETA = 1000000.0
LOG2E = 1.4426950408889634
SCALE = HD**-0.5
F32 = jnp.float32
BF16 = jnp.bfloat16
VMEM_LIMIT = 40 * 1024 * 1024

CORE = [(i, i ^ 1) for i in range(4)]
XSIDE = [(i, i ^ 2) for i in range(4)]
Z_XOR = {d: [(i, i ^ d) for i in range(4)] for d in (1, 2, 3)}
CT = ("ctx", "tp")
SCT = ("shard", "ctx", "tp")
COLUMN = [[(2 * x + k) * 4 + z for k in range(2) for z in range(4)] for x in range(2)]


def nn(left, right):
    return lax.dot_general(left, right, (((1,), (0,)), ((), ())), preferred_element_type=F32)


def nt(left, right):
    return lax.dot_general(left, right, (((1,), (1,)), ((), ())), preferred_element_type=F32)


def tn(left, right):
    return lax.dot_general(left, right, (((0,), (0,)), ((), ())), preferred_element_type=F32)


def rmsnorm(value, gain):
    return value * lax.rsqrt(jnp.mean(value * value, axis=-1, keepdims=True) + EPS) * gain


def order2(own, other, bit, axis=0):
    return jnp.concatenate(
        [jnp.where(bit == 0, own, other), jnp.where(bit == 0, other, own)], axis=axis
    )


def rows_at(value, block, size, axis=0):
    return lax.dynamic_slice_in_dim(value, block * size, size, axis)


def block_ranges(segment, first_query, query_block, key_base, key_block, key_blocks, queries):
    starts = first_query + jnp.arange(queries // query_block, dtype=jnp.int32) * query_block
    seg_first = segment[starts]
    seg_last = segment[starts + query_block - 1]
    low = jnp.clip((seg_first - key_base) // key_block, 0, key_blocks)
    high = jnp.clip(
        (starts + query_block - key_base + key_block - 1) // key_block, 0, key_blocks
    )
    free_low = jnp.clip((seg_last - key_base + key_block - 1) // key_block, 0, key_blocks)
    free_high = jnp.clip((starts + 1 - key_base) // key_block, 0, key_blocks)
    low = jnp.minimum(low, high)
    free_low = jnp.clip(free_low, low, high)
    free_high = jnp.clip(free_high, free_low, high)
    return jnp.stack([low, free_low, free_high, high]).astype(jnp.int32)


def key_loops(info, i, step, acc):
    low, free_low, free_high, high = info[0, i], info[1, i], info[2, i], info[3, i]
    ahead = free_low - low

    def masked(t, carry):
        j = jnp.where(t < ahead, low + t, free_high + t - ahead)
        return step(j, carry, True)

    acc = lax.fori_loop(0, ahead + high - free_high, masked, acc)
    return lax.fori_loop(free_low, free_high, lambda j, carry: step(j, carry, False), acc)


def fwd_kernel(bq, bk, last, info, base, q_ref, kv_ref, seg_ref, *rest):
    if last:
        acc_in, mixed_ref, low_ref, lse_ref, vx = rest
    else:
        acc_ref, vx = rest
    i = pl.program_id(0)
    keys = kv_ref.shape[0]

    @pl.when(i == 0)
    def _():
        col = lax.broadcasted_iota(jnp.int32, (keys, 2 * HD), 1)
        kv = kv_ref[...]
        swapped = jnp.concatenate([kv[:, HD:], kv[:, :HD]], axis=1)
        ones = jnp.where(col == HD, 1.0, 0.0).astype(BF16)
        vx[...] = jnp.where(col < HD, swapped, ones)

    q = q_ref[...]
    both = jnp.concatenate([q[:, :HD], q[:, HD:]], axis=0)
    q_base, k_base = base[0], base[1]

    def step(j, acc, masked):
        off = pl.multiple_of(j * bk, bk)
        scores = nt(both, kv_ref[pl.ds(off, bk), :HD])
        probs = jnp.exp2(scores * (SCALE * LOG2E))
        if masked:
            qi = q_base + i * bq + lax.broadcasted_iota(jnp.int32, (bq, bk), 0)
            ki = k_base + off + lax.broadcasted_iota(jnp.int32, (bq, bk), 1)
            allowed = (ki <= qi) & (ki >= seg_ref[...])
            probs = jnp.where(jnp.concatenate([allowed, allowed], axis=0), probs, 0.0)
        return acc + nn(probs.astype(BF16), vx[pl.ds(off, bk), :])

    if last:
        acc = jnp.concatenate([acc_in[0], acc_in[1]], axis=0)
    else:
        acc = jnp.zeros((2 * bq, 2 * HD), F32)
    acc = key_loops(info, i, step, acc)
    if last:
        total = acc[:, HD : HD + 1]
        out = acc[:, :HD] / total
        out = jnp.concatenate([out[:bq], out[bq:]], axis=1)
        mixed_ref[...] = out
        low_ref[...] = out.astype(BF16)
        lse = jnp.log2(total)
        lse_ref[...] = jnp.concatenate([lse[:bq], lse[bq:]], axis=1)
    else:
        acc_ref[0] = acc[:bq]
        acc_ref[1] = acc[bq:]


def attention_forward(q, kv, seg, info, base, acc_in=None, bq=256, bk=1024):
    rows, keys = q.shape[0], kv.shape[0]
    last = acc_in is not None
    row = lambda i, *_: (i, 0)
    whole = lambda i, *_: (0, 0)
    heads = lambda i, *_: (0, i, 0)
    in_specs = [
        pl.BlockSpec((bq, 2 * HD), row),
        pl.BlockSpec((keys, 2 * HD), whole),
        pl.BlockSpec((bq, 1), row),
    ]
    args = [q, kv, seg]
    if last:
        in_specs.append(pl.BlockSpec((2, bq, 2 * HD), heads))
        args.append(acc_in)
        out_specs = [
            pl.BlockSpec((bq, 2 * HD), row),
            pl.BlockSpec((bq, 2 * HD), row),
            pl.BlockSpec((bq, 2), row),
        ]
        out_shape = [
            jax.ShapeDtypeStruct((rows, 2 * HD), F32),
            jax.ShapeDtypeStruct((rows, 2 * HD), BF16),
            jax.ShapeDtypeStruct((rows, 2), F32),
        ]
    else:
        out_specs = pl.BlockSpec((2, bq, 2 * HD), heads)
        out_shape = jax.ShapeDtypeStruct((2, rows, 2 * HD), F32)
    area = rows * keys // (1 if last else 2)
    return pl.pallas_call(
        functools.partial(fwd_kernel, bq, bk, last),
        grid_spec=pltpu.PrefetchScalarGridSpec(
            num_scalar_prefetch=2,
            grid=(rows // bq,),
            in_specs=in_specs,
            out_specs=out_specs,
            scratch_shapes=[pltpu.VMEM((keys, 2 * HD), BF16)],
        ),
        out_shape=out_shape,
        compiler_params=pltpu.CompilerParams(vmem_limit_bytes=VMEM_LIMIT),
        cost_estimate=pl.CostEstimate(
            flops=2 * 2 * 2 * 128 * area * 2, bytes_accessed=8 << 20, transcendentals=2 * area
        ),
        name="attn_fwd_last" if last else "attn_fwd_first",
    )(info, base, *args)


def bwd_kernel(bq, bk, first, info, base, q_ref, kv_ref, seg_ref, do_ref, lse_ref, del_ref, *rest):
    if first:
        dq_ref, dkv_ref, dk, dv = rest
    else:
        dq_in, dq_ref, dkv_ref, dk, dv = rest
    i = pl.program_id(0)

    @pl.when(i == 0)
    def _():
        dk[...] = jnp.zeros_like(dk)
        dv[...] = jnp.zeros_like(dv)

    q = q_ref[...]
    do = do_ref[...]
    both = jnp.concatenate([q[:, :HD], q[:, HD:]], axis=0)
    both_do = jnp.concatenate([do[:, :HD], do[:, HD:]], axis=0)
    lse = lse_ref[0]
    delta = del_ref[0]
    q_base, k_base = base[0], base[1]

    def step(j, acc, masked):
        off = pl.multiple_of(j * bk, bk)
        kv = kv_ref[pl.ds(off, bk), :]
        k, v = kv[:, :HD], kv[:, HD:]
        probs = jnp.exp2(nt(k, both) * (SCALE * LOG2E) - lse)
        if masked:
            ki = k_base + off + lax.broadcasted_iota(jnp.int32, (bk, bq), 0)
            qi = q_base + i * bq + lax.broadcasted_iota(jnp.int32, (bk, bq), 1)
            allowed = (ki <= qi) & (ki >= seg_ref[0])
            probs = jnp.where(jnp.concatenate([allowed, allowed], axis=1), probs, 0.0)
        dscores = (probs * (nt(v, both_do) - delta)).astype(BF16)
        dv[pl.ds(off, bk), :] += nn(probs.astype(BF16), both_do)
        dk[pl.ds(off, bk), :] += nn(dscores, both)
        return acc + tn(dscores, k)

    acc = key_loops(info, i, step, jnp.zeros((2 * bq, HD), F32))
    acc = jnp.concatenate([acc[:bq], acc[bq:]], axis=1) * SCALE
    dq_ref[...] = acc if first else dq_in[...] + acc

    @pl.when(i == pl.num_programs(0) - 1)
    def _():
        dkv_ref[...] = jnp.concatenate([dk[...] * SCALE, dv[...]], axis=1).astype(dkv_ref.dtype)


def attention_backward(q, kv, seg, do, lse, delta, info, base, dq_in=None, bq=256, bk=512):
    rows, keys = q.shape[0], kv.shape[0]
    first = dq_in is None
    row = lambda i, *_: (i, 0)
    whole = lambda i, *_: (0, 0)
    flat = lambda i, *_: (i, 0, 0)
    in_specs = [
        pl.BlockSpec((bq, 2 * HD), row),
        pl.BlockSpec((keys, 2 * HD), whole),
        pl.BlockSpec((1, 1, bq), flat),
        pl.BlockSpec((bq, 2 * HD), row),
        pl.BlockSpec((1, 1, 2 * bq), flat),
        pl.BlockSpec((1, 1, 2 * bq), flat),
    ]
    args = [q, kv, seg, do, lse, delta]
    if not first:
        in_specs.append(pl.BlockSpec((bq, 2 * HD), row))
        args.append(dq_in)
    area = rows * keys // (1 if first else 2)
    return pl.pallas_call(
        functools.partial(bwd_kernel, bq, bk, first),
        grid_spec=pltpu.PrefetchScalarGridSpec(
            num_scalar_prefetch=2,
            grid=(rows // bq,),
            in_specs=in_specs,
            out_specs=[pl.BlockSpec((bq, 2 * HD), row), pl.BlockSpec((keys, 2 * HD), whole)],
            scratch_shapes=[pltpu.VMEM((keys, HD), F32), pltpu.VMEM((keys, HD), F32)],
        ),
        out_shape=[
            jax.ShapeDtypeStruct((rows, 2 * HD), F32),
            jax.ShapeDtypeStruct((keys, 2 * HD), BF16 if first else F32),
        ],
        compiler_params=pltpu.CompilerParams(vmem_limit_bytes=VMEM_LIMIT),
        cost_estimate=pl.CostEstimate(
            flops=2 * 5 * 2 * 128 * area * 2, bytes_accessed=8 << 20, transcendentals=2 * area
        ),
        name="attn_bwd_first" if first else "attn_bwd_last",
    )(info, base, *args)


def after(value, *others):
    return lax.optimization_barrier((value, others))[0]


def heads_tokens(value):
    return lax.all_to_all(value, CT, 0, 0, axis_index_groups=COLUMN, tiled=True)


def z_gather(own, z):
    up = {}
    down = {}
    ahead = back = own
    for d in (1, 2, 3):
        ahead = lax.ppermute(ahead, "tp", [(i, i + 1) for i in range(3)])
        back = lax.ppermute(back, "tp", [(i + 1, i) for i in range(3)])
        up[d], down[d] = ahead, back
    out = []
    for place in range(4):
        value = own
        for here in range(4):
            if here < place:
                value = jnp.where(z == here, down[place - here], value)
            elif here > place:
                value = jnp.where(z == here, up[here - place], value)
        out.append(value)
    return out


def body(
    shards,
    inputs,
    cotangent,
    segments,
    adapter_index,
    query_weight,
    key_value_weight,
    output_weight,
    gate_up_weight,
    down_weight,
    norm_attn,
    norm_ffn,
    q_gain,
    k_gain,
    input_adapter_lower,
    query_adapter_upper,
    key_value_adapter_upper,
    gate_up_adapter_upper,
    output_adapter_lower,
    output_adapter_upper,
    down_adapter_lower,
    down_adapter_upper,
):
    ctx = lax.axis_index("ctx")
    x, k = ctx // 2, ctx % 2
    z = lax.axis_index("tp")
    y = lax.axis_index("shard")
    tok = inputs.shape[1]
    half = 2 * tok
    sub = tok // 4
    width = inputs.shape[2]
    slot = adapter_index[0]
    segment = segments[0]
    pair = shards == 2
    swap_y = [(0, 1), (1, 0)]

    def chosen(table):
        return lax.dynamic_index_in_dim(table, slot, 0, keepdims=False)

    def shard_rows(piece, axis):
        if pair:
            return order2(piece, lax.ppermute(piece, "shard", swap_y), y, axis)
        return lax.all_gather(piece, "shard", axis=axis, tiled=True)

    head_q = rows_at(query_weight, k, 2 * HD, 1)
    head_kv = rows_at(key_value_weight, k, HD, 2)
    dense_qkv = shard_rows(jnp.concatenate([head_q, head_kv[0], head_kv[1]], axis=1), 0)
    tokens_other = lax.ppermute(inputs[0], "ctx", CORE)
    out_rows = shard_rows(rows_at(output_weight, k, 2 * HD, 0), 1)
    adapter_in = chosen(input_adapter_lower)
    up_q = rows_at(chosen(query_adapter_upper), k, 2 * HD, 1)
    up_kv = rows_at(chosen(key_value_adapter_upper), k, HD, 2)
    lower_down = chosen(down_adapter_lower)
    upper_down = chosen(down_adapter_upper)
    lower_out = rows_at(chosen(output_adapter_lower), k, 2 * HD, 0)
    upper_out = chosen(output_adapter_upper)
    merged_qkv = (
        dense_qkv.astype(F32)
        + ADAPTER_SCALING
        * jnp.concatenate(
            [
                nn(adapter_in[:, :RANK], up_q),
                nn(adapter_in[:, RANK : 2 * RANK], up_kv[0]),
                nn(adapter_in[:, 2 * RANK : 3 * RANK], up_kv[1]),
            ],
            axis=1,
        )
    ).astype(BF16)

    def quarter(weight):
        if not pair:
            full = lax.all_gather(weight, "shard", axis=1, tiled=True)
            return jnp.where(k == 0, full, lax.ppermute(full, "tp", Z_XOR[2]))

        def over_y(cores):
            return [
                ((s * 4 + c) * 4 + t, ((s ^ 1) * 4 + c) * 4 + t)
                for s in range(2)
                for c in cores
                for t in range(4)
            ]

        piece = rows_at(weight, x, weight.shape[1] // 2, 1)
        piece = lax.ppermute(
            piece, CT, [(c * 4 + t, c * 4 + (t ^ 2)) for c in (1, 3) for t in range(4)]
        )
        mine = lax.ppermute(after(weight, dense_qkv), SCT, over_y((0, 2)))
        piece_x = lax.ppermute(piece, "ctx", [(1, 3), (3, 1)])
        far = order2(piece, piece_x, x, 1)
        far_y = lax.ppermute(far, SCT, over_y((1, 3)))
        return order2(jnp.where(k == 0, weight, far), jnp.where(k == 0, mine, far_y), y, 1)

    frozen = jnp.concatenate([gate_up_weight, down_weight.T[None]], axis=0)
    dense_ffn = quarter(after(frozen, tokens_other))
    small_ffn = jnp.concatenate([chosen(gate_up_adapter_upper), lower_down.T[None]], axis=0)
    small_far = lax.ppermute(after(small_ffn, dense_qkv), "tp", Z_XOR[2])
    small_ffn = jnp.where(k == 0, small_ffn, small_far)
    lower_gate_up = adapter_in[:, 3 * RANK :]
    merged_gate, merged_up, merged_down = (
        (dense_ffn[i].astype(F32) + ADAPTER_SCALING * term).astype(BF16)
        for i, term in enumerate(
            (
                nn(lower_gate_up[:, :RANK], small_ffn[0]),
                nn(lower_gate_up[:, RANK:], small_ffn[1]),
                tn(upper_down, small_ffn[2]),
            )
        )
    )

    out_rows = (out_rows.astype(F32) + ADAPTER_SCALING * nn(lower_out, upper_out)).astype(BF16)
    small_rows = lower_out.reshape(-1, width)
    out_rows = jnp.concatenate(
        [out_rows, small_rows, jnp.zeros((16 - small_rows.shape[0], width), BF16)], axis=0
    )
    out_own = lax.all_gather(out_rows, "tp", axis=0)
    out_own = order2(out_own, lax.ppermute(out_own, "ctx", CORE), k)
    merged_out = out_own[:, : 2 * HD].reshape(-1, width)
    lower_whole = out_own[:, 2 * HD : 2 * HD + small_rows.shape[0]].reshape(-1, RANK)

    tokens = order2(inputs[0], tokens_other, k)
    normalized = rmsnorm(tokens.astype(F32), norm_attn).astype(BF16)
    narrow = nn(normalized, adapter_in[:, : 3 * RANK]).astype(BF16)
    projected = nn(normalized, merged_qkv)
    first_query = x * half
    half_dim = HD // 2
    inverse = THETA ** (-(jnp.arange(half_dim, dtype=F32) * 2.0 / HD))
    places = first_query + jnp.arange(half, dtype=jnp.int32)
    angles = places.astype(F32)[:, None] * inverse[None, :]
    cosines, sines = jnp.cos(angles), jnp.sin(angles)

    def shape_head(value, gain):
        value = rmsnorm(value, gain)
        first, second = value[:, :half_dim], value[:, half_dim:]
        return jnp.concatenate(
            [first * cosines - second * sines, second * cosines + first * sines], axis=1
        )

    def shape_heads(q0, q1, key):
        return shape_head(q0, q_gain), shape_head(q1, q_gain), shape_head(key, k_gain)

    raw = (projected[:, :HD], projected[:, HD : 2 * HD], projected[:, 2 * HD : 3 * HD])
    heads, heads_back = jax.vjp(shape_heads, *raw)
    queries = jnp.concatenate([heads[0], heads[1]], axis=1).astype(BF16)
    keyvals = jnp.concatenate([heads[2], projected[:, 3 * HD :]], axis=1).astype(BF16)
    keyvals_before = lax.ppermute(keyvals, "ctx", [(0, 2), (1, 3)])

    fq, fk, bq, bk = 256, 1024, 256, 512
    base_here = jnp.stack([first_query, first_query]).astype(jnp.int32)
    base_before = jnp.stack([first_query, first_query - half]).astype(jnp.int32)
    segment_here = lax.dynamic_slice_in_dim(segment, first_query, half)

    def info_of(size_q, size_k, key_base):
        return block_ranges(segment, first_query, size_q, key_base, size_k, half // size_k, half)

    seg_col = segment_here[:, None]
    acc = attention_forward(
        queries, keyvals, seg_col, info_of(fq, fk, first_query), base_here, None, fq, fk
    )
    mixed, mixed_low, lse = attention_forward(
        queries,
        keyvals_before,
        seg_col,
        info_of(fq, fk, first_query - half),
        base_before,
        acc,
        fq,
        fk,
    )

    def to_tokens(value):
        arrived = heads_tokens(value.reshape(8, sub, value.shape[1]))
        return jnp.concatenate([arrived[i] for i in range(8)], axis=1)

    mixed_all = to_tokens(mixed_low)
    tokens_own = rows_at(inputs[0], z, sub).astype(F32)
    hidden_state = tokens_own + nn(mixed_all, merged_out)
    normalized_second = rmsnorm(hidden_state, norm_ffn).astype(BF16)

    zbit = z % 2
    second_pair = order2(normalized_second, lax.ppermute(normalized_second, "tp", Z_XOR[1]), zbit)
    second_all = order2(second_pair, lax.ppermute(second_pair, "ctx", CORE), k)
    grad_pair = rows_at(cotangent[0], z // 2, 2 * sub)
    grad_all = order2(grad_pair, lax.ppermute(after(grad_pair, dense_qkv), "ctx", CORE), k)
    gate = nn(second_all, merged_gate)
    up = nn(second_all, merged_up)
    sig = 1.0 / (1.0 + jnp.exp(-gate))
    silu = gate * sig
    active = (silu * up).astype(BF16)
    grad_active = nn(grad_all, merged_down)
    grad_gate = (grad_active * up * (sig + silu * (1.0 - sig))).astype(BF16)
    grad_up = (grad_active * silu).astype(BF16)
    ffn_part = (nt(grad_gate, merged_gate) + nt(grad_up, merged_up)).astype(BF16)

    def summed_to_owner(part):
        mine = rows_at(part, k, 2 * sub).astype(F32)
        arrived = lax.ppermute(rows_at(part, 1 - k, 2 * sub), "ctx", CORE)
        mine = mine + arrived.astype(F32)
        give = rows_at(mine, 1 - zbit, sub).astype(BF16)
        return rows_at(mine, zbit, sub) + lax.ppermute(give, "tp", Z_XOR[1]).astype(F32)

    grad_normalized_second = summed_to_owner(ffn_part)

    grad_own = rows_at(cotangent[0], z, sub).astype(F32)
    unused, norm_two_back = jax.vjp(lambda value: rmsnorm(value, norm_ffn), hidden_state)
    grad_hidden = grad_own + norm_two_back(grad_normalized_second)[0]
    grad_hidden_low = grad_hidden.astype(BF16)
    grad_mixed_all = nt(grad_hidden_low, merged_out).astype(BF16)
    cols = 2 * HD
    grad_mixed = heads_tokens(
        jnp.stack([grad_mixed_all[:, i * cols : (i + 1) * cols] for i in range(8)])
    ).reshape(half, cols)

    active_later, second_later = after((active, second_all), grad_mixed_all)
    down_part = nt(active_later, merged_down).astype(BF16)
    down_sum = summed_to_owner(down_part)
    result = lax.all_gather((hidden_state + down_sum).astype(BF16), "tp", axis=0, tiled=True)
    narrow_second = nn(second_later, lower_gate_up).astype(BF16)
    du2 = ADAPTER_SCALING * jnp.concatenate(
        [nt(grad_gate, small_ffn[0]), nt(grad_up, small_ffn[1])], axis=1
    )
    zd = nt(active_later, small_ffn[2]).astype(BF16)
    dzd = (ADAPTER_SCALING * nt(grad_all, upper_down)).astype(BF16)
    zo = nn(mixed_all, lower_whole).astype(BF16)
    dzo = (ADAPTER_SCALING * nt(grad_hidden_low, upper_out)).astype(BF16)
    wide_grads = jnp.concatenate(
        [
            ADAPTER_SCALING * tn(zo, grad_hidden_low),
            ADAPTER_SCALING * tn(zd, grad_all),
            tn(dzo, mixed_all),
            tn(du2.astype(BF16), second_later),
        ],
        axis=0,
    ).astype(BF16)
    quarter_grads = jnp.concatenate(
        [
            ADAPTER_SCALING * tn(narrow_second[:, :RANK], grad_gate),
            ADAPTER_SCALING * tn(narrow_second[:, RANK:], grad_up),
            tn(dzd, active_later),
        ],
        axis=0,
    ).astype(BF16)

    slots = jnp.arange(ADAPT, dtype=jnp.int32)
    if pair:
        slot_other = lax.ppermute(after(adapter_index, dense_qkv), "shard", swap_y)[0]
        shard_slots = [jnp.where(y == 0, slot, slot_other), jnp.where(y == 0, slot_other, slot)]
    else:
        shard_slots = list(lax.all_gather(adapter_index[0], "shard"))
    kept = min(shards, ADAPT)

    def placed(grads):
        if shards > ADAPT:
            return grads.astype(F32)
        out = 0.0
        for i in range(shards):
            mask = (slots == shard_slots[i]).astype(F32).reshape((ADAPT,) + (1,) * (grads.ndim - 1))
            out = out + mask * grads[i].astype(F32)[None]
        return out

    def by_shard(arrived):
        sums = jnp.sum(
            arrived.astype(F32).reshape((shards, -1) + arrived.shape[1:]), axis=1
        )
        if shards <= ADAPT:
            return sums
        out = 0.0
        for i in range(shards):
            mask = (slots == shard_slots[i]).astype(F32).reshape((ADAPT,) + (1,) * (sums.ndim - 1))
            out = out + mask * sums[i][None]
        return out

    def split_columns(value, parts):
        return jnp.moveaxis(value.reshape(value.shape[0], parts, -1), 1, 0)

    def to_all(value, axes, parts):
        return lax.all_to_all(
            jnp.broadcast_to(value[None], (parts,) + value.shape), axes, 0, 0, tiled=True
        )

    def joined(value):
        value = jnp.moveaxis(value, 0, 2)
        return value.reshape(value.shape[:2] + (-1,))

    devices = shards * 16
    rows_axes = ("shard", "ctx")
    wide_grads, quarter_grads = after((wide_grads, quarter_grads), grad_mixed)
    wide_parts = lax.all_to_all(split_columns(wide_grads, devices), SCT, 0, 0, tiled=True)
    quarter_far = lax.ppermute(quarter_grads, "tp", Z_XOR[2])
    quarter_grads = jnp.where(k == 0, quarter_grads, quarter_far)

    product = grad_mixed.astype(F32) * mixed
    delta = jnp.stack([jnp.sum(product[:, :HD], 1), jnp.sum(product[:, HD:], 1)], axis=1)

    def lanes(value):
        blocks = value.reshape(half // bq, bq, 2).transpose(0, 2, 1)
        return blocks.reshape(half // bq, 1, 2 * bq)

    lse_rows, delta_rows = lanes(lse), lanes(delta)
    seg_rows = segment_here.reshape(half // bq, 1, bq)
    dq_before, dkv_before = attention_backward(
        queries,
        keyvals_before,
        seg_rows,
        grad_mixed,
        lse_rows,
        delta_rows,
        info_of(bq, bk, first_query - half),
        base_before,
        None,
        bq,
        bk,
    )
    dkv_after = lax.ppermute(dkv_before, "ctx", [(2, 0), (3, 1)])
    wide_parts, quarter_grads = after((wide_parts, quarter_grads), dq_before)
    wide_sums = by_shard(wide_parts).astype(BF16)
    wide_all = to_all(wide_sums, SCT, devices)
    quarter_parts = lax.all_to_all(
        split_columns(quarter_grads, shards * 4), rows_axes, 0, 0, tiled=True
    )
    dq, dkv = attention_backward(
        queries,
        keyvals,
        seg_rows,
        grad_mixed,
        lse_rows,
        delta_rows,
        info_of(bq, bk, first_query),
        base_here,
        dq_before,
        bq,
        bk,
    )
    dkv = (dkv + dkv_after.astype(F32)).astype(BF16)
    dq = dq.astype(BF16).astype(F32)
    d_raw = heads_back((dq[:, :HD], dq[:, HD:], dkv[:, :HD].astype(F32)))
    d_projected = jnp.concatenate(
        [d_raw[0].astype(BF16), d_raw[1].astype(BF16), d_raw[2].astype(BF16), dkv[:, HD:]], axis=1
    )

    qkv_own = lax.all_gather(after(merged_qkv, normalized_second).T, "tp", axis=0)
    qkv_all = order2(qkv_own, lax.ppermute(qkv_own, "ctx", CORE), k).reshape(-1, width)
    grad_normalized = nn(to_tokens(d_projected), qkv_all)
    unused, norm_back = jax.vjp(lambda value: rmsnorm(value, norm_attn), tokens_own)
    grad_tokens = (grad_hidden + norm_back(grad_normalized)[0]).astype(BF16)
    grad_inputs = jnp.concatenate(z_gather(grad_tokens, z), axis=0).astype(F32)

    wide_all, quarter_parts = after((wide_all, quarter_parts), d_projected)
    quarter_all = to_all(by_shard(quarter_parts).astype(BF16), rows_axes, shards * 4)
    grad_b_qkv = ADAPTER_SCALING * jnp.concatenate(
        [
            tn(narrow[:, :RANK], d_projected[:, : 2 * HD]),
            tn(narrow[:, RANK : 2 * RANK], d_projected[:, 2 * HD : 3 * HD]),
            tn(narrow[:, 2 * RANK :], d_projected[:, 3 * HD :]),
        ],
        axis=1,
    )
    du1 = ADAPTER_SCALING * jnp.concatenate(
        [
            nt(d_projected[:, : 2 * HD], up_q),
            nt(d_projected[:, 2 * HD : 3 * HD], up_kv[0]),
            nt(d_projected[:, 3 * HD :], up_kv[1]),
        ],
        axis=1,
    )
    in_attn = tn(du1.astype(BF16), normalized).astype(BF16)
    in_parts = lax.all_to_all(split_columns(in_attn, devices), SCT, 0, 0, tiled=True)
    in_all = joined(to_all(by_shard(in_parts).astype(BF16), "tp", 4))
    qkv_parts = to_all(grad_b_qkv.astype(BF16), rows_axes, shards * 4)
    qkv_parts = qkv_parts.reshape(shards, 2, 2, RANK, 4 * HD).astype(F32)
    qkv_sums = jnp.moveaxis(jnp.sum(qkv_parts, axis=1), 0, 1).reshape(2 * shards, RANK, 4 * HD)
    qkv_sums = [by_shard(qkv_sums[i * shards : (i + 1) * shards]) for i in range(2)]
    grad_b_query = jnp.concatenate([part[..., : 2 * HD] for part in qkv_sums], axis=-1)
    grad_b_keyval = jnp.stack(
        [
            jnp.concatenate([part[..., c * HD : (c + 1) * HD] for part in qkv_sums], axis=-1)
            for c in (2, 3)
        ],
        axis=1,
    )
    wide_all = joined(wide_all)
    grad_b_out = wide_all[:, :RANK]
    grad_b_down = wide_all[:, RANK : 2 * RANK]
    grad_a_out = wide_all[:, 2 * RANK : 3 * RANK]
    grad_a_out = jnp.concatenate(
        [rows_at(grad_a_out, z, cols, 2), rows_at(grad_a_out, 4 + z, cols, 2)], axis=2
    )
    own_width = width // (shards * 4)
    in_ffn = rows_at(wide_all[:, 3 * RANK :], y * 4 + ctx, own_width, 2)
    grad_adapt_in = jnp.concatenate([in_all, in_ffn], axis=1)
    quarter_all = joined(quarter_all)
    grad_b_gate_up = quarter_all[:, : 2 * RANK].reshape(kept, 2, RANK, -1)
    grad_a_down = quarter_all[:, 2 * RANK :]
    return (
        result[None],
        grad_inputs[None],
        jnp.swapaxes(placed(grad_adapt_in), 1, 2),
        placed(grad_b_query),
        placed(grad_b_keyval),
        placed(grad_b_gate_up),
        jnp.swapaxes(placed(grad_a_out), 1, 2),
        placed(grad_b_out),
        jnp.swapaxes(placed(grad_a_down), 1, 2),
        placed(grad_b_down),
    )


def solution(mesh):
    return jax.shard_map(
        functools.partial(body, mesh.shape["shard"]),
        mesh=mesh,
        in_specs=(
            P("shard", "ctx", None),
            P("shard", "ctx", None),
            P("shard", None),
            P("shard"),
            P("shard", "tp"),
            P(None, "shard", "tp"),
            P("tp", "shard"),
            P(None, "shard", "tp"),
            P("tp", "shard"),
            P(),
            P(),
            P(),
            P(),
            P(),
            P(None, None, "tp"),
            P(None, None, None, "tp"),
            P(None, None, None, "tp"),
            P(None, "tp", None),
            P(),
            P(None, "tp", None),
            P(),
        ),
        out_specs=(
            P("shard", "ctx", None),
            P("shard", "ctx", None),
            P(None, ("shard", "ctx"), None),
            P(None, None, "tp"),
            P(None, None, None, "tp"),
            P(None, None, None, "tp"),
            P(None, "tp", None),
            P(),
            P(None, "tp", None),
            P(),
        ),
        check_vma=False,
    )
```

time: 908 us -> 615 us (0.68)
  waiting for transfers between devices: 595 us -> 176 us
  starting transfers between devices: 4.98 us -> 138 us
  matrix products: 148 us -> 77.4 us
  blocking collectives: 68.8 us -> 0 us
  other arithmetic: 35 us -> 94 us
  Pallas kernels: 0 us -> 38.3 us
  local copies, waits for them, and re-layouts: 31.6 us -> 63.3 us
    psum x4 -> x0, waiting for transfers between devices: 373 us -> none  [the longest x1 122 us: body(): lax.psum(down_term.astype(jnp.bfloat16), 'tp').astype(jnp.float32)]
    reduce_scatter x2 -> x0, waiting for transfers between devices: 142 us -> none  [the longest x1 119 us: body(): lax.psum_scatter(grad_keys.astype(jnp.bfloat16), 'ctx', scatter_dimension...]
    ppermute x0 -> x27, starting transfers between devices: none -> 93.5 us  [the longest x1 25.8 us: body(): second_all = order2(second_pair, lax.ppermute(second_pair, 'ctx', CORE), k)]
    ppermute x0 -> x27, waiting for transfers between devices: none -> 71.8 us  [the longest x1 26.6 us: body(): dkv_after = lax.ppermute(dkv_before, 'ctx', [(2, 0), (3, 1)])]
    dot_general x54 -> x35, matrix products: 148 us -> 77.4 us  [the longest x14 33.9 us: nn(): lax.dot_general(left, right, (((1,), (0,)), ((), ())), preferred_element_...]
    all_to_all x1 -> x10, waiting for transfers between devices: 20.2 us -> 80.1 us  [the longest x3 48.1 us: heads_tokens(): return lax.all_to_all(value, CT, 0, 0, axis_index_groups=COLUMN, tiled=True)]
    psum x2 -> x0, blocking collectives: 40.5 us -> none  [the longest x1 21.6 us: body(): lax.psum(compressed_second_contribution.astype(jnp.bfloat16), 'tp')]
    all_to_all x1 -> x10, starting transfers between devices: 4.57 us -> 44.1 us  [the longest x4 20.7 us: to_all(): lax.all_to_all(jnp.broadcast_to(value[None], (parts,) + value.shape), axe...]
  transfers between devices with their start and end apart: 11 -> 40, of which waited for: 9 -> 16; matrix products, arithmetic and copies ran while one was open for 11% -> 31% of each run, Pallas kernels for 0% -> 6%
where the time goes in v1:
time: 615 us; the launch traced here: 604 us
  waiting for transfers between devices  176 us (29%)
  starting transfers between devices  138 us (22%)
  other arithmetic  94 us (15%)
  matrix products  77.4 us (13%)
  local copies, waits for them, and re-layouts  63.3 us (10%)
  Pallas kernels  38.3 us (6%)
  between operations  18.1 us (3%)
    all_to_all x3, waiting for transfers between devices, heads_tokens(): return lax.all_to_all(value, CT, 0, 0, axis_index_groups=COLUMN, tiled=True)  48.1 us
    dot_general x14, matrix products, nn(): lax.dot_general(left, right, (((1,), (0,)), ((), ())), preferred_element_...  33.9 us
    unnamed x197, local copies, waits for them, and re-layouts  31.4 us
    ppermute x1, waiting for transfers between devices, body(): dkv_after = lax.ppermute(dkv_before, 'ctx', [(2, 0), (3, 1)])  26.6 us
    ppermute x1, starting transfers between devices, body(): second_all = order2(second_pair, lax.ppermute(second_pair, 'ctx', CORE), k)  25.8 us
    all_gather x1, waiting for transfers between devices, body(): out_own = lax.all_gather(out_rows, 'tp', axis=0)  23.7 us
    dot_general x12, matrix products, tn(): lax.dot_general(left, right, (((0,), (0,)), ((), ())), preferred_element_...  22.1 us
    dot_general x9, matrix products, nt(): lax.dot_general(left, right, (((1,), (1,)), ((), ())), preferred_element_...  21.5 us
  transfers between devices with their start and end apart: 40, of which 16 were waited for; matrix products, arithmetic and copies ran while one was open for 31% of the time, Pallas kernels for 6%

profile of v1, /device:TPU:0, one launch (start us, length us, event | category | flops | bytes accessed | tf_op | source)
XLA Modules:
  0.0 604.5 jit_solution(5386027603207857394)
XLA Ops:
  8.3 3.0 collective-permute-start.3
  24.4 3.8 pad_maximum_fusion.2
  30.9 23.7 %all-gather.8.cloned.1.call-done = bf16[576,1024]{1,0:T(8,128)(2,1)} async-done(((bf16[144,1024]{1,0:T(8,128)(2,1)}), bf16[576,1024]{1,0:T(8,128)(2,1)}) %all-gather.8.cloned.1.call-update) | async-done | bytes 1179664 | tf_op jit(solution)/shard_map/all_gather | solution.py:407
  54.7 2.5 broadcast_select_fusion.7
  70.0 5.4 fusion.55
  75.9 3.8 collective-permute-start.2
  80.4 12.2 %attn_fwd_first.1.rest_0_ = f32[2,2048,128]{2,1,0:T(8,128)S(1)} custom-call(s32[4,8]{1,0:T(4,128)S(1)} %get-tuple-element.169.info, s32[2]{0:T(128)S(1)} %get-tuple-element.173.base, bf16[2048,128]{1,0:T(8,128)(2,1)S(1)} %pad_maximum_fusion.14.q_ref, bf16[2048,128]{1,0:T(8,128)(2,1)S(1)} %pad_maximum_fusion.15.kv_ref, s32[2048,1]{1,0:T(8,128)S(1)} %copy.159.seg_ref), custom_call_target="tpu_custom_call" | custom-call | flops 4294967296 | bytes 8388608 | tf_op jit(solution)/shard_map/attn_fwd_first/pallas_call | solution.py:162
  94.0 5.1 attn_fwd_last.1
  99.2 4.2 all-to-all-start
  103.4 3.4 collective-permute-start.9
  111.5 10.6 %all-to-all-done = bf16[8,256,128]{2,1,0:T(8,128)(2,1)} async-done(((bf16[8,256,128]{2,1,0:T(8,128)(2,1)}), bf16[8,256,128]{2,1,0:T(8,128)(2,1)}, u32[]{:S(2)}, u32[]{:S(2)}) %all-to-all-start) | async-done | bytes 524320 | tf_op jit(solution)/shard_map/all_to_all | solution.py:269
  129.7 2.5 multiply_reduce_fusion.4
  137.3 2.5 collective-permute-start.10
  145.0 21.1 %collective-permute-start.12 = (bf16[512,1024]{1,0:T(8,128)(2,1)}, bf16[512,1024]{1,0:T(8,128)(2,1)}, u32[]{:S(2)}, u32[]{:S(2)}) collective-permute-start(bf16[512,1024]{1,0:T(8,128)(2,1)} %dynamic-slice_bitcast_fusion), channel_id=1, source_target_pairs={{0,4},{4,0},{8,12},{12,8},{1,5},{5,1},{9,13},{13,9},{2,6},{6,2},{1... | collective-permute-start | bytes 3145736 | tf_op jit(solution)/shard_map/ppermute | solution.py:475
  167.6 25.8 %collective-permute-start.6 = (bf16[512,1024]{1,0:T(8,128)(2,1)}, bf16[512,1024]{1,0:T(8,128)(2,1)}, u32[]{:S(2)}, u32[]{:S(2)}) collective-permute-start(bf16[512,1024]{1,0:T(8,128)(2,1)} %pad_maximum_fusion.7), channel_id=1, source_target_pairs={{0,4},{4,0},{8,12},{12,8},{1,5},{5,1},{9,13},{13,9},{2,6},{6,2},{1... | collective-permute-start | bytes 3145736 | tf_op jit(solution)/shard_map/ppermute | solution.py:473
  193.4 3.8 collective-permute-done.25
  199.0 10.7 %collective-permute-done.11 = bf16[3,16,1152]{2,1,0:T(8,128)(2,1)} collective-permute-done((bf16[3,16,1152]{2,1,0:T(8,128)(2,1)S(1)}, bf16[3,16,1152]{2,1,0:T(8,128)(2,1)}, u32[]{:S(2)}, u32[]{:S(2)}) %collective-permute-start.11) | collective-permute-done | bytes 110624 | tf_op jit(solution)/shard_map/ppermute | solution.py:388
  209.8 3.4 broadcast_select_fusion.13
  213.2 3.1 broadcast_select_fusion.15
  217.3 6.7 %broadcast_select_fusion.2 = (bf16[3,512,1152]{2,1,0:T(8,128)(2,1)S(1)}, bf16[3,512,1152]{2,1,0:T(8,128)(2,1)S(1)}) fusion(pred[]{:T(512)S(6)} %eq.44, bf16[3,512,1152]{2,1,0:T(8,128)(2,1)} %pad_maximum_fusion.2, pred[]{:T(512)S(6)} %eq.43, bf16[3,512,1152]{2,1,0:T(8,128)(2,1)} %collective-permute-done.9, bf16[3,512,1152]{2,1,0:T(8,128)(2,1)} %collective-permute-done.10, ...), kind=kLoop, calls=%fused_computation.31 | loop fusion | flops 14155776 | bytes 21233666 | tf_op jit(solution)/shard_map/jit(_where)/select_n | solution.py:48
  227.4 2.9 fusion.207
  230.3 5.4 fusion.206
  235.7 8.0 %multiply_convert_fusion = (bf16[1024,1152]{1,0:T(8,128)(2,1)S(1)}, bf16[1024,1152]{1,0:T(8,128)(2,1)S(1)}, bf16[1024,1152]{1,0:T(8,128)(2,1)}) fusion(f32[1024,1152]{1,0:T(8,128)S(1)} %fusion.207, f32[1024,1152]{1,0:T(8,128)} %fusion.206, bf16[1024,1152]{1,0:T(8,128)(2,1)S(1)} %fusion.8, bf16[512,1024]{1,0:T(8,128)(2,1)S(1)} %copy-done.51, ...), kind=kOutput, calls=%fused_computation.17 | convolution fusion | flops 2436628480 | bytes 20971520 | tf_op jit(solution)/shard_map/dot_general | solution.py:31
  243.7 2.9 fusion.212
  246.6 3.3 add_convert_fusion
  255.5 2.8 pad_maximum_fusion.5
  260.5 2.4 pad_maximum_fusion.1
  267.7 11.4 %collective-permute-done.14 = bf16[256,1024]{1,0:T(8,128)(2,1)S(1)} collective-permute-done((bf16[256,1024]{1,0:T(8,128)(2,1)S(1)}, bf16[256,1024]{1,0:T(8,128)(2,1)S(1)}, u32[]{:S(2)}, u32[]{:S(2)}) %collective-permute-start.14) | collective-permute-done | bytes 524320 | tf_op jit(solution)/shard_map/ppermute | solution.py:491
  285.9 6.6 %convolution_convert_fusion.2 = bf16[1024,1024]{1,0:T(8,128)(2,1)} fusion(bf16[1024,1152]{1,0:T(8,128)(2,1)} %get-tuple-element.36, bf16[1024,1152]{1,0:T(8,128)(2,1)} %copy-done.39), kind=kOutput, calls=%fused_computation.58 | convolution fusion | flops 2416967680 | bytes 6815744 | tf_op jit(solution)/shard_map/dot_general | solution.py:35
  292.5 3.9 fusion.42
  299.7 2.4 convolution_convert_fusion.5
  302.1 2.7 fusion.16
  309.4 3.8 all-to-all-start.1
  313.2 2.4 constant_dynamic-slice_fusion.5
  317.7 3.9 convolution_convert_fusion.1
  322.4 5.6 all-to-all-done.1
  329.9 3.4 all-to-all-start.5
  333.3 2.7 collective-permute-start.26
  336.0 3.6 attn_bwd_first.1
  339.6 17.4 %attn_bwd_last.1 = (f32[2048,128]{1,0:T(8,128)S(1)}, f32[2048,128]{1,0:T(8,128)S(1)}) custom-call(s32[4,8]{1,0:T(4,128)S(1)} %get-tuple-element.170.info, s32[2]{0:T(128)S(1)} %get-tuple-element.173.base, bf16[2048,128]{1,0:T(8,128)(2,1)S(1)} %pad_maximum_fusion.14.q_ref, bf16[2048,128]{1,0:T(8,128)(2,1)S(1)} %copy-done.5, s32[8,1,256]{2,1,0:T(1,128)S(1)} %bitcast.463, ...), custom_call_target="tpu_custom_call" | custom-call | flops 10737418240 | bytes 8388608 | tf_op jit(solution)/shard_map/attn_bwd_last/pallas_call | solution.py:243
  366.6 26.6 %collective-permute-done.17 = bf16[2048,128]{1,0:T(8,128)(2,1)} collective-permute-done((bf16[2048,128]{1,0:T(8,128)(2,1)}, bf16[2048,128]{1,0:T(8,128)(2,1)}, u32[]{:S(2)}, u32[]{:S(2)}) %collective-permute-start.17) | collective-permute-done | bytes 524320 | tf_op jit(solution)/shard_map/ppermute | solution.py:605
  397.4 5.5 fusion.62
  405.1 3.3 fusion.65
  412.5 8.9 %all-to-all-start.8 = ((bf16[8,16,256]{2,1,0:T(8,128)(2,1)}), bf16[8,16,256]{2,1,0:T(8,128)(2,1)S(1)}, u32[]{:S(2)}, u32[]{:S(2)}) async-start(bf16[8,16,256]{2,1,0:T(8,128)(2,1)} %broadcast_in_dim.40), calls=%async_computation.8 | async-start | bytes 131072 | tf_op jit(solution)/shard_map/all_to_all | solution.py:568
  421.4 3.2 convolution_convert_fusion.4
  428.0 4.3 all-to-all-start.3
  432.2 7.9 %all-to-all-done.3 = bf16[32,2,768]{2,1,0:T(2,128)(2,1)S(1)} async-done(((bf16[32,2,768]{2,1,0:T(2,128)(2,1)}), bf16[32,2,768]{2,1,0:T(2,128)(2,1)S(1)}, u32[]{:S(2)}, u32[]{:S(2)}) %all-to-all-start.3) | async-done | bytes 98336 | tf_op jit(solution)/shard_map/all_to_all | solution.py:658
  440.2 3.4 all-to-all-start.7
  444.6 5.1 all-to-all-done.7
  449.7 3.3 all-to-all-start.4
  453.1 5.5 all-to-all-done.4
  459.5 2.6 all-to-all-start.6
  463.0 13.5 %all-to-all-done.6 = bf16[32,2,80,32]{2,3,1,0:T(8,128)(2,1)S(1)} async-done(((bf16[32,2,80,32]{2,3,1,0:T(8,128)(2,1)}), bf16[32,2,80,32]{2,3,1,0:T(8,128)(2,1)S(1)}, u32[]{:S(2)}, u32[]{:S(2)}) %all-to-all-start.6) | async-done | bytes 327712 | tf_op jit(solution)/shard_map/all_to_all | solution.py:568
  476.5 4.2 all-to-all-start.2
  481.6 2.4 add_convert_fusion.2
  487.6 32.0 %all-to-all-done.2 = bf16[8,256,256]{2,1,0:T(8,128)(2,1)} async-done(((bf16[8,256,256]{2,1,0:T(8,128)(2,1)}), bf16[8,256,256]{2,1,0:T(8,128)(2,1)}, u32[]{:S(2)}, u32[]{:S(2)}) %all-to-all-start.2) | async-done | bytes 1048608 | tf_op jit(solution)/shard_map/all_to_all | solution.py:269
  520.3 6.0 all-to-all-start.9
  533.7 3.7 fusion.70
  539.8 9.3 %collective-permute-start.19 = (bf16[256,1024]{1,0:T(8,128)(2,1)}, bf16[256,1024]{1,0:T(8,128)(2,1)S(1)}, u32[]{:S(2)}, u32[]{:S(2)}) collective-permute-start(bf16[256,1024]{1,0:T(8,128)(2,1)} %fusion.69), channel_id=1, source_target_pairs={{0,1},{1,2},{2,3},{4,5},{5,6},{6,7},{8,9},{9,10},{10,11},{12,13},{... | collective-permute-start | bytes 1572872 | tf_op jit(solution)/shard_map/ppermute | solution.py:277
  560.8 5.5 collective-permute-start.20
  567.2 8.9 %collective-permute-done.23 = bf16[256,1024]{1,0:T(8,128)(2,1)S(1)} collective-permute-done((bf16[256,1024]{1,0:T(8,128)(2,1)S(1)}, bf16[256,1024]{1,0:T(8,128)(2,1)S(1)}, u32[]{:S(2)}, u32[]{:S(2)}) %collective-permute-start.23) | collective-permute-done | bytes 524320 | tf_op jit(solution)/shard_map/ppermute | solution.py:278
  577.5 5.4 collective-permute-start.21
  584.1 7.0 %collective-permute-done.24 = bf16[256,1024]{1,0:T(8,128)(2,1)S(1)} collective-permute-done((bf16[256,1024]{1,0:T(8,128)(2,1)S(1)}, bf16[256,1024]{1,0:T(8,128)(2,1)S(1)}, u32[]{:S(2)}, u32[]{:S(2)}) %collective-permute-start.24) | collective-permute-done | bytes 524320 | tf_op jit(solution)/shard_map/ppermute | solution.py:278
  593.6 2.5 maximum_convert_fusion
  (413 shorter events, 151.7 us)
Async XLA Ops:
  7.2 12.3 %copy-start = (bf16[8,1024,80]{1,2,0:T(8,128)(2,1)S(1)}, bf16[8,1024,80]{1,2,0:T(8,128)(2,1)}, u32[]{:S(2)}) copy-start(bf16[8,1024,80]{1,2,0:T(8,128)(2,1)} %param.34) | copy-start | bytes 3932164
  7.2 8.0 %copy-start.10 = (s32[1,4096]{1,0:T(1,128)S(1)}, s32[1,4096]{1,0:T(1,128)}, u32[]{:S(2)}) copy-start(s32[1,4096]{1,0:T(1,128)} %param.23) | copy-start | bytes 49156
  7.2 47.4 %all-gather.8.cloned.1.call-start = ((), (), s32[]{:S(2)}) async-start(), calls=%async_computation.11 | async-start | bytes 1474560 | tf_op jit(solution)/shard_map/all_gather | solution.py:407
  8.3 11.2 %collective-permute-start.3 = (bf16[128,512]{1,0:T(8,128)(2,1)S(1)}, bf16[128,512]{1,0:T(8,128)(2,1)S(1)}, u32[]{:S(2)}, u32[]{:S(2)}) collective-permute-start(bf16[128,512]{1,0:T(8,128)(2,1)S(1)} %constant_dynamic-slice_fusion.9), channel_id=1, source_target_pairs={{0,16},{16,0},{1,17},{17,1},{2,18},{18,2},{3,19},{19,3},{4,20},{20... | collective-permute-start | bytes 393224 | tf_op jit(solution)/shard_map/ppermute | solution.py:334
  14.4 15.3 %collective-permute-start.1 = (bf16[512,256]{0,1:T(8,128)(2,1)}, bf16[512,256]{0,1:T(8,128)(2,1)}, u32[]{:S(2)}, u32[]{:S(2)}) collective-permute-start(bf16[512,256]{0,1:T(8,128)(2,1)} %pad_maximum_fusion.17), channel_id=1, source_target_pairs={{0,16},{16,0},{1,17},{17,1},{2,18},{18,2},{3,19},{19,3},{4,20},{20... | collective-permute-start | bytes 786440 | tf_op jit(solution)/shard_map/ppermute | solution.py:334
  14.4 40.2 %collective-permute-start = (bf16[1024,1024]{1,0:T(8,128)(2,1)}, bf16[1024,1024]{1,0:T(8,128)(2,1)}, u32[]{:S(2)}, u32[]{:S(2)}) collective-permute-start(bf16[1024,1024]{1,0:T(8,128)(2,1)} %bitcast.472), channel_id=1, source_target_pairs={{0,4},{4,0},{8,12},{12,8},{1,5},{5,1},{9,13},{13,9},{2,6},{6,2},{1... | collective-permute-start | bytes 6291464 | tf_op jit(solution)/shard_map/ppermute | solution.py:340
  19.5 9.1 %copy-start.48 = (bf16[1024,80]{0,1:T(8,128)(2,1)}, bf16[1024,80]{0,1:T(8,128)(2,1)S(1)}, u32[]{:S(2)}) copy-start(bf16[1024,80]{0,1:T(8,128)(2,1)S(1)} %dynamic-slice_bitcast_fusion.1) | copy-start | bytes 491524
  28.2 41.8 %copy-start.81 = (f32[32]{0:T(128)}, f32[32]{0:T(128)S(1)}, u32[]{:S(2)}) copy-start(f32[32]{0:T(128)S(1)} %negate_power_fusion) | copy-start | bytes 388
  28.6 51.8 %copy-start.2 = (s32[2048,1]{1,0:T(8,128)}, s32[2048,1]{1,0:T(8,128)S(1)}, u32[]{:S(2)}) copy-start(s32[2048,1]{1,0:T(8,128)S(1)} %copy.159.seg_ref) | copy-start | bytes 24580
  30.9 29.6 %copy-start.46 = (bf16[1024,256]{0,1:T(8,128)(2,1)}, bf16[1024,256]{0,1:T(8,128)(2,1)S(1)}, u32[]{:S(2)}) copy-start(bf16[1024,256]{0,1:T(8,128)(2,1)S(1)} %fusion.73) | copy-start | bytes 1572868
  54.7 52.2 %collective-permute-start.4 = (bf16[4,144,1024]{2,1,0:T(8,128)(2,1)}, bf16[4,144,1024]{2,1,0:T(8,128)(2,1)}, u32[]{:S(2)}, u32[]{:S(2)}) collective-permute-start(bf16[4,144,1024]{2,1,0:T(8,128)(2,1)} %bitcast.480), channel_id=1, source_target_pairs={{0,4},{4,0},{8,12},{12,8},{1,5},{5,1},{9,13},{13,9},{2,6},{6,2},{1... | collective-permute-start | bytes 3538952 | tf_op jit(solution)/shard_map/ppermute | solution.py:408
  66.7 56.2 %collective-permute-start.7 = (bf16[3,256,1152]{2,1,0:T(8,128)(2,1)}, bf16[3,256,1152]{2,1,0:T(8,128)(2,1)}, u32[]{:S(2)}, u32[]{:S(2)}) collective-permute-start(bf16[3,256,1152]{2,1,0:T(8,128)(2,1)} %constant_dynamic-slice_fusion.7), channel_id=1, source_target_pairs={{4,6},{5,7},{6,4},{7,5},{12,14},{13,15},{14,12},{15,13},{20,22},{2... | collective-permute-start | bytes 5308424 | tf_op jit(solution)/shard_map/ppermute | solution.py:376
  75.8 16.8 %copy-start.4 = (bf16[2048,128]{1,0:T(8,128)(2,1)}, bf16[2048,128]{1,0:T(8,128)(2,1)S(1)}, u32[]{:S(2)}) copy-start(bf16[2048,128]{1,0:T(8,128)(2,1)S(1)} %pad_maximum_fusion.15.kv_ref) | copy-start | bytes 1572868
  75.9 16.7 %collective-permute-start.2 = (bf16[2048,128]{1,0:T(8,128)(2,1)S(1)}, bf16[2048,128]{1,0:T(8,128)(2,1)S(1)}, u32[]{:S(2)}, u32[]{:S(2)}) collective-permute-start(bf16[2048,128]{1,0:T(8,128)(2,1)S(1)} %pad_maximum_fusion.15.kv_ref), channel_id=1, source_target_pairs={{0,8},{4,12},{1,9},{5,13},{2,10},{6,14},{3,11},{7,15},{16,24},{20,... | collective-permute-start | bytes 1572872 | tf_op jit(solution)/shard_map/ppermute | solution.py:437
  99.2 22.9 %all-to-all-start = ((bf16[8,256,128]{2,1,0:T(8,128)(2,1)}), bf16[8,256,128]{2,1,0:T(8,128)(2,1)}, u32[]{:S(2)}, u32[]{:S(2)}) async-start(bf16[8,256,128]{2,1,0:T(8,128)(2,1)} %bitcast.19), calls=%async_computation | async-start | bytes 1048576 | tf_op jit(solution)/shard_map/all_to_all | solution.py:269
  103.4 113.0 %all-gather.10.cloned.1.call-start = ((), (), s32[]{:S(2)}) async-start(), calls=%async_computation.12 | async-start | bytes 2621440 | tf_op jit(solution)/shard_map/all_gather | solution.py:632
  103.4 113.9 %collective-permute-start.9 = (bf16[3,512,1152]{2,1,0:T(8,128)(2,1)}, bf16[3,512,1152]{2,1,0:T(8,128)(2,1)}, u32[]{:S(2)}, u32[]{:S(2)}) collective-permute-start(bf16[3,512,1152]{2,1,0:T(8,128)(2,1)} %pad_maximum_fusion.2), channel_id=1, source_target_pairs={{0,16},{1,17},{2,18},{3,19},{8,24},{9,25},{10,26},{11,27},{16,0},{... | collective-permute-start | bytes 10616840 | tf_op jit(solution)/shard_map/ppermute | solution.py:379
  122.9 9.3 %collective-permute-start.8 = (bf16[3,256,1152]{2,1,0:T(8,128)(2,1)}, bf16[3,256,1152]{2,1,0:T(8,128)(2,1)S(1)}, u32[]{:S(2)}, u32[]{:S(2)}) collective-permute-start(bf16[3,256,1152]{2,1,0:T(8,128)(2,1)} %collective-permute-done.7), channel_id=1, source_target_pairs={{4,12},{12,4},{5,13},{13,5},{6,14},{14,6},{7,15},{15,7},{20,28},{2... | collective-permute-start | bytes 5308424 | tf_op jit(solution)/shard_map/ppermute | solution.py:380
  132.2 7.6 %copy-start.73 = (f32[256]{0:T(256)}, f32[256]{0:T(256)S(1)}, u32[]{:S(2)}) copy-start(f32[256]{0:T(256)S(1)} %get-tuple-element.165) | copy-start | bytes 3076
  132.2 7.6 %copy-start.13 = (f32[256,1024]{1,0:T(8,128)}, f32[256,1024]{1,0:T(8,128)S(1)}, u32[]{:S(2)}) copy-start(f32[256,1024]{1,0:T(8,128)S(1)} %get-tuple-element.166) | copy-start | bytes 3145732
  137.3 80.0 %collective-permute-start.10 = (bf16[3,512,1152]{2,1,0:T(8,128)(2,1)}, bf16[3,512,1152]{2,1,0:T(8,128)(2,1)}, u32[]{:S(2)}, u32[]{:S(2)}) collective-permute-start(bf16[3,512,1152]{2,1,0:T(8,128)(2,1)} %pad_maximum_fusion.3), channel_id=1, source_target_pairs={{4,20},{5,21},{6,22},{7,23},{12,28},{13,29},{14,30},{15,31},{20,4}... | collective-permute-start | bytes 10616840 | tf_op jit(solution)/shard_map/ppermute | solution.py:382
  140.9 25.2 %copy-start.14 = (f32[256,1024]{1,0:T(8,128)S(1)}, f32[256,1024]{1,0:T(8,128)}, u32[]{:S(2)}) copy-start(f32[256,1024]{1,0:T(8,128)} %copy-done.13) | copy-start | bytes 3145732
  144.1 22.0 %collective-permute-start.5 = (bf16[256,1024]{1,0:T(8,128)(2,1)}, bf16[256,1024]{1,0:T(8,128)(2,1)S(1)}, u32[]{:S(2)}, u32[]{:S(2)}) collective-permute-start(bf16[256,1024]{1,0:T(8,128)(2,1)} %multiply_convert_fusion.3), channel_id=1, source_target_pairs={{0,1},{1,0},{2,3},{3,2},{4,5},{5,4},{6,7},{7,6},{8,9},{9,8},{10,11... | collective-permute-start | bytes 1572872 | tf_op jit(solution)/shard_map/ppermute | solution.py:472
  145.0 64.8 %collective-permute-start.12 = (bf16[512,1024]{1,0:T(8,128)(2,1)}, bf16[512,1024]{1,0:T(8,128)(2,1)}, u32[]{:S(2)}, u32[]{:S(2)}) collective-permute-start(bf16[512,1024]{1,0:T(8,128)(2,1)} %dynamic-slice_bitcast_fusion), channel_id=1, source_target_pairs={{0,4},{4,0},{8,12},{12,8},{1,5},{5,1},{9,13},{13,9},{2,6},{6,2},{1... | collective-permute-start | bytes 3145736 | tf_op jit(solution)/shard_map/ppermute | solution.py:475
  166.4 27.0 %copy-start.31 = (bf16[256,1024]{1,0:T(8,128)(2,1)}, bf16[256,1024]{1,0:T(8,128)(2,1)S(1)}, u32[]{:S(2)}) copy-start(bf16[256,1024]{1,0:T(8,128)(2,1)S(1)} %get-tuple-element.109) | copy-start | bytes 1572868
  166.4 27.0 %copy-start.33 = (bf16[256,1024]{1,0:T(8,128)(2,1)}, bf16[256,1024]{1,0:T(8,128)(2,1)S(1)}, u32[]{:S(2)}) copy-start(bf16[256,1024]{1,0:T(8,128)(2,1)S(1)} %get-tuple-element.110) | copy-start | bytes 1572868
  167.6 45.6 %collective-permute-start.6 = (bf16[512,1024]{1,0:T(8,128)(2,1)}, bf16[512,1024]{1,0:T(8,128)(2,1)}, u32[]{:S(2)}, u32[]{:S(2)}) collective-permute-start(bf16[512,1024]{1,0:T(8,128)(2,1)} %pad_maximum_fusion.7), channel_id=1, source_target_pairs={{0,4},{4,0},{8,12},{12,8},{1,5},{5,1},{9,13},{13,9},{2,6},{6,2},{1... | collective-permute-start | bytes 3145736 | tf_op jit(solution)/shard_map/ppermute | solution.py:473
  193.4 3.9 collective-permute-start.25
  197.2 12.5 %collective-permute-start.11 = (bf16[3,16,1152]{2,1,0:T(8,128)(2,1)S(1)}, bf16[3,16,1152]{2,1,0:T(8,128)(2,1)}, u32[]{:S(2)}, u32[]{:S(2)}) collective-permute-start(bf16[3,16,1152]{2,1,0:T(8,128)(2,1)S(1)} %pad_maximum_fusion.19), channel_id=1, source_target_pairs={{0,2},{1,3},{2,0},{3,1},{4,6},{5,7},{6,4},{7,5},{8,10},{9,11},{10,... | collective-permute-start | bytes 331784 | tf_op jit(solution)/shard_map/ppermute | solution.py:388
  198.5 14.7 %copy-start.32 = (bf16[256,1024]{1,0:T(8,128)(2,1)S(1)}, bf16[256,1024]{1,0:T(8,128)(2,1)}, u32[]{:S(2)}) copy-start(bf16[256,1024]{1,0:T(8,128)(2,1)} %copy-done.31) | copy-start | bytes 1572868
  198.5 14.7 %copy-start.34 = (bf16[256,1024]{1,0:T(8,128)(2,1)S(1)}, bf16[256,1024]{1,0:T(8,128)(2,1)}, u32[]{:S(2)}) copy-start(bf16[256,1024]{1,0:T(8,128)(2,1)} %copy-done.33) | copy-start | bytes 1572868
  216.3 7.7 %copy-start.49 = (bf16[1024,80]{0,1:T(8,128)(2,1)S(1)}, bf16[1024,80]{0,1:T(8,128)(2,1)}, u32[]{:S(2)}) copy-start(bf16[1024,80]{0,1:T(8,128)(2,1)} %copy-done.48) | copy-start | bytes 491524
  216.3 42.0 %collective-permute-start.18 = (bf16[4,256,1024]{2,1,0:T(8,128)(2,1)}, bf16[4,256,1024]{2,1,0:T(8,128)(2,1)}, u32[]{:S(2)}, u32[]{:S(2)}) collective-permute-start(bf16[4,256,1024]{2,1,0:T(8,128)(2,1)} %bitcast.477), channel_id=1, source_target_pairs={{0,4},{4,0},{8,12},{12,8},{1,5},{5,1},{9,13},{13,9},{2,6},{6,2},{1... | collective-permute-start | bytes 6291464 | tf_op jit(solution)/shard_map/ppermute | solution.py:633
  227.4 8.3 %copy-start.39 = (bf16[1024,1152]{1,0:T(8,128)(2,1)}, bf16[1024,1152]{1,0:T(8,128)(2,1)S(1)}, u32[]{:S(2)}) copy-start(bf16[1024,1152]{1,0:T(8,128)(2,1)S(1)} %fusion.8) | copy-start | bytes 7077892
  251.1 11.7 %collective-permute-start.13 = (bf16[512,1024]{1,0:T(8,128)(2,1)}, bf16[512,1024]{1,0:T(8,128)(2,1)}, u32[]{:S(2)}, u32[]{:S(2)}) collective-permute-start(bf16[512,1024]{1,0:T(8,128)(2,1)} %constant_dynamic-slice_fusion.6), channel_id=1, source_target_pairs={{0,4},{4,0},{8,12},{12,8},{1,5},{5,1},{9,13},{13,9},{2,6},{6,2},{1... | collective-permute-start | bytes 3145736 | tf_op jit(solution)/shard_map/ppermute | solution.py:488
  264.7 14.4 %copy-start.15 = (f32[256,1024]{1,0:T(8,128)S(1)}, f32[256,1024]{1,0:T(8,128)}, u32[]{:S(2)}) copy-start(f32[256,1024]{1,0:T(8,128)} %copy-done.13) | copy-start | bytes 3145732
  264.7 14.4 %collective-permute-start.14 = (bf16[256,1024]{1,0:T(8,128)(2,1)S(1)}, bf16[256,1024]{1,0:T(8,128)(2,1)S(1)}, u32[]{:S(2)}, u32[]{:S(2)}) collective-permute-start(bf16[256,1024]{1,0:T(8,128)(2,1)S(1)} %dynamic-slice_convert_fusion.1), channel_id=1, source_target_pairs={{0,1},{1,0},{2,3},{3,2},{4,5},{5,4},{6,7},{7,6},{8,9},{9,8},{10,11... | collective-permute-start | bytes 1572872 | tf_op jit(solution)/shard_map/ppermute | solution.py:491
  266.3 13.1 %copy-start.74 = (f32[256]{0:T(256)S(1)}, f32[256]{0:T(256)}, u32[]{:S(2)}) copy-start(f32[256]{0:T(256)} %copy-done.73) | copy-start | bytes 3076
  304.8 11.3 %copy-start.54 = (f32[1024,16]{0,1:T(8,128)S(1)}, f32[1024,16]{0,1:T(8,128)}, u32[]{:S(2)}) copy-start(f32[1024,16]{0,1:T(8,128)} %fusion.139) | copy-start | bytes 196612
  304.8 11.3 %copy-start.55 = (f32[1024,16]{0,1:T(8,128)S(1)}, f32[1024,16]{0,1:T(8,128)}, u32[]{:S(2)}) copy-start(f32[1024,16]{0,1:T(8,128)} %fusion.138) | copy-start | bytes 196612
  309.4 18.6 %all-to-all-start.1 = ((bf16[8,256,128]{2,1,0:T(8,128)(2,1)}), bf16[8,256,128]{2,1,0:T(8,128)(2,1)S(1)}, u32[]{:S(2)}, u32[]{:S(2)}) async-start(bf16[8,256,128]{2,1,0:T(8,128)(2,1)} %fusion.101), calls=%async_computation.1 | async-start | bytes 1048576 | tf_op jit(solution)/shard_map/all_to_all | solution.py:269
  315.6 43.6 %collective-permute-start.15 = (bf16[512,1024]{1,0:T(8,128)(2,1)}, bf16[512,1024]{1,0:T(8,128)(2,1)}, u32[]{:S(2)}, u32[]{:S(2)}) collective-permute-start(bf16[512,1024]{1,0:T(8,128)(2,1)} %constant_dynamic-slice_fusion.5), channel_id=1, source_target_pairs={{0,4},{4,0},{8,12},{12,8},{1,5},{5,1},{9,13},{13,9},{2,6},{6,2},{1... | collective-permute-start | bytes 3145736 | tf_op jit(solution)/shard_map/ppermute | solution.py:488
  328.1 7.9 %copy-start.7 = (bf16[2048,128]{1,0:T(8,128)(2,1)S(1)}, bf16[2048,128]{1,0:T(8,128)(2,1)}, u32[]{:S(2)}) copy-start(bf16[2048,128]{1,0:T(8,128)(2,1)} %copy-done.6) | copy-start | bytes 1572868
  329.9 34.7 %all-to-all-start.5 = ((bf16[32,80,32]{1,2,0:T(8,128)(2,1)}), bf16[32,80,32]{1,2,0:T(8,128)(2,1)}, u32[]{:S(2)}, u32[]{:S(2)}) async-start(bf16[32,80,32]{1,2,0:T(8,128)(2,1)} %bitcast.88), calls=%async_computation.5 | async-start | bytes 524288 | tf_op jit(solution)/shard_map/all_to_all | solution.py:579
  333.3 25.2 %collective-permute-start.26 = (bf16[48,1152]{1,0:T(8,128)(2,1)S(1)}, bf16[48,1152]{1,0:T(8,128)(2,1)S(1)}, u32[]{:S(2)}, u32[]{:S(2)}) collective-permute-start(bf16[48,1152]{1,0:T(8,128)(2,1)S(1)} %pad_maximum_fusion.20), channel_id=1, source_target_pairs={{0,2},{1,3},{2,0},{3,1},{4,6},{5,7},{6,4},{7,5},{8,10},{9,11},{10,... | collective-permute-start | bytes 331784 | tf_op jit(solution)/shard_map/ppermute | solution.py:580
  357.1 36.0 %collective-permute-start.17 = (bf16[2048,128]{1,0:T(8,128)(2,1)}, bf16[2048,128]{1,0:T(8,128)(2,1)}, u32[]{:S(2)}, u32[]{:S(2)}) collective-permute-start(bf16[2048,128]{1,0:T(8,128)(2,1)} %get-tuple-element.42), channel_id=1, source_target_pairs={{8,0},{12,4},{9,1},{13,5},{10,2},{14,6},{11,3},{15,7},{24,16},{28,... | collective-permute-start | bytes 1572872 | tf_op jit(solution)/shard_map/ppermute | solution.py:605
  363.1 118.5 %collective-permute-start.16 = (bf16[256,1024]{1,0:T(8,128)(2,1)}, bf16[256,1024]{1,0:T(8,128)(2,1)}, u32[]{:S(2)}, u32[]{:S(2)}) collective-permute-start(bf16[256,1024]{1,0:T(8,128)(2,1)} %dynamic-slice_convert_fusion), channel_id=1, source_target_pairs={{0,1},{1,0},{2,3},{3,2},{4,5},{5,4},{6,7},{7,6},{8,9},{9,8},{10,11... | collective-permute-start | bytes 1572872 | tf_op jit(solution)/shard_map/ppermute | solution.py:491
  412.5 15.5 %all-to-all-start.8 = ((bf16[8,16,256]{2,1,0:T(8,128)(2,1)}), bf16[8,16,256]{2,1,0:T(8,128)(2,1)S(1)}, u32[]{:S(2)}, u32[]{:S(2)}) async-start(bf16[8,16,256]{2,1,0:T(8,128)(2,1)} %broadcast_in_dim.40), calls=%async_computation.8 | async-start | bytes 131072 | tf_op jit(solution)/shard_map/all_to_all | solution.py:568
  426.5 35.7 %copy-start.71 = (f32[8]{0:T(128)S(1)}, f32[8]{0:T(128)}, u32[]{:S(2)}) copy-start(f32[8]{0:T(128)} %get-tuple-element.177) | copy-start | bytes 100
  428.0 12.2 %all-to-all-start.3 = ((bf16[32,2,768]{2,1,0:T(2,128)(2,1)}), bf16[32,2,768]{2,1,0:T(2,128)(2,1)S(1)}, u32[]{:S(2)}, u32[]{:S(2)}) async-start(bf16[32,2,768]{2,1,0:T(2,128)(2,1)} %reshape.1411), calls=%async_computation.3 | async-start | bytes 196608 | tf_op jit(solution)/shard_map/all_to_all | solution.py:658
  440.2 9.6 %all-to-all-start.7 = ((bf16[8,48,144]{2,1,0:T(8,128)(2,1)}), bf16[8,48,144]{2,1,0:T(8,128)(2,1)S(1)}, u32[]{:S(2)}, u32[]{:S(2)}) async-start(bf16[8,48,144]{2,1,0:T(8,128)(2,1)} %bitcast.452), calls=%async_computation.7 | async-start | bytes 393216 | tf_op jit(solution)/shard_map/all_to_all | solution.py:609
  449.7 8.9 %all-to-all-start.4 = ((bf16[4,2,1536]{2,1,0:T(2,128)(2,1)}), bf16[4,2,1536]{2,1,0:T(2,128)(2,1)S(1)}, u32[]{:S(2)}, u32[]{:S(2)}) async-start(bf16[4,2,1536]{2,1,0:T(2,128)(2,1)} %reshape.1413), calls=%async_computation.4 | async-start | bytes 49152 | tf_op jit(solution)/shard_map/all_to_all | solution.py:568
  459.5 17.0 %all-to-all-start.6 = ((bf16[32,2,80,32]{2,3,1,0:T(8,128)(2,1)}), bf16[32,2,80,32]{2,3,1,0:T(8,128)(2,1)S(1)}, u32[]{:S(2)}, u32[]{:S(2)}) async-start(bf16[32,2,80,32]{2,3,1,0:T(8,128)(2,1)} %broadcast_in_dim.39), calls=%async_computation.6 | async-start | bytes 1048576 | tf_op jit(solution)/shard_map/all_to_all | solution.py:568
  476.5 43.0 %all-to-all-start.2 = ((bf16[8,256,256]{2,1,0:T(8,128)(2,1)}), bf16[8,256,256]{2,1,0:T(8,128)(2,1)}, u32[]{:S(2)}, u32[]{:S(2)}) async-start(bf16[8,256,256]{2,1,0:T(8,128)(2,1)} %bitcast.65), calls=%async_computation.2 | async-start | bytes 2097152 | tf_op jit(solution)/shard_map/all_to_all | solution.py:269
  480.7 103.4 %all-gather.6.cloned.1.call-start = ((), (), s32[]{:S(2)}) async-start(), calls=%async_computation.10 | async-start | bytes 2621440 | tf_op jit(solution)/shard_map/all_gather | solution.py:508
  487.6 46.1 %copy-start.35 = (bf16[1,1024,1024]{2,1,0:T(8,128)(2,1)S(1)}, bf16[1,1024,1024]{2,1,0:T(8,128)(2,1)}, u32[]{:S(2)}) copy-start(bf16[1,1024,1024]{2,1,0:T(8,128)(2,1)} %param.21) | copy-start | bytes 6291460
  487.6 46.1 %copy-start.80 = (f32[1024]{0:T(1024)S(1)}, f32[1024]{0:T(1024)}, u32[]{:S(2)}) copy-start(f32[1024]{0:T(1024)} %param.30) | copy-start | bytes 12292
  520.3 35.6 %all-to-all-start.9 = ((bf16[8,2,48,144]{3,2,1,0:T(8,128)(2,1)}), bf16[8,2,48,144]{3,2,1,0:T(8,128)(2,1)}, u32[]{:S(2)}, u32[]{:S(2)}) async-start(bf16[8,2,48,144]{3,2,1,0:T(8,128)(2,1)} %broadcast_in_dim.41), calls=%async_computation.9 | async-start | bytes 786432 | tf_op jit(solution)/shard_map/all_to_all | solution.py:568
  538.5 21.0 %collective-permute-start.22 = (bf16[256,1024]{1,0:T(8,128)(2,1)}, bf16[256,1024]{1,0:T(8,128)(2,1)S(1)}, u32[]{:S(2)}, u32[]{:S(2)}) collective-permute-start(bf16[256,1024]{1,0:T(8,128)(2,1)} %fusion.69), channel_id=1, source_target_pairs={{1,0},{2,1},{3,2},{5,4},{6,5},{7,6},{9,8},{10,9},{11,10},{13,12},{... | collective-permute-start | bytes 1572872 | tf_op jit(solution)/shard_map/ppermute | solution.py:278
  539.8 21.0 %collective-permute-start.19 = (bf16[256,1024]{1,0:T(8,128)(2,1)}, bf16[256,1024]{1,0:T(8,128)(2,1)S(1)}, u32[]{:S(2)}, u32[]{:S(2)}) collective-permute-start(bf16[256,1024]{1,0:T(8,128)(2,1)} %fusion.69), channel_id=1, source_target_pairs={{0,1},{1,2},{2,3},{4,5},{5,6},{6,7},{8,9},{9,10},{10,11},{12,13},{... | collective-permute-start | bytes 1572872 | tf_op jit(solution)/shard_map/ppermute | solution.py:277
  559.5 16.7 %collective-permute-start.23 = (bf16[256,1024]{1,0:T(8,128)(2,1)S(1)}, bf16[256,1024]{1,0:T(8,128)(2,1)S(1)}, u32[]{:S(2)}, u32[]{:S(2)}) collective-permute-start(bf16[256,1024]{1,0:T(8,128)(2,1)S(1)} %collective-permute-done.22), channel_id=1, source_target_pairs={{1,0},{2,1},{3,2},{5,4},{6,5},{7,6},{9,8},{10,9},{11,10},{13,12},{... | collective-permute-start | bytes 1572872 | tf_op jit(solution)/shard_map/ppermute | solution.py:278
  560.8 16.7 %collective-permute-start.20 = (bf16[256,1024]{1,0:T(8,128)(2,1)S(1)}, bf16[256,1024]{1,0:T(8,128)(2,1)S(1)}, u32[]{:S(2)}, u32[]{:S(2)}) collective-permute-start(bf16[256,1024]{1,0:T(8,128)(2,1)S(1)} %collective-permute-done.19), channel_id=1, source_target_pairs={{0,1},{1,2},{2,3},{4,5},{5,6},{6,7},{8,9},{9,10},{10,11},{12,13},{... | collective-permute-start | bytes 1572872 | tf_op jit(solution)/shard_map/ppermute | solution.py:277
  576.2 15.0 %collective-permute-start.24 = (bf16[256,1024]{1,0:T(8,128)(2,1)S(1)}, bf16[256,1024]{1,0:T(8,128)(2,1)S(1)}, u32[]{:S(2)}, u32[]{:S(2)}) collective-permute-start(bf16[256,1024]{1,0:T(8,128)(2,1)S(1)} %collective-permute-done.23), channel_id=1, source_target_pairs={{1,0},{2,1},{3,2},{5,4},{6,5},{7,6},{9,8},{10,9},{11,10},{13,12},{... | collective-permute-start | bytes 1572872 | tf_op jit(solution)/shard_map/ppermute | solution.py:278
  577.5 14.8 %collective-permute-start.21 = (bf16[256,1024]{1,0:T(8,128)(2,1)S(1)}, bf16[256,1024]{1,0:T(8,128)(2,1)}, u32[]{:S(2)}, u32[]{:S(2)}) collective-permute-start(bf16[256,1024]{1,0:T(8,128)(2,1)S(1)} %collective-permute-done.20), channel_id=1, source_target_pairs={{0,1},{1,2},{2,3},{4,5},{5,6},{6,7},{8,9},{9,10},{10,11},{12,13},{... | collective-permute-start | bytes 1572872 | tf_op jit(solution)/shard_map/ppermute | solution.py:277
  (59 other events, 199.3 us)
Sparse Core Ops, SparseCore 0:
  22.5 32.1 all-gather.7
  140.9 67.8 all-gather.9
  484.2 57.4 all-gather.5

commit v2 on v1

v2 whole, which is shorter than its diff:
```python
import functools

import jax
import jax.numpy as jnp
from jax import lax
from jax.experimental import pallas as pl
from jax.experimental.pallas import tpu as pltpu
from jax.sharding import PartitionSpec as P

HD = 64
RANK = 16
ADAPT = 8
EPS = 1e-05
ADAPTER_SCALING = 2.0
THETA = 1000000.0
LOG2E = 1.4426950408889634
SCALE = HD**-0.5
F32 = jnp.float32
BF16 = jnp.bfloat16
VMEM_LIMIT = 62 * 1024 * 1024

CORE = [(i, i ^ 1) for i in range(4)]
XSIDE = [(i, i ^ 2) for i in range(4)]
Z_XOR = {d: [(i, i ^ d) for i in range(4)] for d in (1, 2, 3)}
CT = ("ctx", "tp")
SCT = ("shard", "ctx", "tp")
COLUMN = [[(2 * x + k) * 4 + z for k in range(2) for z in range(4)] for x in range(2)]

COST = pl.CostEstimate(flops=1 << 20, bytes_accessed=1 << 16, transcendentals=0)
LONG = pl.CostEstimate(flops=30 << 30, bytes_accessed=16 << 20, transcendentals=0)
HIGHEST = lax.Precision.HIGHEST


def nn(left, right):
    return lax.dot_general(left, right, (((1,), (0,)), ((), ())), preferred_element_type=F32)


def nt(left, right):
    return lax.dot_general(left, right, (((1,), (1,)), ((), ())), preferred_element_type=F32)


def tn(left, right):
    return lax.dot_general(left, right, (((0,), (0,)), ((), ())), preferred_element_type=F32)


def rmsnorm(value, gain):
    return value * lax.rsqrt(jnp.mean(value * value, axis=-1, keepdims=True) + EPS) * gain


def order2(own, other, bit, axis=0):
    return jnp.concatenate(
        [jnp.where(bit == 0, own, other), jnp.where(bit == 0, other, own)], axis=axis
    )


def rows_at(value, block, size, axis=0):
    return lax.dynamic_slice_in_dim(value, block * size, size, axis)


def key_loops(segment, base, i, bq, bk, keys, step, acc):
    blocks = keys // bk
    first, key_base = base[0] + i * bq, base[1]
    low = jnp.minimum(jnp.maximum(segment[first] - key_base, 0) // bk, blocks)
    high = jnp.clip((first + bq - key_base + bk - 1) // bk, 0, blocks)
    low = jnp.minimum(low, high)
    free_low = (jnp.maximum(segment[first + bq - 1] - key_base, 0) + bk - 1) // bk
    free_low = jnp.clip(free_low, low, high)
    free_high = jnp.clip(jnp.maximum(first + 1 - key_base, 0) // bk, free_low, high)
    ahead = free_low - low

    def masked(t, carry):
        j = jnp.where(t < ahead, low + t, free_high + t - ahead)
        return step(j, carry, True)

    acc = lax.fori_loop(0, ahead + high - free_high, masked, acc)
    return lax.fori_loop(free_low, free_high, lambda j, carry: step(j, carry, False), acc)


def row_sums(weights, value):
    return lax.dot_general(
        weights, value, (((1,), (1,)), ((), ())), precision=HIGHEST, preferred_element_type=F32
    )


def fwd_kernel(bq, bk, last, segment, base, q_ref, kv_ref, seg_ref, *rest):
    if last:
        acc_in, mixed_ref, low_ref, lse_ref, vx = rest
    else:
        acc_ref, vx = rest
    i = pl.program_id(0)
    keys = kv_ref.shape[0]

    @pl.when(i == 0)
    def _():
        col = lax.broadcasted_iota(jnp.int32, (keys, 2 * HD), 1)
        kv = kv_ref[...]
        swapped = jnp.concatenate([kv[:, HD:], kv[:, :HD]], axis=1)
        ones = jnp.where(col == HD, 1.0, 0.0).astype(BF16)
        vx[...] = jnp.where(col < HD, swapped, ones)

    q = q_ref[...]
    both = jnp.concatenate([q[:, :HD], q[:, HD:]], axis=0)
    q_base, k_base = base[0], base[1]
    seg_col = jnp.broadcast_to(seg_ref[0].astype(F32), (8, bq))
    seg_col = jnp.transpose(seg_col)[:, :1].astype(jnp.int32)

    def step(j, acc, masked):
        off = pl.multiple_of(j * bk, bk)
        scores = nt(both, kv_ref[pl.ds(off, bk), :HD])
        probs = jnp.exp2(scores * (SCALE * LOG2E))
        if masked:
            qi = q_base + i * bq + lax.broadcasted_iota(jnp.int32, (bq, bk), 0)
            ki = k_base + off + lax.broadcasted_iota(jnp.int32, (bq, bk), 1)
            allowed = (ki <= qi) & (ki >= seg_col)
            probs = jnp.where(jnp.concatenate([allowed, allowed], axis=0), probs, 0.0)
        return acc + nn(probs.astype(BF16), vx[pl.ds(off, bk), :])

    if last:
        acc = jnp.concatenate([acc_in[0], acc_in[1]], axis=0)
    else:
        acc = jnp.zeros((2 * bq, 2 * HD), F32)
    acc = key_loops(segment, base, i, bq, bk, keys, step, acc)
    if last:
        total = acc[:, HD : HD + 1]
        out = acc[:, :HD] / total
        out = jnp.concatenate([out[:bq], out[bq:]], axis=1)
        mixed_ref[...] = out
        low_ref[...] = out.astype(BF16)
        pick = jnp.where(lax.broadcasted_iota(jnp.int32, (8, 2 * HD), 1) == HD, 1.0, 0.0)
        lse_ref[0] = jnp.log2(row_sums(pick, acc)[:1])
    else:
        acc_ref[0] = acc[:bq]
        acc_ref[1] = acc[bq:]


def attention_forward(q, kv, seg, segment, base, bq, bk, acc_in=None):
    rows, keys = q.shape[0], kv.shape[0]
    last = acc_in is not None
    row = lambda i, *_: (i, 0)
    everything = lambda i, *_: (0, 0)
    heads = lambda i, *_: (0, i, 0)
    in_specs = [
        pl.BlockSpec((bq, 2 * HD), row),
        pl.BlockSpec((keys, 2 * HD), everything),
        pl.BlockSpec((1, 1, bq), lambda i, *_: (i, 0, 0)),
    ]
    args = [q, kv, seg]
    if last:
        in_specs.append(pl.BlockSpec((2, bq, 2 * HD), heads))
        args.append(acc_in)
        out_specs = [
            pl.BlockSpec((bq, 2 * HD), row),
            pl.BlockSpec((bq, 2 * HD), row),
            pl.BlockSpec((1, 1, 2 * bq), lambda i, *_: (i, 0, 0)),
        ]
        out_shape = [
            jax.ShapeDtypeStruct((rows, 2 * HD), F32),
            jax.ShapeDtypeStruct((rows, 2 * HD), BF16),
            jax.ShapeDtypeStruct((rows // bq, 1, 2 * bq), F32),
        ]
    else:
        out_specs = pl.BlockSpec((2, bq, 2 * HD), heads)
        out_shape = jax.ShapeDtypeStruct((2, rows, 2 * HD), F32)
    return pl.pallas_call(
        functools.partial(fwd_kernel, bq, bk, last),
        grid_spec=pltpu.PrefetchScalarGridSpec(
            num_scalar_prefetch=2,
            grid=(rows // bq,),
            in_specs=in_specs,
            out_specs=out_specs,
            scratch_shapes=[pltpu.VMEM((keys, 2 * HD), BF16)],
        ),
        out_shape=out_shape,
        compiler_params=pltpu.CompilerParams(vmem_limit_bytes=VMEM_LIMIT),
        cost_estimate=LONG,
        name="attn_fwd_last" if last else "attn_fwd_first",
    )(segment, base, *args)


def bwd_kernel(
    bq, bk, first, segment, base, q_ref, kv_ref, seg_ref, do_ref, out_ref, lse_ref, *rest
):
    if first:
        dq_ref, dkv_ref, dk, dv = rest
    else:
        dq_in, dq_ref, dkv_ref, dk, dv = rest
    i = pl.program_id(0)

    @pl.when(i == 0)
    def _():
        dk[...] = jnp.zeros_like(dk)
        dv[...] = jnp.zeros_like(dv)

    q = q_ref[...]
    do = do_ref[...]
    both = jnp.concatenate([q[:, :HD], q[:, HD:]], axis=0)
    both_do = jnp.concatenate([do[:, :HD], do[:, HD:]], axis=0)
    lse = lse_ref[0]
    lane = lax.broadcasted_iota(jnp.int32, (8, 2 * HD), 1)
    row = lax.broadcasted_iota(jnp.int32, (8, 2 * HD), 0)
    pick = jnp.where(lane // HD == row, 1.0, 0.0)
    deltas = row_sums(pick, do.astype(F32) * out_ref[...])
    delta = jnp.concatenate([deltas[:1], deltas[1:2]], axis=1)
    q_base, k_base = base[0], base[1]

    def step(j, acc, masked):
        off = pl.multiple_of(j * bk, bk)
        kv = kv_ref[pl.ds(off, bk), :]
        k, v = kv[:, :HD], kv[:, HD:]
        probs = jnp.exp2(nt(k, both) * (SCALE * LOG2E) - lse)
        if masked:
            ki = k_base + off + lax.broadcasted_iota(jnp.int32, (bk, bq), 0)
            qi = q_base + i * bq + lax.broadcasted_iota(jnp.int32, (bk, bq), 1)
            allowed = (ki <= qi) & (ki >= seg_ref[0])
            probs = jnp.where(jnp.concatenate([allowed, allowed], axis=1), probs, 0.0)
        dscores = (probs * (nt(v, both_do) - delta)).astype(BF16)
        dv[pl.ds(off, bk), :] += nn(probs.astype(BF16), both_do)
        dk[pl.ds(off, bk), :] += nn(dscores, both)
        return acc + tn(k, dscores)

    acc = key_loops(
        segment, base, i, bq, bk, kv_ref.shape[0], step, jnp.zeros((HD, 2 * bq), F32)
    )
    acc = jnp.transpose(acc) * SCALE
    acc = jnp.concatenate([acc[:bq], acc[bq:]], axis=1)
    dq_ref[...] = acc if first else dq_in[...] + acc

    @pl.when(i == pl.num_programs(0) - 1)
    def _():
        dkv_ref[...] = jnp.concatenate([dk[...] * SCALE, dv[...]], axis=1).astype(dkv_ref.dtype)


def attention_backward(q, kv, seg, do, out, lse, segment, base, bq, bk, dq_in=None):
    rows, keys = q.shape[0], kv.shape[0]
    first = dq_in is None
    row = lambda i, *_: (i, 0)
    everything = lambda i, *_: (0, 0)
    flat = lambda i, *_: (i, 0, 0)
    in_specs = [
        pl.BlockSpec((bq, 2 * HD), row),
        pl.BlockSpec((keys, 2 * HD), everything),
        pl.BlockSpec((1, 1, bq), flat),
        pl.BlockSpec((bq, 2 * HD), row),
        pl.BlockSpec((bq, 2 * HD), row),
        pl.BlockSpec((1, 1, 2 * bq), flat),
    ]
    args = [q, kv, seg, do, out, lse]
    if not first:
        in_specs.append(pl.BlockSpec((bq, 2 * HD), row))
        args.append(dq_in)
    return pl.pallas_call(
        functools.partial(bwd_kernel, bq, bk, first),
        grid_spec=pltpu.PrefetchScalarGridSpec(
            num_scalar_prefetch=2,
            grid=(rows // bq,),
            in_specs=in_specs,
            out_specs=[pl.BlockSpec((bq, 2 * HD), row), pl.BlockSpec((keys, 2 * HD), everything)],
            scratch_shapes=[pltpu.VMEM((keys, HD), F32), pltpu.VMEM((keys, HD), F32)],
        ),
        out_shape=[
            jax.ShapeDtypeStruct((rows, 2 * HD), F32),
            jax.ShapeDtypeStruct((keys, 2 * HD), BF16 if first else F32),
        ],
        compiler_params=pltpu.CompilerParams(vmem_limit_bytes=VMEM_LIMIT),
        cost_estimate=LONG,
        name="attn_bwd_first" if first else "attn_bwd_last",
    )(segment, base, *args)


def run(kernel, name, grid, scalars, inputs, outputs, scratch=(), cost=COST):
    return pl.pallas_call(
        kernel,
        grid_spec=pltpu.PrefetchScalarGridSpec(
            num_scalar_prefetch=1,
            grid=grid,
            in_specs=[
                pl.BlockSpec(memory_space=pl.ANY) if block is None else pl.BlockSpec(block, index)
                for _, block, index in inputs
            ],
            out_specs=[
                pl.BlockSpec(memory_space=pl.ANY) if block is None else pl.BlockSpec(block, index)
                for _, _, block, index in outputs
            ],
            scratch_shapes=list(scratch),
        ),
        out_shape=[jax.ShapeDtypeStruct(shape, kind) for shape, kind, _, _ in outputs],
        compiler_params=pltpu.CompilerParams(vmem_limit_bytes=VMEM_LIMIT),
        cost_estimate=cost,
        name=name,
    )(scalars, *[array for array, _, _ in inputs])


def fixed(*index):
    return lambda i, s: index


def whole(array):
    return (array, array.shape, fixed(*(0,) * array.ndim))


def out_whole(shape, kind):
    return (shape, kind, shape, fixed(*(0,) * len(shape)))


def place_matrix(back):
    at_row = lax.broadcasted_iota(jnp.int32, (4 * HD, 4 * HD), 0)
    at_col = lax.broadcasted_iota(jnp.int32, (4 * HD, 4 * HD), 1)
    if back:
        at_row, at_col = at_col, at_row
    part = HD // 2
    moved = at_row // part % 2 * (2 * HD) + at_row // HD * part + at_row % part
    return jnp.where(moved == at_col, 1.0, 0.0).astype(BF16)


def head_means(value):
    at_row = lax.broadcasted_iota(jnp.int32, (2 * HD, 2 * HD), 0) // (HD // 2)
    at_col = lax.broadcasted_iota(jnp.int32, (2 * HD, 2 * HD), 1) // (HD // 2)
    same = jnp.where(at_row == at_col, 1.0 / HD, 0.0).astype(BF16)
    high = value.astype(BF16)
    rest = value - high.astype(F32)
    middle = rest.astype(BF16)
    return nn(high, same) + nn(middle, same) + nn((rest - middle.astype(F32)).astype(BF16), same)


def rotation(step, inner, outer):
    cos_in, sin_in = inner[0], inner[1]
    cos_out, sin_out = outer[0, pl.ds(step, 1)], outer[1, pl.ds(step, 1)]
    return cos_in * cos_out - sin_in * sin_out, sin_in * cos_out + cos_in * sin_out


def head_root(first, second):
    lane = lax.broadcasted_iota(jnp.int32, first.shape, 1)
    root = lax.rsqrt(head_means(first * first + second * second) + EPS)
    return jnp.where(lane < 3 * (HD // 2), root, 1.0), lane


def pieces_kernel(at, gate_up, down, gate_o, down_o):
    gate_o[...] = gate_up[0]
    down_o[...] = down[...]


def prepare_kernel(
    at, q, kv, out_w, up_gate_up, lower_down, up_q, up_kv, lower_out,
    qkv_o, rows_o, small_o, upper_o, low_o,
):
    k = at[0]
    value = kv[...].astype(F32)
    value = jnp.where(k == 0, value[:, :, :HD], value[:, :, HD:]).astype(BF16)
    value = jnp.concatenate([q[...], value[0], value[1]], axis=1)
    qkv_o[...] = nt(place_matrix(True), value).astype(BF16)
    rows_o[...] = out_w[...]
    small_o[:2] = up_gate_up[0]
    small_o[2] = lower_down[0]
    table = up_kv[0].astype(F32)
    table = jnp.where(k == 0, table[:, :, :HD], table[:, :, HD:]).astype(BF16)
    zero = jnp.zeros_like(table[0])
    wide = jnp.zeros((RANK, 2 * HD), BF16)
    rows = [
        jnp.concatenate([up_q[0], wide], axis=1),
        jnp.concatenate([wide, table[0], zero], axis=1),
        jnp.concatenate([wide, zero, table[1]], axis=1),
    ] + [jnp.concatenate([wide, wide], axis=1)] * 5
    upper_o[...] = nt(place_matrix(True), jnp.concatenate(rows, axis=0)).astype(BF16)
    table = jnp.transpose(lower_out[0].astype(F32))
    low_o[...] = jnp.concatenate(
        [table, jnp.zeros((table.shape[0], 2 * HD - RANK), F32)], axis=1
    ).astype(BF16)


def project_kernel(
    at, own, oth, gain, dense, lower, upper, inner, outer, gains,
    normal_o, narrow_o, q_o, kv_o, raw_o, weights,
):
    width = 4 * HD
    step = pl.program_id(0)
    steps = pl.num_programs(0)

    @pl.when(step == 0)
    def _():
        weights[:width] = dense[...]
        weights[width : width + 3 * RANK] = lower[0]
        weights[width + 3 * RANK :] = jnp.zeros(
            (weights.shape[0] - width - 3 * RANK, weights.shape[1]), BF16
        )

    value = jnp.where(step < steps // 2, own[...].astype(F32), oth[...].astype(F32))
    root = lax.rsqrt(jnp.mean(value * value, axis=1, keepdims=True) + EPS)
    normal = (value * root * gain[...]).astype(BF16)
    normal_o[...] = normal
    raw = nt(normal, weights[...])
    narrow = raw[:, width:].astype(BF16)
    narrow_o[...] = narrow[:, : 3 * RANK]
    raw = raw[:, :width] + ADAPTER_SCALING * nt(narrow, upper[...])
    raw_o[...] = raw
    first, second = raw[:, : 2 * HD], raw[:, 2 * HD :]
    root, _ = head_root(first, second)
    place = jnp.where(step < steps // 2, at[0] * (steps // 2) + step, (1 - at[0]) * (steps // 2) + step - steps // 2)
    cos, sin = rotation(place, inner, outer)
    first = first * root * gains[0:1]
    second = second * root * gains[1:2]
    turned = jnp.concatenate([first * cos - second * sin, second * cos + first * sin], axis=1)
    out = nn(turned.astype(BF16), place_matrix(True)).astype(BF16)
    q_o[...] = out[:, : 2 * HD]
    kv_o[...] = out[:, 2 * HD :]


def project_back_kernel(
    at, dq, dkv, dkv_after, raw, inner, outer, gains, narrow, normal, upper,
    out, wide_o, heads_o, wide, heads,
):
    step = pl.program_id(0)

    @pl.when(step == 0)
    def _():
        wide[...] = jnp.zeros_like(wide)
        heads[...] = jnp.zeros_like(heads)

    cos, sin = rotation(2 * step, inner, outer)
    grad_kv = (dkv[...] + dkv_after[...].astype(F32)).astype(BF16)
    grad = nn(jnp.concatenate([dq[...].astype(BF16), grad_kv], axis=1), place_matrix(False))
    first, second = raw[:, : 2 * HD], raw[:, 2 * HD :]
    root, lane = head_root(first, second)
    first, second = first * root, second * root
    back_first = grad[:, : 2 * HD] * cos + grad[:, 2 * HD :] * sin
    back_second = grad[:, 2 * HD :] * cos - grad[:, : 2 * HD] * sin
    back_first = back_first * gains[0:1]
    back_second = back_second * gains[1:2]
    mean = head_means(back_first * first + back_second * second)
    mean = jnp.where(lane < 3 * (HD // 2), mean, 0.0)
    back_first = (root * (back_first - first * mean)).astype(BF16)
    back_second = (root * (back_second - second * mean)).astype(BF16)
    grad = jnp.concatenate([back_first, back_second], axis=1)
    out[...] = grad
    inside = (ADAPTER_SCALING * nn(grad, upper[...])).astype(BF16)
    wide[...] += tn(inside[:, : 3 * RANK], normal[...])
    heads[...] += tn(narrow[...], grad)

    @pl.when(step == pl.num_programs(0) - 1)
    def _():
        wide_o[...] = wide[...].astype(BF16)
        total = (heads[...] * ADAPTER_SCALING).astype(BF16)
        total = nn(total, place_matrix(True))
        total = jnp.concatenate(
            [
                total[:RANK, : 2 * HD],
                total[RANK : 2 * RANK, 2 * HD : 3 * HD],
                total[2 * RANK :, 3 * HD :],
            ],
            axis=1,
        )
        zero = jnp.zeros_like(total)
        heads_o[:, : 4 * HD] = jnp.where(at[0] == 0, total, zero).astype(BF16)
        heads_o[:, 4 * HD :] = jnp.where(at[0] == 0, zero, total).astype(BF16)


def head_blocks(value, which):
    return jnp.concatenate([value[which * 4 + place] for place in range(4)], axis=1)


def mix_kernel(at, mixed, out_own, out_oth, upper, tokens, gain, hidden_o, normal_o, narrow_o):
    k = at[0]
    width = tokens.shape[2]
    total = nn(head_blocks(mixed, k), out_own[...]) + nn(head_blocks(mixed, 1 - k), out_oth[...])
    narrow = total[:, width : width + RANK].astype(BF16)
    narrow_o[...] = narrow
    total = tokens[0].astype(F32) + total[:, :width] + ADAPTER_SCALING * nn(narrow, upper[0])
    hidden_o[...] = total
    root = lax.rsqrt(jnp.mean(total * total, axis=1, keepdims=True) + EPS)
    normal_o[...] = (total * root * gain[...]).astype(BF16)


def norm_back(value, grad, gain):
    root = lax.rsqrt(jnp.mean(value * value, axis=1, keepdims=True) + EPS)
    unit = value * root
    grad = grad * gain
    return root * (grad - unit * jnp.mean(grad * unit, axis=1, keepdims=True))


def mix_back_kernel(
    at, hidden, cotangent, own, arrived, far, gain, out_own, out_oth, upper,
    grad_o, low_o, mixed_o, narrow_o,
):
    k = at[0]
    rows = hidden.shape[0]
    grad = own[:rows].astype(F32) + arrived[:rows].astype(F32) + far[...].astype(F32)
    grad = cotangent[0].astype(F32) + norm_back(hidden[...], grad, gain[...])
    grad_o[...] = grad
    low = grad.astype(BF16)
    low_o[...] = low
    table = jnp.transpose(upper[0].astype(F32))
    table = jnp.concatenate([table, jnp.zeros((table.shape[0], 2 * HD - RANK), F32)], axis=1)
    narrow = (ADAPTER_SCALING * nn(low, table.astype(BF16))).astype(BF16)
    narrow_o[...] = narrow[:, :RANK]
    low = jnp.concatenate([low, narrow], axis=1)
    for which, source in ((k, out_own), (1 - k, out_oth)):
        value = nt(low, source[...]).astype(BF16)
        for place in range(4):
            mixed_o[which * 4 + place] = value[:, place * 2 * HD : (place + 1) * 2 * HD]


def mix_grads_kernel(at, mixed, low, narrow, narrow_back, out_o):
    out_o[:RANK] = (ADAPTER_SCALING * tn(narrow[...], low[...])).astype(BF16)
    for i in range(8):
        value = tn(narrow_back[...], mixed[i])
        out_o[RANK:, i * 2 * HD : (i + 1) * 2 * HD] = value.astype(BF16)


def last_kernel(at, grads, own, own_x, oth, oth_x, lower, hidden, tokens, gain, out):
    k, x = at[0], at[1]
    width = hidden.shape[1]
    total = 0.0
    for which, side, source in ((k, x, own), (k, 1 - x, own_x), (1 - k, x, oth), (1 - k, 1 - x, oth_x)):
        lanes = pl.ds(pl.multiple_of(side * 2 * HD, 2 * HD), 2 * HD)
        value = [grads[which * 4 + place, :, lanes] for place in range(4)]
        total += nn(jnp.concatenate(value, axis=1), source[...])
    narrow = (ADAPTER_SCALING * total[:, width : width + 3 * RANK]).astype(BF16)
    total = total[:, :width] + nn(narrow, lower[0])
    value = tokens[0].astype(F32)
    out[...] = (hidden[...] + norm_back(value, total, gain[...])).astype(BF16)


def weight_copies(at, sources, dst, sem, down):
    k, x, y = at[0], at[1], at[2]

    def lanes(start, size):
        return pl.ds(pl.multiple_of(start, 2 * HD), size)

    def rows(start, size):
        return pl.ds(pl.multiple_of(start, 16), size)

    if down:
        height, width = dst.shape[0], sources[0].shape[1]
    else:
        height, width = sources[0].shape[1:]
    if len(sources) == 1:
        if down:
            pairs = [(sources[0], dst.at[:, pl.ds(0, width)])]
        else:
            pairs = [
                (sources[0].at[m], dst.at[pl.ds(0, height), pl.ds(m * width, width)])
                for m in range(2)
            ]
        return [
            (None, [pltpu.make_async_copy(a, b, sem.at[i]) for i, (a, b) in enumerate(pairs)])
        ]
    local, mine, *pieces = sources
    zero, one = [], []
    if down:
        part = height // 2
        for j, source in enumerate((local, mine)):
            zero.append((source, dst.at[:, lanes((y + j) % 2 * width, width)]))
        for j, source in enumerate(pieces):
            at_row = rows((x + j) % 2 * part, part)
            one.append((source, dst.at[at_row, lanes((y + j // 2) % 2 * width, width)]))
    else:
        for j, source in enumerate((local, mine)):
            for m in range(2):
                at_row = rows((y + j) % 2 * height, height)
                zero.append((source.at[m], dst.at[at_row, pl.ds(m * width, width)]))
        for j, source in enumerate(pieces):
            at_row = rows((y + j // 2) % 2 * height, height)
            one.append((source, dst.at[at_row, lanes((x + j) % 2 * width, width)]))
    return [
        (when, [pltpu.make_async_copy(a, b, sem.at[i]) for i, (a, b) in enumerate(pairs)])
        for when, pairs in ((k == 0, zero), (k == 1, one))
    ]


def for_copies(groups, what):
    for when, copies in groups:
        if when is None:
            for copy in copies:
                what(copy)
        else:

            @pl.when(when)
            def _():
                for copy in copies:
                    what(copy)


def put_down_lower(down, small):
    width = 2 * HD
    table = jnp.transpose(small[2].astype(F32))
    table = jnp.concatenate(
        [table, jnp.zeros((table.shape[0], width - table.shape[1]), F32)], axis=1
    )
    down[:, down.shape[1] - width :] = table.astype(BF16)


def both_tokens(step, own, far, own_oth, far_oth):
    here = jnp.concatenate([own[...], far[...]], axis=0).astype(F32)
    there = jnp.concatenate([own_oth[...], far_oth[...]], axis=0).astype(F32)
    return jnp.where(step == 0, here, there).astype(BF16)


def wide_table(table):
    table = jnp.transpose(table.astype(F32))
    return jnp.concatenate(
        [table, jnp.zeros((table.shape[0], 2 * HD - table.shape[1]), F32)], axis=1
    ).astype(BF16)


def ffn_kernel(many, at, own, far, own_oth, far_oth, cot, cot_far, cot_oth, cot_far_oth, *rest):
    lower, small, upper = rest[:3]
    sources, down_sources = rest[3 : 3 + many], rest[3 + many : 3 + 2 * many]
    part_own, part_oth, act_o, grad_o, narrow_o, back_o, weights, down, tables, sem = rest[
        3 + 2 * many :
    ]
    step = pl.program_id(0)
    units = small.shape[2]
    first = weight_copies(at, sources, weights, sem.at[0], False)
    second = weight_copies(at, down_sources, down, sem.at[1], True)

    @pl.when(step == 0)
    def _():
        for_copies(first, lambda copy: copy.start())
        for_copies(second, lambda copy: copy.start())
        put_down_lower(down, small)
        tables[0] = wide_table(lower[0][3 * RANK :])
        tables[1] = wide_table(upper[0])
        for_copies(first, lambda copy: copy.wait())
        for i in range(2):
            term = lower[0][(3 + i) * RANK : (4 + i) * RANK]
            at_lanes = slice(i * units, (i + 1) * units)
            merged = weights[:, at_lanes].astype(F32) + ADAPTER_SCALING * tn(term, small[i])
            weights[:, at_lanes] = merged.astype(BF16)
        for_copies(second, lambda copy: copy.wait())

    value = both_tokens(step, own, far, own_oth, far_oth)
    grad = both_tokens(step, cot.at[0], cot_far.at[0], cot_oth, cot_far_oth)
    narrow_o[0] = nn(value, tables[0]).astype(BF16)[:, : 2 * RANK]
    narrow = (ADAPTER_SCALING * nn(grad, tables[1])).astype(BF16)
    back_o[0] = narrow[:, :RANK]
    grad = jnp.concatenate([grad, narrow], axis=1)
    both = nn(value, weights[...])
    gate, up = both[:, :units], both[:, units:]
    grad_act = nt(grad, down[...])
    sig = 0.5 * jnp.tanh(0.5 * gate) + 0.5
    silu = gate * sig
    act_o[0] = (silu * up).astype(BF16)
    grad_gate = (grad_act * up * (sig + silu * (1.0 - sig))).astype(BF16)
    grad_up = (grad_act * silu).astype(BF16)
    grad_both = jnp.concatenate([grad_gate, grad_up], axis=1)
    grad_o[0] = grad_both
    part = nt(grad_both, weights[...]).astype(BF16)

    @pl.when(step == 0)
    def _():
        part_own[...] = part

    @pl.when(step == 1)
    def _():
        part_oth[...] = part


def ffn_down_kernel(many, at, act, small, upper, *rest):
    sources = rest[:many]
    part_own, part_oth, zd_o, down, sem = rest[many:]
    step = pl.program_id(0)
    width = upper.shape[2]
    copies = weight_copies(at, sources, down, sem.at[0], True)

    @pl.when(step == 0)
    def _():
        for_copies(copies, lambda copy: copy.start())
        put_down_lower(down, small)
        for_copies(copies, lambda copy: copy.wait())

    part = nn(act[0], down[...])
    zd = part[:, width : width + RANK].astype(BF16)
    zd_o[0] = zd
    part = (part[:, :width] + ADAPTER_SCALING * nn(zd, upper[0])).astype(BF16)

    @pl.when(step == 0)
    def _():
        part_own[...] = part

    @pl.when(step == 1)
    def _():
        part_oth[...] = part


def ffn_grads_kernel(at, own, far, own_oth, far_oth, cot, cot_far, cot_oth, cot_far_oth, *rest):
    act, grads, narrow, narrow_back, zd, small, wide_o, quarter_o, lanes, wide, quarter = rest
    step = pl.program_id(0)
    units = small.shape[2]

    @pl.when(step == 0)
    def _():
        wide[...] = jnp.zeros_like(wide)
        quarter[...] = jnp.zeros_like(quarter)
        lanes[...] = jnp.zeros_like(lanes)
        for i in range(2):
            table = jnp.transpose(small[i].astype(F32))
            zero = jnp.zeros_like(table)
            table = jnp.concatenate([table, zero] if i == 0 else [zero, table], axis=1)
            lanes[i * units : (i + 1) * units, : 2 * RANK] = table.astype(BF16)

    value = both_tokens(step, own, far, own_oth, far_oth)
    grad = both_tokens(step, cot.at[0], cot_far.at[0], cot_oth, cot_far_oth)
    inner = (ADAPTER_SCALING * nn(grads[0], lanes[...])).astype(BF16)[:, : 2 * RANK]
    wide[:RANK] += ADAPTER_SCALING * tn(zd[0], grad)
    wide[RANK:] += tn(inner, value)
    both = tn(narrow[0], grads[0])
    quarter[:RANK] += ADAPTER_SCALING * both[:RANK, :units]
    quarter[RANK : 2 * RANK] += ADAPTER_SCALING * both[RANK:, units:]
    quarter[2 * RANK :] += tn(narrow_back[0], act[0])

    @pl.when(step == 1)
    def _():
        wide_o[...] = wide[...].astype(BF16)
        quarter_o[...] = quarter[...].astype(BF16)


def assemble_kernel(at, own, *rest):
    z = at[4]
    up, down, out = rest[:3], rest[3:6], rest[6]
    place = pl.program_id(0)

    @pl.when(place == z)
    def _():
        out[0] = own[...].astype(out.dtype)

    for d in range(3):

        @pl.when(z - place == d + 1)
        def _():
            out[0] = up[d][...].astype(out.dtype)

        @pl.when(place - z == d + 1)
        def _():
            out[0] = down[d][...].astype(out.dtype)


def plus(here, there):
    return (here.astype(F32) + there.astype(F32)).astype(BF16)


def tie(*values):
    return lax.optimization_barrier(values)


def tie_all(values):
    return lax.optimization_barrier(values)


def heads_tokens(value):
    return lax.all_to_all(value, CT, 0, 0, axis_index_groups=COLUMN, tiled=True)


UP = [(i, i + 1) for i in range(3)]
DOWN = [(i + 1, i) for i in range(3)]


def body(
    shards,
    inputs,
    cotangent,
    segments,
    adapter_index,
    query_weight,
    key_value_weight,
    output_weight,
    gate_up_weight,
    down_weight,
    norm_attn,
    norm_ffn,
    q_gain,
    k_gain,
    input_adapter_lower,
    query_adapter_upper,
    key_value_adapter_upper,
    gate_up_adapter_upper,
    output_adapter_lower,
    output_adapter_upper,
    down_adapter_lower,
    down_adapter_upper,
):
    ctx = lax.axis_index("ctx")
    x, k = ctx // 2, ctx % 2
    z = lax.axis_index("tp")
    y = lax.axis_index("shard")
    tok = inputs.shape[1]
    half = 2 * tok
    sub = tok // 4
    width = inputs.shape[2]
    hidden_units = gate_up_weight.shape[2]
    slot = adapter_index[0]
    segment = segments[0]
    pair = shards == 2
    swap_y = [(0, 1), (1, 0)]
    cols = 2 * HD
    at = jnp.stack([k, x, y, slot, z]).astype(jnp.int32)
    K, X, Y, SLOT, Z = range(5)

    def shard_rows(piece, axis):
        if pair:
            return order2(piece, lax.ppermute(piece, "shard", swap_y), y, axis)
        return lax.all_gather(piece, "shard", axis=axis, tiled=True)

    def over_y(cores):
        return [
            ((s * 4 + c) * 4 + t, ((s ^ 1) * 4 + c) * 4 + t)
            for s in range(2)
            for c in cores
            for t in range(4)
        ]

    tokens_other = lax.ppermute(inputs[0], "ctx", CORE)
    by_slot = lambda i, s: (s[SLOT], 0, 0)
    prepared = run(
        prepare_kernel,
        "prepare",
        (1,),
        at,
        [
            (query_weight, (query_weight.shape[0], cols), lambda i, s: (0, s[K])),
            whole(key_value_weight),
            (output_weight, (cols, output_weight.shape[1]), lambda i, s: (s[K], 0)),
            (gate_up_adapter_upper, (1, 2, RANK, hidden_units), lambda i, s: (s[SLOT], 0, 0, 0)),
            (jnp.swapaxes(down_adapter_lower, 1, 2), (1, RANK, hidden_units), by_slot),
            (query_adapter_upper, (1, RANK, cols), lambda i, s: (s[SLOT], 0, s[K])),
            (key_value_adapter_upper, (1, 2, RANK, cols), lambda i, s: (s[SLOT], 0, 0, 0)),
            (
                jnp.swapaxes(output_adapter_lower, 1, 2),
                (1, RANK, cols),
                lambda i, s: (s[SLOT], 0, s[K]),
            ),
        ],
        [
            out_whole((2 * cols, query_weight.shape[0]), BF16),
            out_whole((cols, output_weight.shape[1]), BF16),
            out_whole((3, RANK, hidden_units), BF16),
            out_whole((2 * cols, cols), BF16),
            out_whole((cols, cols), BF16),
        ],
    )
    dense_piece, rows_piece, small_ffn, upper_qkv, low_rows = prepared
    dense_qkv = shard_rows(dense_piece, 1)
    rows_here = shard_rows(rows_piece, 1)

    far_z = [(c * 4 + t, c * 4 + (t ^ 2)) for c in (1, 3) for t in range(4)]
    far_x = [(1, 3), (3, 1)]
    if pair:
        piece_g, piece_d = run(
            pieces_kernel,
            "pieces",
            (1,),
            at,
            [
                (gate_up_weight, (1,) + gate_up_weight.shape[1:], lambda i, s: (s[X], 0, 0)),
                (down_weight, (hidden_units // 2, down_weight.shape[1]), lambda i, s: (s[X], 0)),
            ],
            [
                out_whole(gate_up_weight.shape[1:], BF16),
                out_whole((hidden_units // 2, down_weight.shape[1]), BF16),
            ],
        )
        piece_g = lax.ppermute(piece_g, CT, far_z)
        piece_d = lax.ppermute(piece_d, CT, far_z)

    block = tok // 4
    blocks = half // block
    half_dim = HD // 2
    first_query = x * half
    inverse = THETA ** (-(jnp.arange(half_dim, dtype=F32) * 2.0 / HD))
    inverse = jnp.concatenate([inverse] * 3 + [jnp.zeros_like(inverse)])

    def turns(places):
        angles = places.astype(F32)[:, None] * inverse[None, :]
        return jnp.stack([jnp.cos(angles), jnp.sin(angles)])

    inner = turns(jnp.arange(2 * block, dtype=jnp.int32))
    outer = turns(first_query + block * jnp.arange(blocks, dtype=jnp.int32))

    by_row = lambda i, s: (i, 0)
    by_step = lambda i, s: (i, 0, 0)
    lower_table = jnp.swapaxes(input_adapter_lower, 1, 2)
    lower_spec = (lower_table, (1, 5 * RANK, width), by_slot)
    ones = jnp.ones((half_dim,), F32)
    gains = jnp.stack(
        [
            jnp.concatenate([q_gain[part], q_gain[part], k_gain[part], ones])
            for part in (slice(0, half_dim), slice(half_dim, HD))
        ]
    )
    gain_attn, gain_ffn = norm_attn[None], norm_ffn[None]
    own_row = lambda i, s: (jnp.minimum(i, 3), 0)
    oth_row = lambda i, s: (jnp.maximum(i - 4, 0), 0)
    chip_row = lambda i, s: (jnp.where(i < 4, s[K] * 4 + i, (1 - s[K]) * 4 + i - 4), 0)
    normalized, narrow, queries, keyvals, raw = run(
        project_kernel,
        "project",
        (8,),
        at,
        [
            (inputs[0], (block, width), own_row),
            (tokens_other, (block, width), oth_row),
            whole(gain_attn),
            whole(dense_qkv),
            (lower_table, (1, 3 * RANK, width), by_slot),
            whole(upper_qkv),
            (inner, (2, block, cols), fixed(0, 0, 0)),
            whole(outer),
            whole(gains),
        ],
        [
            ((half, width), BF16, (block, width), chip_row),
            ((half, 3 * RANK), BF16, (block, 3 * RANK), chip_row),
            ((half, cols), BF16, (block, cols), chip_row),
            ((half, cols), BF16, (block, cols), chip_row),
            ((half, 2 * cols), F32, (block, 2 * cols), chip_row),
        ],
        [pltpu.VMEM((3 * cols, width), BF16)],
    )
    keyvals_before = lax.ppermute(keyvals, "ctx", [(0, 2), (1, 3)])

    base_here = jnp.stack([first_query, first_query]).astype(jnp.int32)
    base_before = jnp.stack([first_query, first_query - half]).astype(jnp.int32)
    segment_here = lax.dynamic_slice_in_dim(segment, first_query, half)
    size = half // 4
    seg_rows = segment_here.reshape(half // size, 1, size)
    keyvals, small_from = tie(keyvals, small_ffn)
    small_far = lax.ppermute(small_from, "tp", Z_XOR[2])
    if pair:
        keyvals, gate_up_from = tie(keyvals, gate_up_weight)
        mine_g = lax.ppermute(gate_up_from, SCT, over_y((0, 2)))
    acc = attention_forward(queries, keyvals, seg_rows, segment, base_here, size, size)
    acc, cot_here, out_rows = tie(acc, cotangent[0], jnp.concatenate([rows_here, low_rows], axis=1))
    out_own = lax.all_gather(out_rows, "tp", axis=0, tiled=True)
    cot_oth = lax.ppermute(cot_here, "ctx", CORE)
    if pair:
        acc, piece_g = tie(acc, piece_g)
        piece_gx = lax.ppermute(piece_g, "ctx", far_x)
        piece_gy = lax.ppermute(piece_g, SCT, over_y((1, 3)))
    mixed, mixed_low, lse = attention_forward(
        queries, keyvals_before, seg_rows, segment, base_before, size, 2 * size, acc
    )
    mixed_low, small_far = tie(mixed_low, small_far)
    small_ffn = jnp.where(k == 0, small_ffn, small_far)
    if pair:
        mixed_low, piece_d, piece_gx, piece_gy, down_from = tie(
            mixed_low, piece_d, piece_gx, piece_gy, down_weight
        )
        mine_d = lax.ppermute(down_from, SCT, over_y((0, 2)))
        piece_gxy = lax.ppermute(piece_gy, "ctx", far_x)
        piece_dx = lax.ppermute(piece_d, "ctx", far_x)
        piece_dy = lax.ppermute(piece_d, SCT, over_y((1, 3)))

    mixed_all = heads_tokens(mixed_low.reshape(8, sub, cols))
    qkv_rows = rows_at(jnp.concatenate([dense_qkv, upper_qkv], axis=1), x, cols)
    mixed_all, small_ffn, cot_oth, qkv_rows = tie(mixed_all, small_ffn, cot_oth, qkv_rows)
    out_oth = lax.ppermute(out_own, "ctx", CORE)
    if pair:
        mixed_all, mine_g, piece_gxy, piece_dx, piece_dy, out_own = tie(
            mixed_all, mine_g, piece_gxy, piece_dx, piece_dy, out_own
        )
        piece_dxy = lax.ppermute(piece_dy, "ctx", far_x)
        sources = [gate_up_weight, mine_g, piece_g, piece_gx, piece_gy, piece_gxy]
        down_sources = [down_weight, mine_d, piece_d, piece_dx, piece_dy, piece_dxy]
    else:
        full_g = lax.all_gather(gate_up_weight, "shard", axis=1, tiled=True)
        full_d = lax.all_gather(down_weight, "shard", axis=1, tiled=True)
        sources = [jnp.where(k == 0, full_g, lax.ppermute(full_g, "tp", Z_XOR[2]))]
        down_sources = [jnp.where(k == 0, full_d, lax.ppermute(full_d, "tp", Z_XOR[2]))]
    z_block = lambda i, s: (0, s[Z], 0)
    upper_out_spec = (output_adapter_upper, (1, RANK, width), lambda i, s: (s[SLOT], 0, 0))
    hidden_state, normalized_second, narrow_out = run(
        mix_kernel,
        "mix",
        (1,),
        at,
        [
            whole(mixed_all),
            whole(out_own),
            whole(out_oth),
            upper_out_spec,
            (inputs, (1, sub, width), z_block),
            whole(gain_ffn),
        ],
        [
            out_whole((sub, width), F32),
            out_whole((sub, width), BF16),
            out_whole((sub, RANK), BF16),
        ],
    )

    second = normalized_second
    second_oth = lax.ppermute(second, "ctx", CORE)
    second_far = lax.ppermute(second, "tp", Z_XOR[1])
    second_far_oth = lax.ppermute(second_far, "ctx", CORE)
    upper_down_spec = (down_adapter_upper, (1, RANK, width), by_slot)
    z_far = lambda i, s: (0, s[Z] ^ 1, 0)
    ffn_tokens = [
        whole(second),
        whole(second_far),
        whole(second_oth),
        whole(second_far_oth),
        (cotangent, (1, sub, width), z_block),
        (cotangent, (1, sub, width), z_far),
        (cot_oth, (sub, width), lambda i, s: (s[Z], 0)),
        (cot_oth, (sub, width), lambda i, s: (s[Z] ^ 1, 0)),
    ]
    tall = 2 * sub
    qkv_rows, second_far_oth = tie(qkv_rows, second_far_oth)
    qkv_own = lax.all_gather(qkv_rows, "tp", axis=0, tiled=True)
    ffn_tokens[3] = whole(second_far_oth)
    part_own, part_oth, active, grad_both, narrow_second, narrow_back_second = run(
        functools.partial(ffn_kernel, len(sources)),
        "ffn",
        (2,),
        at,
        ffn_tokens
        + [lower_spec, whole(small_ffn), upper_down_spec]
        + [(source, None, None) for source in sources + down_sources],
        [
            out_whole((tall, width), BF16),
            out_whole((tall, width), BF16),
            ((2, tall, hidden_units), BF16, (1, tall, hidden_units), by_step),
            ((2, tall, 2 * hidden_units), BF16, (1, tall, 2 * hidden_units), by_step),
            ((2, tall, 2 * RANK), BF16, (1, tall, 2 * RANK), by_step),
            ((2, tall, RANK), BF16, (1, tall, RANK), by_step),
        ],
        [
            pltpu.VMEM((width, 2 * hidden_units), BF16),
            pltpu.VMEM((hidden_units, width + cols), BF16),
            pltpu.VMEM((2, width, cols), BF16),
            pltpu.SemaphoreType.DMA((2, 4)),
        ],
        LONG,
    )
    part_arrived = lax.ppermute(part_oth, "ctx", CORE)
    part_give = (part_own[sub:].astype(F32) + part_arrived[sub:].astype(F32)).astype(BF16)
    part_give, active, qkv_own = tie(part_give, active, qkv_own)
    part_far = lax.ppermute(part_give, "tp", Z_XOR[1])
    qkv_own_x = lax.ppermute(qkv_own, "ctx", XSIDE)

    down_own, down_oth, zd = run(
        functools.partial(ffn_down_kernel, len(sources)),
        "ffn_down",
        (2,),
        at,
        [
            (active, (1, tall, hidden_units), by_step),
            whole(small_ffn),
            upper_down_spec,
        ]
        + [(source, None, None) for source in down_sources],
        [
            out_whole((tall, width), BF16),
            out_whole((tall, width), BF16),
            ((2, tall, RANK), BF16, (1, tall, RANK), by_step),
        ],
        [pltpu.VMEM((hidden_units, width + cols), BF16), pltpu.SemaphoreType.DMA((1, 4))],
        LONG,
    )
    hidden_back, down_own, down_oth, zd = tie(hidden_state, down_own, down_oth, zd)

    grad_hidden, grad_hidden_low, grad_mixed_all, narrow_back = run(
        mix_back_kernel,
        "mix_back",
        (1,),
        at,
        [
            whole(hidden_back),
            (cotangent, (1, sub, width), z_block),
            whole(part_own),
            whole(part_arrived),
            whole(part_far),
            whole(gain_ffn),
            whole(out_own),
            whole(out_oth),
            upper_out_spec,
        ],
        [
            out_whole((sub, width), F32),
            out_whole((sub, width), BF16),
            out_whole((8, sub, cols), BF16),
            out_whole((sub, RANK), BF16),
        ],
    )
    grad_mixed_all, grad_both, down_oth = tie(grad_mixed_all, grad_both, down_oth)
    grad_mixed = heads_tokens(grad_mixed_all).reshape(half, cols)
    down_arrived = lax.ppermute(down_oth, "ctx", CORE)
    down_give = (down_own[sub:].astype(F32) + down_arrived[sub:].astype(F32)).astype(BF16)
    down_far = lax.ppermute(down_give, "tp", Z_XOR[1])
    final = hidden_state + (
        down_own[:sub].astype(F32) + down_arrived[:sub].astype(F32) + down_far.astype(F32)
    )
    final = final.astype(BF16)
    wide_ffn, quarter_grads = run(
        ffn_grads_kernel,
        "ffn_grads",
        (2,),
        at,
        ffn_tokens
        + [
            (active, (1, tall, hidden_units), by_step),
            (grad_both, (1, tall, 2 * hidden_units), by_step),
            (narrow_second, (1, tall, 2 * RANK), by_step),
            (narrow_back_second, (1, tall, RANK), by_step),
            (zd, (1, tall, RANK), by_step),
            whole(small_ffn),
        ],
        [out_whole((3 * RANK, width), BF16), out_whole((3 * RANK, hidden_units), BF16)],
        [
            pltpu.VMEM((2 * hidden_units, cols), BF16),
            pltpu.VMEM((3 * RANK, width), F32),
            pltpu.VMEM((3 * RANK, hidden_units), F32),
        ],
        LONG,
    )
    (wide_mix,) = run(
        mix_grads_kernel,
        "mix_grads",
        (1,),
        at,
        [whole(mixed_all), whole(grad_hidden_low), whole(narrow_out), whole(narrow_back)],
        [out_whole((2 * RANK, width), BF16)],
    )
    wide_early = jnp.concatenate([wide_mix, wide_ffn], axis=0)
    grad_mixed, wide_early, final, qkv_own_x = tie(grad_mixed, wide_early, final, qkv_own_x)
    wide_near = lax.ppermute(wide_early, "tp", Z_XOR[1])
    out_up_1 = lax.ppermute(final, "tp", UP)
    out_down_1 = lax.ppermute(final, "tp", DOWN)
    if pair:
        slot_other = lax.ppermute(adapter_index, "shard", swap_y)[0]

    dq_before, dkv_before = attention_backward(
        queries,
        keyvals_before,
        seg_rows,
        grad_mixed,
        mixed,
        lse,
        segment,
        base_before,
        size,
        size,
    )
    dkv_after = lax.ppermute(dkv_before, "ctx", [(2, 0), (3, 1)])
    dq_before, wide_near, quarter_grads, qkv_own, qkv_own_x, out_up_1, out_down_1 = tie(
        dq_before, wide_near, quarter_grads, qkv_own, qkv_own_x, out_up_1, out_down_1
    )
    out_up_2 = lax.ppermute(out_up_1, "tp", UP)
    out_down_2 = lax.ppermute(out_down_1, "tp", DOWN)
    if pair:
        dq_before, slot_other = tie(dq_before, slot_other)
    qkv_oth = lax.ppermute(qkv_own, "ctx", CORE)
    qkv_oth_x = lax.ppermute(qkv_own_x, "ctx", CORE)
    wide_early = plus(wide_early, wide_near)
    wide_far = lax.ppermute(wide_early, "tp", Z_XOR[2])
    quarter_far = lax.ppermute(quarter_grads, "tp", Z_XOR[2])
    dq, dkv = attention_backward(
        queries,
        keyvals,
        seg_rows,
        grad_mixed,
        mixed,
        lse,
        segment,
        base_here,
        size,
        size,
        dq_before,
    )
    dq, wide_far, quarter_far, out_up_2, out_down_2 = tie(
        dq, wide_far, quarter_far, out_up_2, out_down_2
    )
    out_up_3 = lax.ppermute(out_up_2, "tp", UP)
    out_down_3 = lax.ppermute(out_down_2, "tp", DOWN)
    wide_early = plus(wide_early, wide_far)
    tall_blocks = blocks // 2
    d_projected, wide_attn, head_grads = run(
        project_back_kernel,
        "project_back",
        (tall_blocks,),
        at,
        [
            (dq, (2 * block, cols), by_row),
            (dkv, (2 * block, cols), by_row),
            (dkv_after, (2 * block, cols), by_row),
            (raw, (2 * block, 2 * cols), by_row),
            whole(inner),
            whole(outer),
            whole(gains),
            (narrow, (2 * block, 3 * RANK), by_row),
            (normalized, (2 * block, width), by_row),
            whole(upper_qkv),
        ],
        [
            ((half, 2 * cols), BF16, (2 * block, 2 * cols), by_row),
            out_whole((3 * RANK, width), BF16),
            out_whole((RANK, 4 * cols), BF16),
        ],
        [pltpu.VMEM((3 * RANK, width), F32), pltpu.VMEM((3 * RANK, 2 * cols), F32)],
        LONG,
    )
    d_projected, out_up_3, out_down_3 = tie(d_projected, out_up_3, out_down_3)

    d_all = heads_tokens(d_projected.reshape(8, sub, 2 * cols))
    def lanes_to(value, size):
        return jnp.pad(value, ((0, 0), (0, size - value.shape[1])))

    wide_count = 8 * RANK
    packed = jnp.concatenate(
        [
            lanes_to(jnp.concatenate([wide_early, wide_attn], axis=0), hidden_units),
            jnp.where(k == 0, quarter_grads, quarter_far),
            lanes_to(head_grads, hidden_units),
        ],
        axis=0,
    )

    packed = plus(packed, lax.ppermute(packed, "ctx", CORE))
    packed = plus(packed, lax.ppermute(packed, "ctx", XSIDE))
    slots = jnp.arange(ADAPT, dtype=jnp.int32)

    def placed(value, which):
        mask = (slots == which).astype(F32).reshape((ADAPT,) + (1,) * value.ndim)
        return mask * value.astype(F32)[None]

    if pair:
        both = jnp.stack([packed, lax.ppermute(packed, "shard", swap_y)])
    else:
        both = lax.psum(placed(packed, slot), "shard")
    (grad_tokens,) = run(
        last_kernel,
        "last",
        (1,),
        at,
        [
            whole(d_all),
            whole(qkv_own),
            whole(qkv_own_x),
            whole(qkv_oth),
            whole(qkv_oth_x),
            (lower_table, (1, 3 * RANK, width), by_slot),
            whole(grad_hidden),
            (inputs, (1, sub, width), z_block),
            whole(gain_attn),
        ],
        [out_whole((sub, width), BF16)],
    )
    up_1 = lax.ppermute(grad_tokens, "tp", UP)
    down_1 = lax.ppermute(grad_tokens, "tp", DOWN)
    own_width = width // (shards * 4)
    in_attn = rows_at(both[:, 5 * RANK : wide_count, :width], y * 4 + ctx, own_width, 2)
    in_attn = plus(in_attn, lax.ppermute(in_attn, "tp", Z_XOR[1]))
    up_1, down_1, in_attn, both = tie(up_1, down_1, in_attn, both)
    up_2 = lax.ppermute(up_1, "tp", UP)
    down_2 = lax.ppermute(down_1, "tp", DOWN)
    in_far = lax.ppermute(in_attn, "tp", Z_XOR[2])
    wide = both[:, : 5 * RANK, :width]
    in_ffn = rows_at(wide[:, 3 * RANK :], y * 4 + ctx, own_width, 2)
    rest = both[:, wide_count:]
    if pair:
        slots_here = (slot, slot_other)
        rest = sum(placed(rest[i], which) for i, which in enumerate(slots_here))
    quarter_sum, heads = rest[:, : 3 * RANK], rest[:, 3 * RANK :, : 4 * cols]
    grad_b_query = jnp.concatenate([heads[..., :cols], heads[..., 2 * cols : 3 * cols]], axis=-1)
    grad_b_keyval = jnp.stack(
        [
            jnp.concatenate(
                [heads[..., core * 2 * cols + c * HD :][..., :HD] for core in range(2)], axis=-1
            )
            for c in (2, 3)
        ],
        axis=1,
    )
    grad_b_gate_up = quarter_sum[:, : 2 * RANK].reshape(ADAPT, 2, RANK, -1)
    grad_a_down = jnp.swapaxes(quarter_sum[:, 2 * RANK :], 1, 2)
    in_all = jnp.concatenate([plus(in_attn, in_far), in_ffn], axis=1)
    if pair:
        wide = sum(placed(wide[i, : 3 * RANK], which) for i, which in enumerate(slots_here))
        in_all = sum(placed(in_all[i], which) for i, which in enumerate(slots_here))
    else:
        wide, in_all = wide.astype(F32), in_all.astype(F32)
    grad_b_out = wide[:, :RANK]
    grad_a_out = wide[:, RANK : 2 * RANK]
    grad_b_down = wide[:, 2 * RANK : 3 * RANK]
    grad_a_out = jnp.concatenate(
        [rows_at(grad_a_out, z, cols, 2), rows_at(grad_a_out, 4 + z, cols, 2)], axis=2
    )
    grad_a_out = jnp.swapaxes(grad_a_out, 1, 2)
    grad_adapt_in = jnp.swapaxes(in_all, 1, 2)
    up_2, down_2, final, grad_b_query, grad_b_keyval, grad_b_gate_up, grad_a_down = tie(
        up_2, down_2, final, grad_b_query, grad_b_keyval, grad_b_gate_up, grad_a_down
    )
    up_3 = lax.ppermute(up_2, "tp", UP)
    down_3 = lax.ppermute(down_2, "tp", DOWN)
    line = [grad_tokens, up_1, up_2, up_3, down_1, down_2, down_3]
    z_row = lambda i, s: (0, i, 0)
    (grad_inputs,) = run(
        assemble_kernel,
        "assemble",
        (4,),
        at,
        [whole(part) for part in line],
        [((1, tok, width), F32, (1, sub, width), z_row)],
    )
    line = [final, out_up_1, out_up_2, out_up_3, out_down_1, out_down_2, out_down_3]
    (result,) = run(
        assemble_kernel,
        "assemble_out",
        (4,),
        at,
        [whole(part) for part in line],
        [((1, tok, width), BF16, (1, sub, width), z_row)],
        cost=LONG,
    )
    return (
        result,
        grad_inputs,
        grad_adapt_in,
        grad_b_query,
        grad_b_keyval,
        grad_b_gate_up,
        grad_a_out,
        grad_b_out,
        grad_a_down,
        grad_b_down,
    )


def solution(mesh):
    return jax.shard_map(
        functools.partial(body, mesh.shape["shard"]),
        mesh=mesh,
        in_specs=(
            P("shard", "ctx", None),
            P("shard", "ctx", None),
            P("shard", None),
            P("shard"),
            P("shard", "tp"),
            P(None, "shard", "tp"),
            P("tp", "shard"),
            P(None, "shard", "tp"),
            P("tp", "shard"),
            P(),
            P(),
            P(),
            P(),
            P(),
            P(None, None, "tp"),
            P(None, None, None, "tp"),
            P(None, None, None, "tp"),
            P(None, "tp", None),
            P(),
            P(None, "tp", None),
            P(),
        ),
        out_specs=(
            P("shard", "ctx", None),
            P("shard", "ctx", None),
            P(None, ("shard", "ctx"), None),
            P(None, None, "tp"),
            P(None, None, None, "tp"),
            P(None, None, None, "tp"),
            P(None, "tp", None),
            P(),
            P(None, "tp", None),
            P(),
        ),
        check_vma=False,
    )
```

time: 615 us -> 421 us (0.68)
  Pallas kernels: 38.3 us -> 149 us
  matrix products: 77.4 us -> 0 us
  waiting for transfers between devices: 176 us -> 99.2 us
  other arithmetic: 94 us -> 20.2 us
  local copies, waits for them, and re-layouts: 63.3 us -> 12.6 us
  starting transfers between devices: 138 us -> 118 us
    pallas_call x0 -> x13, Pallas kernels: none -> 105 us  [run(): pl.pallas_call(kernel, grid_spec=pltpu.PrefetchScalarGridSpec(num_scalar_...]
    dot_general x35 -> x0, matrix products: 77.4 us -> none  [the longest x14 33.9 us: nn(): lax.dot_general(left, right, (((1,), (0,)), ((), ())), preferred_element_...]
    all_to_all x3, waiting for transfers between devices: 48.1 us -> 6.07 us  [heads_tokens(): return lax.all_to_all(value, CT, 0, 0, axis_index_groups=COLUMN, tiled=True)]
    all_to_all x7 -> x0, waiting for transfers between devices: 32 us -> none  [the longest x4 19 us: to_all(): lax.all_to_all(jnp.broadcast_to(value[None], (parts,) + value.shape), axe...]
    all_to_all x7 -> x0, starting transfers between devices: 31.8 us -> none  [the longest x4 20.7 us: to_all(): lax.all_to_all(jnp.broadcast_to(value[None], (parts,) + value.shape), axe...]
    ppermute x21 -> x43, waiting for transfers between devices: 45.2 us -> 76.1 us  [the longest x1 11.3 us: body(): second_far = lax.ppermute(second, 'tp', Z_XOR[1])]
    ppermute x1, waiting for transfers between devices: 26.6 us -> 0.01 us  [body(): dkv_after = lax.ppermute(dkv_before, 'ctx', [(2, 0), (3, 1)])]
    unnamed x197 -> x63, local copies, waits for them, and re-layouts: 31.4 us -> 6.65 us
  transfers between devices with their start and end apart: 40 -> 54, of which waited for: 16 -> 17; matrix products, arithmetic and copies ran while one was open for 31% -> 6% of each run, Pallas kernels for 6% -> 31%
where the time goes in v2:
time: 421 us; the launch traced here: 415 us
  Pallas kernels  149 us (35%)
  starting transfers between devices  118 us (28%)
  waiting for transfers between devices  99.2 us (24%)
  other arithmetic  20.2 us (5%)
  between operations  16 us (4%)
  local copies, waits for them, and re-layouts  12.6 us (3%)
    pallas_call x13, Pallas kernels, run(): pl.pallas_call(kernel, grid_spec=pltpu.PrefetchScalarGridSpec(num_scalar_...  105 us
    pallas_call x2, Pallas kernels, attention_backward(): pl.pallas_call(functools.partial(bwd_kernel, bq, bk, first), grid_spec=pl...  26.2 us
    pallas_call x2, Pallas kernels, attention_forward(): pl.pallas_call(functools.partial(fwd_kernel, bq, bk, last), grid_spec=plt...  18.1 us
    all_gather x1, waiting for transfers between devices, body(): out_own = lax.all_gather(out_rows, 'tp', axis=0, tiled=True)  17 us
    ppermute x1, starting transfers between devices, body(): packed = plus(packed, lax.ppermute(packed, 'ctx', XSIDE))  16.7 us
    all_to_all x3, starting transfers between devices, heads_tokens(): return lax.all_to_all(value, CT, 0, 0, axis_index_groups=COLUMN, tiled=True)  11.5 us
    ppermute x1, waiting for transfers between devices, body(): second_far = lax.ppermute(second, 'tp', Z_XOR[1])  11.3 us
    ppermute x1, waiting for transfers between devices, body(): in_attn = plus(in_attn, lax.ppermute(in_attn, 'tp', Z_XOR[1]))  10.4 us
  transfers between devices with their start and end apart: 54, of which 17 were waited for; matrix products, arithmetic and copies ran while one was open for 6% of the time, Pallas kernels for 31%

profile of v2, /device:TPU:0, one launch (start us, length us, event | category | flops | bytes accessed | tf_op | source)
XLA Modules:
  0.0 414.7 jit_solution(3498796654580734716)
XLA Ops:
  8.6 3.0 prepare.1
  11.6 3.0 collective-permute-start.1
  14.8 3.4 pieces.1
  19.0 1.5 collective-permute-start.6
  28.1 12.9 %project.1 = (bf16[2048,1024]{1,0:T(8,128)(2,1)}, bf16[2048,48]{1,0:T(8,128)(2,1)}, bf16[2048,128]{1,0:T(8,128)(2,1)}, bf16[2048,128]{1,0:T(8,128)(2,1)}, f32[2048,256]{1,0:T(8,128)}) custom-call(s32[5]{0:T(128)} %stack.70.at, bf16[1024,1024]{1,0:T(8,128)(2,1)} %bitcast.63, bf16[1024,1024]{1,0:T(8,128)(2,1)} %collective-permute-done.oth, ...), custom_call_target="tpu_custom_call" | custom-call | flops 1048576 | bytes 65536 | tf_op jit(solution)/shard_map/project/pallas_call | solution.py:271
  41.0 4.5 %collective-permute-start.2 = (bf16[2048,128]{1,0:T(8,128)(2,1)}, bf16[2048,128]{1,0:T(8,128)(2,1)}, u32[]{:S(2)}, u32[]{:S(2)}) collective-permute-start(bf16[2048,128]{1,0:T(8,128)(2,1)} %get-tuple-element.126.kv_ref), channel_id=1, source_target_pairs={{0,8},{4,12},{1,9},{5,13},{2,10},{6,14},{3,11},{7,15},{16,24},{20,... | collective-permute-start | bytes 1572872 | tf_op jit(solution)/shard_map/ppermute | solution.py:917
  45.5 2.6 collective-permute-start.5
  48.1 11.4 %attn_fwd_first.1.rest_0_ = f32[2,2048,128]{2,1,0:T(8,128)} custom-call(s32[4096]{0:T(1024)} %bitcast.85, s32[2]{0:T(128)} %pad_add_fusion.base, bf16[2048,128]{1,0:T(8,128)(2,1)} %get-tuple-element.122.q_ref, bf16[2048,128]{1,0:T(8,128)(2,1)} %get-tuple-element.126.kv_ref, s32[4,1,512]{2,1,0:T(1,128)} %bitcast.81), custom_call_target="tpu_custom_call" | custom-call | flops 32212254720 | bytes 16777216 | tf_op jit(solution)/shard_map/attn_fwd_first/pallas_call | solution.py:164
  59.5 1.7 collective-permute-start.7
  61.2 1.7 collective-permute-start.8
  63.0 6.9 %collective-permute-start.9 = (bf16[1024,1024]{1,0:T(8,128)(2,1)}, bf16[1024,1024]{1,0:T(8,128)(2,1)}, u32[]{:S(2)}, u32[]{:S(2)}) collective-permute-start(bf16[1024,1024]{1,0:T(8,128)(2,1)} %bitcast.69), channel_id=1, source_target_pairs={{0,4},{4,0},{8,12},{12,8},{1,5},{5,1},{9,13},{13,9},{2,6},{6,2},{1... | collective-permute-start | bytes 6291464 | tf_op jit(solution)/shard_map/ppermute | solution.py:932
  69.9 2.2 collective-permute-start.10
  72.1 6.7 %attn_fwd_last.1 = (f32[2048,128]{1,0:T(8,128)}, bf16[2048,128]{1,0:T(8,128)(2,1)}, f32[4,1,1024]{2,1,0:T(1,128)}) custom-call(s32[4096]{0:T(1024)} %bitcast.86, s32[2]{0:T(128)} %pad_add_fusion.1.base, bf16[2048,128]{1,0:T(8,128)(2,1)} %get-tuple-element.122.q_ref, bf16[2048,128]{1,0:T(8,128)(2,1)} %collective-permute-done.2.kv_ref, s32[4,1,512]{2,1,0:T(1,128)} %bitcast.82, ...), custom_call_target="tpu_custom_call" | custom-call | flops 32212254720 | bytes 16777216 | tf_op jit(solution)/shard_map/attn_fwd_last/pallas_call | solution.py:164
  81.0 17.0 %all-gather.3.cloned.1.call-done.out_own = bf16[512,1152]{1,0:T(8,128)(2,1)} async-done(((bf16[128,1152]{1,0:T(8,128)(2,1)}), bf16[512,1152]{1,0:T(8,128)(2,1)}) %all-gather.3.cloned.1.call-update) | async-done | bytes 1179664 | tf_op jit(solution)/shard_map/all_gather | solution.py:931
  98.0 3.6 all-to-all-start
  101.7 1.5 collective-permute-start.13
  103.2 1.6 fusion.5
  104.8 4.0 collective-permute-start.18
  108.9 1.6 broadcast_select_fusion.5.rest_1_.small.rest_5_
  110.4 6.1 %all-to-all-done.mixed = bf16[8,256,128]{2,1,0:T(8,128)(2,1)S(1)} async-done(((bf16[8,256,128]{2,1,0:T(8,128)(2,1)}), bf16[8,256,128]{2,1,0:T(8,128)(2,1)S(1)}, u32[]{:S(2)}, u32[]{:S(2)}) %all-to-all-start) | async-done | bytes 524320 | tf_op jit(solution)/shard_map/all_to_all | solution.py:749
  118.6 4.9 %mix.1 = (f32[256,1024]{1,0:T(8,128)}, bf16[256,1024]{1,0:T(8,128)(2,1)}, bf16[256,16]{1,0:T(8,128)(2,1)}) custom-call(s32[5]{0:T(128)} %stack.70.at, bf16[8,256,128]{2,1,0:T(8,128)(2,1)} %copy-done, bf16[512,1152]{1,0:T(8,128)(2,1)} %all-gather.3.cloned.1.call-done.out_own, bf16[512,1152]{1,0:T(8,128)(2,1)} %copy-done.1, bf16[8,16,1024]{2,1,0:T(8,128)(2,1)} %upper.5, ...), custom_call_target="tpu_custom_call" | custom-call | flops 1048576 | bytes 65536 | tf_op jit(solution)/shard_map/mix/pallas_call | solution.py:271
  124.3 11.3 %collective-permute-done.15.far = bf16[256,1024]{1,0:T(8,128)(2,1)S(1)} collective-permute-done((bf16[256,1024]{1,0:T(8,128)(2,1)}, bf16[256,1024]{1,0:T(8,128)(2,1)S(1)}, u32[]{:S(2)}, u32[]{:S(2)}) %collective-permute-start.15) | collective-permute-done | bytes 524320 | tf_op jit(solution)/shard_map/ppermute | solution.py:991
  135.7 2.6 collective-permute-start.17
  138.3 2.2 collective-permute-done.17.far_oth
  141.5 25.0 %ffn.1 = (bf16[512,1024]{1,0:T(8,128)(2,1)}, bf16[512,1024]{1,0:T(8,128)(2,1)}, bf16[2,512,1152]{2,1,0:T(8,128)(2,1)}, bf16[2,512,2304]{2,1,0:T(8,128)(2,1)}, bf...) custom-call(s32[5]{0:T(128)} %stack.70.at, bf16[256,1024]{1,0:T(8,128)(2,1)} %get-tuple-element.148.own, ...), custom_call_target="tpu_custom_call" | custom-call | flops 32212254720 | bytes 16777216 | tf_op jit(solution)/shard_map/ffn/pallas_call | solution.py:271
  167.0 2.5 collective-permute-done.20.arrived
  169.5 1.6 add_convert_fusion.2
  171.8 10.6 %ffn_down.1 = (bf16[512,1024]{1,0:T(8,128)(2,1)}, bf16[512,1024]{1,0:T(8,128)(2,1)}, bf16[2,512,16]{2,1,0:T(8,128)(2,1)}) custom-call(s32[5]{0:T(128)} %stack.70.at, bf16[2,512,1152]{2,1,0:T(8,128)(2,1)} %get-tuple-element.163.act.rest_0_, bf16[3,16,1152]{2,1,0:T(8,128)(2,1)} %broadcast_select_fusion.5.rest_1_.small.rest_5_, bf16[8,16,1024]{2,1,0:T(8,128)(2,1)} %upper.4, ...), custom_call_target="tpu_custom_call" | custom-call | flops 32212254720 | bytes 16777216 | tf_op jit(solution)/shard_map/ffn_down/pallas_call | solution.py:271
  182.4 3.0 collective-permute-done.21.far
  185.4 5.9 %mix_back.1 = (f32[256,1024]{1,0:T(8,128)}, bf16[256,1024]{1,0:T(8,128)(2,1)}, bf16[8,256,128]{2,1,0:T(8,128)(2,1)}, bf16[256,16]{1,0:T(8,128)(2,1)}) custom-call(s32[5]{0:T(128)} %stack.70.at, f32[256,1024]{1,0:T(8,128)} %get-tuple-element.167.hidden, bf16[1,1024,1024]{2,1,0:T(8,128)(2,1)} %cot_far.3, bf16[512,1024]{1,0:T(8,128)(2,1)} %get-tuple-element.159.own, ...), custom_call_target="tpu_custom_call" | custom-call | flops 1048576 | bytes 65536 | tf_op jit(solution)/shard_map/mix_back/pallas_call | solution.py:271
  191.3 2.1 collective-permute-start.28
  193.4 1.8 collective-permute-start.24
  195.2 4.4 %all-to-all-start.1 = ((bf16[8,256,128]{2,1,0:T(8,128)(2,1)}), bf16[8,256,128]{2,1,0:T(8,128)(2,1)}, u32[]{:S(2)}, u32[]{:S(2)}) async-start(bf16[8,256,128]{2,1,0:T(8,128)(2,1)} %get-tuple-element.172), calls=%async_computation.1 | async-start | bytes 1048576 | tf_op jit(solution)/shard_map/all_to_all | solution.py:749
  200.6 1.9 collective-permute-start.23
  202.4 10.8 %ffn_grads.1 = (bf16[48,1024]{1,0:T(8,128)(2,1)}, bf16[48,1152]{1,0:T(8,128)(2,1)}) custom-call(s32[5]{0:T(128)} %stack.70.at, bf16[256,1024]{1,0:T(8,128)(2,1)} %get-tuple-element.148.own, bf16[256,1024]{1,0:T(8,128)(2,1)} %copy-done.29, bf16[256,1024]{1,0:T(8,128)(2,1)} %collective-permute-done.16.own_oth, bf16[256,1024]{1,0:T(8,128)(2,1)} %copy-done.30, ...), custom_call_target="tpu_custom_call" | custom-call | flops 32212254720 | bytes 16777216 | tf_op jit(solution)/shard_map/ffn_grads/pallas_call | solution.py:271
  213.2 2.9 mix_grads.1
  217.1 5.4 %collective-permute-done.23 = bf16[256,1024]{1,0:T(8,128)(2,1)} collective-permute-done((bf16[256,1024]{1,0:T(8,128)(2,1)S(1)}, bf16[256,1024]{1,0:T(8,128)(2,1)}, u32[]{:S(2)}, u32[]{:S(2)}) %collective-permute-start.23) | collective-permute-done | bytes 524320 | tf_op jit(solution)/shard_map/ppermute | solution.py:1087
  222.4 1.7 add_convert_fusion.own
  224.1 3.2 collective-permute-start.26
  228.6 2.7 collective-permute-start.25
  231.3 6.8 %attn_bwd_first.1 = (f32[2048,128]{1,0:T(8,128)}, bf16[2048,128]{1,0:T(8,128)(2,1)}) custom-call(s32[4096]{0:T(1024)} %bitcast.87, s32[2]{0:T(128)} %pad_add_fusion.1.base, bf16[2048,128]{1,0:T(8,128)(2,1)} %get-tuple-element.122.q_ref, bf16[2048,128]{1,0:T(8,128)(2,1)} %collective-permute-done.2.kv_ref, s32[4,1,512]{2,1,0:T(1,128)} %bitcast.83, ...), custom_call_target="tpu_custom_call" | custom-call | flops 32212254720 | bytes 16777216 | tf_op jit(solution)/shard_map/attn_bwd_first/pallas_call | solution.py:251
  239.4 6.7 %collective-permute-done.25 = bf16[80,1024]{1,0:T(8,128)(2,1)S(1)} collective-permute-done((bf16[80,1024]{1,0:T(8,128)(2,1)S(1)}, bf16[80,1024]{1,0:T(8,128)(2,1)S(1)}, u32[]{:S(2)}, u32[]{:S(2)}) %collective-permute-start.25) | collective-permute-done | bytes 163872 | tf_op jit(solution)/shard_map/ppermute | solution.py:1124
  246.2 1.7 collective-permute-start.29
  250.7 4.4 %collective-permute-start.30 = (bf16[48,1152]{1,0:T(8,128)(2,1)S(1)}, bf16[48,1152]{1,0:T(8,128)(2,1)S(1)}, u32[]{:S(2)}, u32[]{:S(2)}) collective-permute-start(bf16[48,1152]{1,0:T(8,128)(2,1)S(1)} %copy-done.18), channel_id=1, source_target_pairs={{0,2},{1,3},{2,0},{3,1},{4,6},{5,7},{6,4},{7,5},{8,10},{9,11},{10,... | collective-permute-start | bytes 331784 | tf_op jit(solution)/shard_map/ppermute | solution.py:1154
  255.1 19.4 %attn_bwd_last.1 = (f32[2048,128]{1,0:T(8,128)}, f32[2048,128]{1,0:T(8,128)}) custom-call(s32[4096]{0:T(1024)} %bitcast.88, s32[2]{0:T(128)} %pad_add_fusion.base, bf16[2048,128]{1,0:T(8,128)(2,1)} %get-tuple-element.122.q_ref, bf16[2048,128]{1,0:T(8,128)(2,1)} %get-tuple-element.126.kv_ref, s32[4,1,512]{2,1,0:T(1,128)} %bitcast.84, ...), custom_call_target="tpu_custom_call" | custom-call | flops 32212254720 | bytes 16777216 | tf_op jit(solution)/shard_map/attn_bwd_last/pallas_call | solution.py:251
  274.7 3.5 collective-permute-start.34
  278.1 1.5 collective-permute-start.35
  279.7 9.3 %project_back.1 = (bf16[2048,256]{1,0:T(8,128)(2,1)}, bf16[48,1024]{1,0:T(8,128)(2,1)}, bf16[16,512]{1,0:T(8,128)(2,1)}) custom-call(s32[5]{0:T(128)} %stack.70.at, f32[2048,128]{1,0:T(8,128)} %get-tuple-element.199.dq, f32[2048,128]{1,0:T(8,128)} %get-tuple-element.200.dkv, bf16[2048,128]{1,0:T(8,128)(2,1)} %collective-permute-done.33.dkv_after, ...), custom_call_target="tpu_custom_call" | custom-call | flops 32212254720 | bytes 16777216 | tf_op jit(solution)/shard_map/project_back/pallas_call | solution.py:271
  291.7 3.6 all-to-all-start.2
  295.4 16.7 %collective-permute-start.41 = (bf16[192,1152]{1,0:T(8,128)(2,1)S(1)}, bf16[192,1152]{1,0:T(8,128)(2,1)S(1)}, u32[]{:S(2)}, u32[]{:S(2)}) collective-permute-start(bf16[192,1152]{1,0:T(8,128)(2,1)S(1)} %add_convert_fusion.4), channel_id=1, source_target_pairs={{0,8},{4,12},{8,0},{12,4},{1,9},{5,13},{9,1},{13,5},{2,10},{6,14},... | collective-permute-start | bytes 1327112 | tf_op jit(solution)/shard_map/ppermute | solution.py:1217
  312.6 10.3 %collective-permute-done.41 = bf16[192,1152]{1,0:T(8,128)(2,1)S(1)} collective-permute-done((bf16[192,1152]{1,0:T(8,128)(2,1)S(1)}, bf16[192,1152]{1,0:T(8,128)(2,1)S(1)}, u32[]{:S(2)}, u32[]{:S(2)}) %collective-permute-start.41) | collective-permute-done | bytes 442400 | tf_op jit(solution)/shard_map/ppermute | solution.py:1217
  323.1 6.1 %collective-permute-start.42 = (bf16[192,1152]{1,0:T(8,128)(2,1)S(1)}, bf16[192,1152]{1,0:T(8,128)(2,1)S(1)}, u32[]{:S(2)}, u32[]{:S(2)}) collective-permute-start(bf16[192,1152]{1,0:T(8,128)(2,1)S(1)} %add_convert_fusion.3), channel_id=1, source_target_pairs={{0,16},{16,0},{1,17},{17,1},{2,18},{18,2},{3,19},{19,3},{4,20},{20... | collective-permute-start | bytes 1327112 | tf_op jit(solution)/shard_map/ppermute | solution.py:1225
  330.5 8.9 %collective-permute-done.42 = bf16[192,1152]{1,0:T(8,128)(2,1)S(1)} collective-permute-done((bf16[192,1152]{1,0:T(8,128)(2,1)S(1)}, bf16[192,1152]{1,0:T(8,128)(2,1)S(1)}, u32[]{:S(2)}, u32[]{:S(2)}) %collective-permute-start.42) | collective-permute-done | bytes 442400 | tf_op jit(solution)/shard_map/ppermute | solution.py:1225
  341.1 6.6 %last.1.own = bf16[256,1024]{1,0:T(8,128)(2,1)} custom-call(s32[5]{0:T(128)} %stack.70.at, bf16[8,256,256]{2,1,0:T(8,128)(2,1)} %copy-done.2, bf16[512,1152]{1,0:T(8,128)(2,1)} %all-gather.5.cloned.1.call-done.own, bf16[512,1152]{1,0:T(8,128)(2,1)} %collective-permute-done.24.own_x, bf16[512,1152]{1,0:T(8,128)(2,1)} %collective-permute-done.36.oth, ...), custom_call_target="tpu_custom_call" | custom-call | flops 1048576 | bytes 65536 | tf_op jit(solution)/shard_map/last/pallas_call | solution.py:271
  347.6 3.3 collective-permute-start.38
  353.0 2.7 collective-permute-start.43
  355.8 10.4 %collective-permute-done.43 = bf16[2,48,128]{2,1,0:T(8,128)(2,1)S(1)} collective-permute-done((bf16[2,48,128]{2,1,0:T(8,128)(2,1)S(1)}, bf16[2,48,128]{2,1,0:T(8,128)(2,1)S(1)}, u32[]{:S(2)}, u32[]{:S(2)}) %collective-permute-start.43) | collective-permute-done | bytes 24608 | tf_op jit(solution)/shard_map/ppermute | solution.py:1250
  369.0 2.3 collective-permute-start.48
  377.7 4.4 %collective-permute-done.44.rest_1_ = bf16[256,1024]{1,0:T(8,128)(2,1)S(1)} collective-permute-done((bf16[256,1024]{1,0:T(8,128)(2,1)S(1)}, bf16[256,1024]{1,0:T(8,128)(2,1)S(1)}, u32[]{:S(2)}, u32[]{:S(2)}) %collective-permute-start.44) | collective-permute-done | bytes 524320 | tf_op jit(solution)/shard_map/ppermute | solution.py:1252
  382.1 4.0 collective-permute-done.45.rest_4_
  386.1 3.4 collective-permute-start.46
  390.8 4.5 %assemble_out.1 = bf16[1,1024,1024]{2,1,0:T(8,128)(2,1)} custom-call(s32[5]{0:T(128)} %stack.70.at, bf16[256,1024]{1,0:T(8,128)(2,1)} %copy-done.13, bf16[256,1024]{1,0:T(8,128)(2,1)} %collective-permute-done.26.rest_0_, bf16[256,1024]{1,0:T(8,128)(2,1)} %copy-done.28, bf16[256,1024]{1,0:T(8,128)(2,1)} %collective-permute-done.34.rest_2_, ...), custom_call_target="tpu_custom_call" | custom-call | flops 32212254720 | bytes 16777216 | tf_op jit(solution)/shard_map/assemble_out/pallas_call | solution.py:271
  397.2 4.4 %collective-permute-done.47.rest_5_ = bf16[256,1024]{1,0:T(8,128)(2,1)S(1)} collective-permute-done((bf16[256,1024]{1,0:T(8,128)(2,1)}, bf16[256,1024]{1,0:T(8,128)(2,1)S(1)}, u32[]{:S(2)}, u32[]{:S(2)}) %collective-permute-start.47) | collective-permute-done | bytes 524320 | tf_op jit(solution)/shard_map/ppermute | solution.py:1292
  402.3 5.1 %assemble.1 = f32[1,1024,1024]{2,1,0:T(8,128)} custom-call(s32[5]{0:T(128)} %stack.70.at, bf16[256,1024]{1,0:T(8,128)(2,1)} %last.1.own, bf16[256,1024]{1,0:T(8,128)(2,1)} %copy-done.8, bf16[256,1024]{1,0:T(8,128)(2,1)} %copy-done.10, bf16[256,1024]{1,0:T(8,128)(2,1)} %copy-done.11, bf16[256,1024]{1,0:T(8,128)(2,1)} %copy-done.9, ...), custom_call_target="tpu_custom_call" | custom-call | flops 1048576 | bytes 65536 | tf_op jit(solution)/shard_map/assemble/pallas_call | solution.py:271
  (187 shorter events, 45.5 us)
Async XLA Ops:
  7.2 90.8 %all-gather.3.cloned.1.call-start = ((), (), s32[]{:S(2)}) async-start(), calls=%async_computation.3 | async-start | bytes 1474560 | tf_op jit(solution)/shard_map/all_gather | solution.py:931
  11.6 14.9 %collective-permute-start.1 = (bf16[256,512]{1,0:T(8,128)(2,1)}, bf16[256,512]{1,0:T(8,128)(2,1)S(1)}, u32[]{:S(2)}, u32[]{:S(2)}) collective-permute-start(bf16[256,512]{1,0:T(8,128)(2,1)} %get-tuple-element.120), channel_id=1, source_target_pairs={{0,16},{16,0},{1,17},{17,1},{2,18},{18,2},{3,19},{19,3},{4,20},{20... | collective-permute-start | bytes 786440 | tf_op jit(solution)/shard_map/ppermute | solution.py:799
  14.6 13.5 %collective-permute-start = (bf16[1024,1024]{1,0:T(8,128)(2,1)}, bf16[1024,1024]{1,0:T(8,128)(2,1)}, u32[]{:S(2)}, u32[]{:S(2)}) collective-permute-start(bf16[1024,1024]{1,0:T(8,128)(2,1)} %bitcast.62), channel_id=1, source_target_pairs={{0,4},{4,0},{8,12},{12,8},{1,5},{5,1},{9,13},{13,9},{2,6},{6,2},{1... | collective-permute-start | bytes 6291464 | tf_op jit(solution)/shard_map/ppermute | solution.py:810
  14.6 11.1 %collective-permute-start.3 = (bf16[128,512]{1,0:T(8,128)(2,1)}, bf16[128,512]{1,0:T(8,128)(2,1)S(1)}, u32[]{:S(2)}, u32[]{:S(2)}) collective-permute-start(bf16[128,512]{1,0:T(8,128)(2,1)} %get-tuple-element.127), channel_id=1, source_target_pairs={{0,16},{16,0},{1,17},{17,1},{2,18},{18,2},{3,19},{19,3},{4,20},{20... | collective-permute-start | bytes 393224 | tf_op jit(solution)/shard_map/ppermute | solution.py:799
  18.1 41.4 %collective-permute-start.4 = (bf16[512,1152]{1,0:T(8,128)(2,1)}, bf16[512,1152]{1,0:T(8,128)(2,1)S(1)}, u32[]{:S(2)}, u32[]{:S(2)}) collective-permute-start(bf16[512,1152]{1,0:T(8,128)(2,1)} %get-tuple-element.130), channel_id=1, source_target_pairs={{4,6},{5,7},{6,4},{7,5},{12,14},{13,15},{14,12},{15,13},{20,22},{2... | collective-permute-start | bytes 3538952 | tf_op jit(solution)/shard_map/ppermute | solution.py:860
  19.0 59.8 %collective-permute-start.6 = (bf16[576,512]{1,0:T(8,128)(2,1)}, bf16[576,512]{1,0:T(8,128)(2,1)}, u32[]{:S(2)}, u32[]{:S(2)}) collective-permute-start(bf16[576,512]{1,0:T(8,128)(2,1)} %get-tuple-element.135), channel_id=1, source_target_pairs={{4,6},{5,7},{6,4},{7,5},{12,14},{13,15},{14,12},{15,13},{20,22},{2... | collective-permute-start | bytes 1769480 | tf_op jit(solution)/shard_map/ppermute | solution.py:861
  28.1 17.4 %copy-start.17 = (bf16[3,16,1152]{2,1,0:T(8,128)(2,1)S(1)}, bf16[3,16,1152]{2,1,0:T(8,128)(2,1)}, u32[]{:S(2)}) copy-start(bf16[3,16,1152]{2,1,0:T(8,128)(2,1)} %get-tuple-element.133) | copy-start | bytes 331780
  41.0 28.9 %collective-permute-start.2 = (bf16[2048,128]{1,0:T(8,128)(2,1)}, bf16[2048,128]{1,0:T(8,128)(2,1)}, u32[]{:S(2)}, u32[]{:S(2)}) collective-permute-start(bf16[2048,128]{1,0:T(8,128)(2,1)} %get-tuple-element.126.kv_ref), channel_id=1, source_target_pairs={{0,8},{4,12},{1,9},{5,13},{2,10},{6,14},{3,11},{7,15},{16,24},{20,... | collective-permute-start | bytes 1572872 | tf_op jit(solution)/shard_map/ppermute | solution.py:917
  45.5 17.4 %collective-permute-start.5 = (bf16[3,16,1152]{2,1,0:T(8,128)(2,1)S(1)}, bf16[3,16,1152]{2,1,0:T(8,128)(2,1)S(1)}, u32[]{:S(2)}, u32[]{:S(2)}) collective-permute-start(bf16[3,16,1152]{2,1,0:T(8,128)(2,1)S(1)} %copy-done.17), channel_id=1, source_target_pairs={{0,2},{1,3},{2,0},{3,1},{4,6},{5,7},{6,4},{7,5},{8,10},{9,11},{10,... | collective-permute-start | bytes 331784 | tf_op jit(solution)/shard_map/ppermute | solution.py:925
  59.5 19.2 %copy-start.25 = (bf16[512,1152]{1,0:T(8,128)(2,1)}, bf16[512,1152]{1,0:T(8,128)(2,1)S(1)}, u32[]{:S(2)}) copy-start(bf16[512,1152]{1,0:T(8,128)(2,1)S(1)} %collective-permute-done.4.rest_5_) | copy-start | bytes 3538948
  59.5 19.2 %collective-permute-start.7 = (bf16[512,1152]{1,0:T(8,128)(2,1)S(1)}, bf16[512,1152]{1,0:T(8,128)(2,1)}, u32[]{:S(2)}, u32[]{:S(2)}) collective-permute-start(bf16[512,1152]{1,0:T(8,128)(2,1)S(1)} %collective-permute-done.4.rest_5_), channel_id=1, source_target_pairs={{4,12},{12,4},{5,13},{13,5},{6,14},{14,6},{7,15},{15,7},{20,28},{2... | collective-permute-start | bytes 3538952 | tf_op jit(solution)/shard_map/ppermute | solution.py:935
  61.2 17.6 %collective-permute-start.8 = (bf16[512,1152]{1,0:T(8,128)(2,1)S(1)}, bf16[512,1152]{1,0:T(8,128)(2,1)}, u32[]{:S(2)}, u32[]{:S(2)}) collective-permute-start(bf16[512,1152]{1,0:T(8,128)(2,1)S(1)} %collective-permute-done.4.rest_5_), channel_id=1, source_target_pairs={{4,20},{5,21},{6,22},{7,23},{12,28},{13,29},{14,30},{15,31},{20,4}... | collective-permute-start | bytes 3538952 | tf_op jit(solution)/shard_map/ppermute | solution.py:936
  62.9 40.3 %copy-start.14 = (bf16[256,128]{1,0:T(8,128)(2,1)S(1)}, bf16[256,128]{1,0:T(8,128)(2,1)}, u32[]{:S(2)}) copy-start(bf16[256,128]{1,0:T(8,128)(2,1)} %get-tuple-element.121.upper) | copy-start | bytes 196612
  63.0 15.8 %copy-start.19 = (bf16[3,16,1152]{2,1,0:T(8,128)(2,1)}, bf16[3,16,1152]{2,1,0:T(8,128)(2,1)S(1)}, u32[]{:S(2)}) copy-start(bf16[3,16,1152]{2,1,0:T(8,128)(2,1)S(1)} %collective-permute-done.5) | copy-start | bytes 331780
  63.0 41.9 %collective-permute-start.9 = (bf16[1024,1024]{1,0:T(8,128)(2,1)}, bf16[1024,1024]{1,0:T(8,128)(2,1)}, u32[]{:S(2)}, u32[]{:S(2)}) collective-permute-start(bf16[1024,1024]{1,0:T(8,128)(2,1)} %bitcast.69), channel_id=1, source_target_pairs={{0,4},{4,0},{8,12},{12,8},{1,5},{5,1},{9,13},{13,9},{2,6},{6,2},{1... | collective-permute-start | bytes 6291464 | tf_op jit(solution)/shard_map/ppermute | solution.py:932
  69.9 46.6 %collective-permute-start.10 = (bf16[2,512,1152]{2,1,0:T(8,128)(2,1)}, bf16[2,512,1152]{2,1,0:T(8,128)(2,1)}, u32[]{:S(2)}, u32[]{:S(2)}) collective-permute-start(bf16[2,512,1152]{2,1,0:T(8,128)(2,1)} %rest_3_.1), channel_id=1, source_target_pairs={{0,16},{1,17},{2,18},{3,19},{8,24},{9,25},{10,26},{11,27},{16,0},{... | collective-permute-start | bytes 7077896 | tf_op jit(solution)/shard_map/ppermute | solution.py:928
  78.8 22.9 %collective-permute-start.12 = (bf16[576,512]{1,0:T(8,128)(2,1)}, bf16[576,512]{1,0:T(8,128)(2,1)}, u32[]{:S(2)}, u32[]{:S(2)}) collective-permute-start(bf16[576,512]{1,0:T(8,128)(2,1)} %collective-permute-done.6.rest_11_.rest_2_), channel_id=1, source_target_pairs={{4,12},{12,4},{5,13},{13,5},{6,14},{14,6},{7,15},{15,7},{20,28},{2... | collective-permute-start | bytes 1769480 | tf_op jit(solution)/shard_map/ppermute | solution.py:948
  80.3 36.2 %collective-permute-start.11 = (bf16[512,1152]{1,0:T(8,128)(2,1)}, bf16[512,1152]{1,0:T(8,128)(2,1)S(1)}, u32[]{:S(2)}, u32[]{:S(2)}) collective-permute-start(bf16[512,1152]{1,0:T(8,128)(2,1)} %collective-permute-done.8.rest_7_), channel_id=1, source_target_pairs={{4,12},{12,4},{5,13},{13,5},{6,14},{14,6},{7,15},{15,7},{20,28},{2... | collective-permute-start | bytes 3538952 | tf_op jit(solution)/shard_map/ppermute | solution.py:947
  98.0 18.5 %collective-permute-start.14 = (bf16[512,1152]{1,0:T(8,128)(2,1)}, bf16[512,1152]{1,0:T(8,128)(2,1)S(1)}, u32[]{:S(2)}, u32[]{:S(2)}) collective-permute-start(bf16[512,1152]{1,0:T(8,128)(2,1)} %all-gather.3.cloned.1.call-done.out_own), channel_id=1, source_target_pairs={{0,4},{4,0},{8,12},{12,8},{1,5},{5,1},{9,13},{13,9},{2,6},{6,2},{1... | collective-permute-start | bytes 3538952 | tf_op jit(solution)/shard_map/ppermute | solution.py:954
  98.0 18.5 %all-to-all-start = ((bf16[8,256,128]{2,1,0:T(8,128)(2,1)}), bf16[8,256,128]{2,1,0:T(8,128)(2,1)S(1)}, u32[]{:S(2)}, u32[]{:S(2)}) async-start(bf16[8,256,128]{2,1,0:T(8,128)(2,1)} %bitcast.74), calls=%async_computation | async-start | bytes 1048576 | tf_op jit(solution)/shard_map/all_to_all | solution.py:749
  101.6 69.5 %all-gather.5.cloned.1.call-start = ((), (), s32[]{:S(2)}) async-start(), calls=%async_computation.4 | async-start | bytes 1474560 | tf_op jit(solution)/shard_map/all_gather | solution.py:1007
  101.7 14.8 %collective-permute-start.13 = (bf16[576,512]{1,0:T(8,128)(2,1)}, bf16[576,512]{1,0:T(8,128)(2,1)}, u32[]{:S(2)}, u32[]{:S(2)}) collective-permute-start(bf16[576,512]{1,0:T(8,128)(2,1)} %collective-permute-done.6.rest_11_.rest_2_), channel_id=1, source_target_pairs={{4,20},{5,21},{6,22},{7,23},{12,28},{13,29},{14,30},{15,31},{20,4}... | collective-permute-start | bytes 1769480 | tf_op jit(solution)/shard_map/ppermute | solution.py:949
  104.8 35.7 %collective-permute-start.18 = (bf16[1152,512]{1,0:T(8,128)(2,1)}, bf16[1152,512]{1,0:T(8,128)(2,1)}, u32[]{:S(2)}, u32[]{:S(2)}) collective-permute-start(bf16[1152,512]{1,0:T(8,128)(2,1)} %rest_0_.1), channel_id=1, source_target_pairs={{0,16},{1,17},{2,18},{3,19},{8,24},{9,25},{10,26},{11,27},{16,0},{... | collective-permute-start | bytes 3538952 | tf_op jit(solution)/shard_map/ppermute | solution.py:946
  123.5 12.2 %collective-permute-start.15 = (bf16[256,1024]{1,0:T(8,128)(2,1)}, bf16[256,1024]{1,0:T(8,128)(2,1)S(1)}, u32[]{:S(2)}, u32[]{:S(2)}) collective-permute-start(bf16[256,1024]{1,0:T(8,128)(2,1)} %get-tuple-element.148.own), channel_id=1, source_target_pairs={{0,1},{1,0},{2,3},{3,2},{4,5},{5,4},{6,7},{7,6},{8,9},{9,8},{10,11... | collective-permute-start | bytes 1572872 | tf_op jit(solution)/shard_map/ppermute | solution.py:991
  123.5 17.1 %collective-permute-start.19 = (bf16[576,512]{1,0:T(8,128)(2,1)}, bf16[576,512]{1,0:T(8,128)(2,1)S(1)}, u32[]{:S(2)}, u32[]{:S(2)}) collective-permute-start(bf16[576,512]{1,0:T(8,128)(2,1)} %collective-permute-done.13.rest_13_.rest_4_), channel_id=1, source_target_pairs={{4,12},{12,4},{5,13},{13,5},{6,14},{14,6},{7,15},{15,7},{20,28},{2... | collective-permute-start | bytes 1769480 | tf_op jit(solution)/shard_map/ppermute | solution.py:959
  135.7 4.9 %collective-permute-start.17 = (bf16[256,1024]{1,0:T(8,128)(2,1)S(1)}, bf16[256,1024]{1,0:T(8,128)(2,1)S(1)}, u32[]{:S(2)}, u32[]{:S(2)}) collective-permute-start(bf16[256,1024]{1,0:T(8,128)(2,1)S(1)} %collective-permute-done.15.far), channel_id=1, source_target_pairs={{0,4},{4,0},{8,12},{12,8},{1,5},{5,1},{9,13},{13,9},{2,6},{6,2},{1... | collective-permute-start | bytes 1572872 | tf_op jit(solution)/shard_map/ppermute | solution.py:992
  138.3 2.6 collective-permute-start.16
  166.5 2.9 collective-permute-start.20
  169.5 12.9 %copy-start.5 = (bf16[512,1024]{1,0:T(8,128)(2,1)}, bf16[512,1024]{1,0:T(8,128)(2,1)S(1)}, u32[]{:S(2)}) copy-start(bf16[512,1024]{1,0:T(8,128)(2,1)S(1)} %collective-permute-done.20.arrived) | copy-start | bytes 3145732
  171.1 14.4 %collective-permute-start.21 = (bf16[256,1024]{1,0:T(8,128)(2,1)S(1)}, bf16[256,1024]{1,0:T(8,128)(2,1)}, u32[]{:S(2)}, u32[]{:S(2)}) collective-permute-start(bf16[256,1024]{1,0:T(8,128)(2,1)S(1)} %add_convert_fusion.2), channel_id=1, source_target_pairs={{0,1},{1,0},{2,3},{3,2},{4,5},{5,4},{6,7},{7,6},{8,9},{9,8},{10,11... | collective-permute-start | bytes 1572872 | tf_op jit(solution)/shard_map/ppermute | solution.py:1036
  182.4 17.2 %copy-start.6 = (bf16[512,1024]{1,0:T(8,128)(2,1)S(1)}, bf16[512,1024]{1,0:T(8,128)(2,1)}, u32[]{:S(2)}) copy-start(bf16[512,1024]{1,0:T(8,128)(2,1)} %get-tuple-element.181) | copy-start | bytes 3145732
  191.3 8.3 %collective-permute-start.22 = (bf16[512,1024]{1,0:T(8,128)(2,1)}, bf16[512,1024]{1,0:T(8,128)(2,1)S(1)}, u32[]{:S(2)}, u32[]{:S(2)}) collective-permute-start(bf16[512,1024]{1,0:T(8,128)(2,1)} %get-tuple-element.182), channel_id=1, source_target_pairs={{0,4},{4,0},{8,12},{12,8},{1,5},{5,1},{9,13},{13,9},{2,6},{6,2},{1... | collective-permute-start | bytes 3145736 | tf_op jit(solution)/shard_map/ppermute | solution.py:1085
  191.3 56.6 %collective-permute-start.28 = (s32[1]{0:T(128)}, s32[1]{0:T(128)}, u32[]{:S(2)}, u32[]{:S(2)}) collective-permute-start(s32[1]{0:T(128)} %param.24), channel_id=1, source_target_pairs={{0,16},{16,0},{1,17},{17,1},{2,18},{18,2},{3,19},{19,3},{4,20},{20... | collective-permute-start | bytes 20 | tf_op jit(solution)/shard_map/ppermute | solution.py:1128
  193.4 30.7 %collective-permute-start.24 = (bf16[512,1152]{1,0:T(8,128)(2,1)}, bf16[512,1152]{1,0:T(8,128)(2,1)}, u32[]{:S(2)}, u32[]{:S(2)}) collective-permute-start(bf16[512,1152]{1,0:T(8,128)(2,1)} %all-gather.5.cloned.1.call-done.own), channel_id=1, source_target_pairs={{0,8},{4,12},{8,0},{12,4},{1,9},{5,13},{9,1},{13,5},{2,10},{6,14},... | collective-permute-start | bytes 3538952 | tf_op jit(solution)/shard_map/ppermute | solution.py:1037
  195.2 28.9 %all-to-all-start.1 = ((bf16[8,256,128]{2,1,0:T(8,128)(2,1)}), bf16[8,256,128]{2,1,0:T(8,128)(2,1)}, u32[]{:S(2)}, u32[]{:S(2)}) async-start(bf16[8,256,128]{2,1,0:T(8,128)(2,1)} %get-tuple-element.172), calls=%async_computation.1 | async-start | bytes 1048576 | tf_op jit(solution)/shard_map/all_to_all | solution.py:749
  200.6 21.9 %collective-permute-start.23 = (bf16[256,1024]{1,0:T(8,128)(2,1)S(1)}, bf16[256,1024]{1,0:T(8,128)(2,1)}, u32[]{:S(2)}, u32[]{:S(2)}) collective-permute-start(bf16[256,1024]{1,0:T(8,128)(2,1)S(1)} %add_convert_fusion.1), channel_id=1, source_target_pairs={{0,1},{1,0},{2,3},{3,2},{4,5},{5,4},{6,7},{7,6},{8,9},{9,8},{10,11... | collective-permute-start | bytes 1572872 | tf_op jit(solution)/shard_map/ppermute | solution.py:1087
  224.1 14.0 %copy-start.13 = (bf16[256,1024]{1,0:T(8,128)(2,1)}, bf16[256,1024]{1,0:T(8,128)(2,1)S(1)}, u32[]{:S(2)}) copy-start(bf16[256,1024]{1,0:T(8,128)(2,1)S(1)} %add_convert_fusion.own) | copy-start | bytes 1572868
  224.1 22.0 %collective-permute-start.26 = (bf16[256,1024]{1,0:T(8,128)(2,1)S(1)}, bf16[256,1024]{1,0:T(8,128)(2,1)}, u32[]{:S(2)}, u32[]{:S(2)}) collective-permute-start(bf16[256,1024]{1,0:T(8,128)(2,1)S(1)} %add_convert_fusion.own), channel_id=1, source_target_pairs={{0,1},{1,2},{2,3},{4,5},{5,6},{6,7},{8,9},{9,10},{10,11},{12,13},{... | collective-permute-start | bytes 1572872 | tf_op jit(solution)/shard_map/ppermute | solution.py:1125
  227.3 18.8 %collective-permute-start.27 = (bf16[256,1024]{1,0:T(8,128)(2,1)S(1)}, bf16[256,1024]{1,0:T(8,128)(2,1)}, u32[]{:S(2)}, u32[]{:S(2)}) collective-permute-start(bf16[256,1024]{1,0:T(8,128)(2,1)S(1)} %add_convert_fusion.own), channel_id=1, source_target_pairs={{1,0},{2,1},{3,2},{5,4},{6,5},{7,6},{9,8},{10,9},{11,10},{13,12},{... | collective-permute-start | bytes 1572872 | tf_op jit(solution)/shard_map/ppermute | solution.py:1126
  228.6 17.6 %collective-permute-start.25 = (bf16[80,1024]{1,0:T(8,128)(2,1)S(1)}, bf16[80,1024]{1,0:T(8,128)(2,1)S(1)}, u32[]{:S(2)}, u32[]{:S(2)}) collective-permute-start(bf16[80,1024]{1,0:T(8,128)(2,1)S(1)} %pad_maximum_fusion.4), channel_id=1, source_target_pairs={{0,1},{1,0},{2,3},{3,2},{4,5},{5,4},{6,7},{7,6},{8,9},{9,8},{10,11... | collective-permute-start | bytes 491528 | tf_op jit(solution)/shard_map/ppermute | solution.py:1124
  231.3 19.4 %copy-start.18 = (bf16[48,1152]{1,0:T(8,128)(2,1)S(1)}, bf16[48,1152]{1,0:T(8,128)(2,1)}, u32[]{:S(2)}) copy-start(bf16[48,1152]{1,0:T(8,128)(2,1)} %get-tuple-element.196) | copy-start | bytes 331780
  238.1 41.6 %collective-permute-start.33 = (bf16[2048,128]{1,0:T(8,128)(2,1)}, bf16[2048,128]{1,0:T(8,128)(2,1)}, u32[]{:S(2)}, u32[]{:S(2)}) collective-permute-start(bf16[2048,128]{1,0:T(8,128)(2,1)} %get-tuple-element.201), channel_id=1, source_target_pairs={{8,0},{12,4},{9,1},{13,5},{10,2},{14,6},{11,3},{15,7},{24,16},{28,... | collective-permute-start | bytes 1572872 | tf_op jit(solution)/shard_map/ppermute | solution.py:1142
  246.2 28.4 %collective-permute-start.29 = (bf16[80,1024]{1,0:T(8,128)(2,1)S(1)}, bf16[80,1024]{1,0:T(8,128)(2,1)S(1)}, u32[]{:S(2)}, u32[]{:S(2)}) collective-permute-start(bf16[80,1024]{1,0:T(8,128)(2,1)S(1)} %add_convert_fusion.6), channel_id=1, source_target_pairs={{0,2},{1,3},{2,0},{3,1},{4,6},{5,7},{6,4},{7,5},{8,10},{9,11},{10,... | collective-permute-start | bytes 491528 | tf_op jit(solution)/shard_map/ppermute | solution.py:1153
  247.9 26.6 %collective-permute-start.31 = (bf16[256,1024]{1,0:T(8,128)(2,1)}, bf16[256,1024]{1,0:T(8,128)(2,1)S(1)}, u32[]{:S(2)}, u32[]{:S(2)}) collective-permute-start(bf16[256,1024]{1,0:T(8,128)(2,1)} %collective-permute-done.26.rest_0_), channel_id=1, source_target_pairs={{0,1},{1,2},{2,3},{4,5},{5,6},{6,7},{8,9},{9,10},{10,11},{12,13},{... | collective-permute-start | bytes 1572872 | tf_op jit(solution)/shard_map/ppermute | solution.py:1146
  249.4 25.2 %collective-permute-start.32 = (bf16[256,1024]{1,0:T(8,128)(2,1)}, bf16[256,1024]{1,0:T(8,128)(2,1)}, u32[]{:S(2)}, u32[]{:S(2)}) collective-permute-start(bf16[256,1024]{1,0:T(8,128)(2,1)} %collective-permute-done.27.rest_3_), channel_id=1, source_target_pairs={{1,0},{2,1},{3,2},{5,4},{6,5},{7,6},{9,8},{10,9},{11,10},{13,12},{... | collective-permute-start | bytes 1572872 | tf_op jit(solution)/shard_map/ppermute | solution.py:1147
  250.7 23.8 %collective-permute-start.30 = (bf16[48,1152]{1,0:T(8,128)(2,1)S(1)}, bf16[48,1152]{1,0:T(8,128)(2,1)S(1)}, u32[]{:S(2)}, u32[]{:S(2)}) collective-permute-start(bf16[48,1152]{1,0:T(8,128)(2,1)S(1)} %copy-done.18), channel_id=1, source_target_pairs={{0,2},{1,3},{2,0},{3,1},{4,6},{5,7},{6,4},{7,5},{8,10},{9,11},{10,... | collective-permute-start | bytes 331784 | tf_op jit(solution)/shard_map/ppermute | solution.py:1154
  274.6 14.4 %copy-start.28 = (bf16[256,1024]{1,0:T(8,128)(2,1)}, bf16[256,1024]{1,0:T(8,128)(2,1)S(1)}, u32[]{:S(2)}) copy-start(bf16[256,1024]{1,0:T(8,128)(2,1)S(1)} %collective-permute-done.31.rest_1_) | copy-start | bytes 1572868
  274.7 16.1 %collective-permute-start.34 = (bf16[256,1024]{1,0:T(8,128)(2,1)S(1)}, bf16[256,1024]{1,0:T(8,128)(2,1)}, u32[]{:S(2)}, u32[]{:S(2)}) collective-permute-start(bf16[256,1024]{1,0:T(8,128)(2,1)S(1)} %collective-permute-done.31.rest_1_), channel_id=1, source_target_pairs={{0,1},{1,2},{2,3},{4,5},{5,6},{6,7},{8,9},{9,10},{10,11},{12,13},{... | collective-permute-start | bytes 1572872 | tf_op jit(solution)/shard_map/ppermute | solution.py:1171
  278.1 13.6 %collective-permute-start.35 = (bf16[256,1024]{1,0:T(8,128)(2,1)}, bf16[256,1024]{1,0:T(8,128)(2,1)}, u32[]{:S(2)}, u32[]{:S(2)}) collective-permute-start(bf16[256,1024]{1,0:T(8,128)(2,1)} %collective-permute-done.32.rest_4_), channel_id=1, source_target_pairs={{1,0},{2,1},{3,2},{5,4},{6,5},{7,6},{9,8},{10,9},{11,10},{13,12},{... | collective-permute-start | bytes 1572872 | tf_op jit(solution)/shard_map/ppermute | solution.py:1172
  290.7 4.6 %collective-permute-start.40 = (bf16[192,1152]{1,0:T(8,128)(2,1)S(1)}, bf16[192,1152]{1,0:T(8,128)(2,1)S(1)}, u32[]{:S(2)}, u32[]{:S(2)}) collective-permute-start(bf16[192,1152]{1,0:T(8,128)(2,1)S(1)} %fusion.3), channel_id=1, source_target_pairs={{0,4},{4,0},{8,12},{12,8},{1,5},{5,1},{9,13},{13,9},{2,6},{6,2},{1... | collective-permute-start | bytes 1327112 | tf_op jit(solution)/shard_map/ppermute | solution.py:1216
  291.7 48.3 %all-to-all-start.2 = ((bf16[8,256,256]{2,1,0:T(8,128)(2,1)}), bf16[8,256,256]{2,1,0:T(8,128)(2,1)S(1)}, u32[]{:S(2)}, u32[]{:S(2)}) async-start(bf16[8,256,256]{2,1,0:T(8,128)(2,1)} %bitcast.73), calls=%async_computation.2 | async-start | bytes 2097152 | tf_op jit(solution)/shard_map/all_to_all | solution.py:749
  295.4 27.5 %collective-permute-start.41 = (bf16[192,1152]{1,0:T(8,128)(2,1)S(1)}, bf16[192,1152]{1,0:T(8,128)(2,1)S(1)}, u32[]{:S(2)}, u32[]{:S(2)}) collective-permute-start(bf16[192,1152]{1,0:T(8,128)(2,1)S(1)} %add_convert_fusion.4), channel_id=1, source_target_pairs={{0,8},{4,12},{8,0},{12,4},{1,9},{5,13},{9,1},{13,5},{2,10},{6,14},... | collective-permute-start | bytes 1327112 | tf_op jit(solution)/shard_map/ppermute | solution.py:1217
  312.1 27.9 %collective-permute-start.36 = (bf16[512,1152]{1,0:T(8,128)(2,1)}, bf16[512,1152]{1,0:T(8,128)(2,1)}, u32[]{:S(2)}, u32[]{:S(2)}) collective-permute-start(bf16[512,1152]{1,0:T(8,128)(2,1)} %all-gather.5.cloned.1.call-done.own), channel_id=1, source_target_pairs={{0,4},{4,0},{8,12},{12,8},{1,5},{5,1},{9,13},{13,9},{2,6},{6,2},{1... | collective-permute-start | bytes 3538952 | tf_op jit(solution)/shard_map/ppermute | solution.py:1150
  312.4 27.7 %collective-permute-start.37 = (bf16[512,1152]{1,0:T(8,128)(2,1)}, bf16[512,1152]{1,0:T(8,128)(2,1)}, u32[]{:S(2)}, u32[]{:S(2)}) collective-permute-start(bf16[512,1152]{1,0:T(8,128)(2,1)} %collective-permute-done.24.own_x), channel_id=1, source_target_pairs={{0,4},{4,0},{8,12},{12,8},{1,5},{5,1},{9,13},{13,9},{2,6},{6,2},{1... | collective-permute-start | bytes 3538952 | tf_op jit(solution)/shard_map/ppermute | solution.py:1151
  323.1 16.3 %collective-permute-start.42 = (bf16[192,1152]{1,0:T(8,128)(2,1)S(1)}, bf16[192,1152]{1,0:T(8,128)(2,1)S(1)}, u32[]{:S(2)}, u32[]{:S(2)}) collective-permute-start(bf16[192,1152]{1,0:T(8,128)(2,1)S(1)} %add_convert_fusion.3), channel_id=1, source_target_pairs={{0,16},{16,0},{1,17},{17,1},{2,18},{18,2},{3,19},{19,3},{4,20},{20... | collective-permute-start | bytes 1327112 | tf_op jit(solution)/shard_map/ppermute | solution.py:1225
  347.6 18.6 %collective-permute-start.38 = (bf16[256,1024]{1,0:T(8,128)(2,1)}, bf16[256,1024]{1,0:T(8,128)(2,1)S(1)}, u32[]{:S(2)}, u32[]{:S(2)}) collective-permute-start(bf16[256,1024]{1,0:T(8,128)(2,1)} %last.1.own), channel_id=1, source_target_pairs={{0,1},{1,2},{2,3},{4,5},{5,6},{6,7},{8,9},{9,10},{10,11},{12,13},{... | collective-permute-start | bytes 1572872 | tf_op jit(solution)/shard_map/ppermute | solution.py:1246
  350.9 15.3 %collective-permute-start.39 = (bf16[256,1024]{1,0:T(8,128)(2,1)}, bf16[256,1024]{1,0:T(8,128)(2,1)S(1)}, u32[]{:S(2)}, u32[]{:S(2)}) collective-permute-start(bf16[256,1024]{1,0:T(8,128)(2,1)} %last.1.own), channel_id=1, source_target_pairs={{1,0},{2,1},{3,2},{5,4},{6,5},{7,6},{9,8},{10,9},{11,10},{13,12},{... | collective-permute-start | bytes 1572872 | tf_op jit(solution)/shard_map/ppermute | solution.py:1247
  353.0 13.2 %collective-permute-start.43 = (bf16[2,48,128]{2,1,0:T(8,128)(2,1)S(1)}, bf16[2,48,128]{2,1,0:T(8,128)(2,1)S(1)}, u32[]{:S(2)}, u32[]{:S(2)}) collective-permute-start(bf16[2,48,128]{2,1,0:T(8,128)(2,1)S(1)} %dynamic-slice_maximum_fusion), channel_id=1, source_target_pairs={{0,1},{1,0},{2,3},{3,2},{4,5},{5,4},{6,7},{7,6},{8,9},{9,8},{10,11... | collective-permute-start | bytes 73736 | tf_op jit(solution)/shard_map/ppermute | solution.py:1250
  369.0 7.8 %collective-permute-start.48 = (bf16[2,48,128]{2,1,0:T(8,128)(2,1)S(1)}, bf16[2,48,128]{2,1,0:T(8,128)(2,1)S(1)}, u32[]{:S(2)}, u32[]{:S(2)}) collective-permute-start(bf16[2,48,128]{2,1,0:T(8,128)(2,1)S(1)} %add_convert_fusion.8), channel_id=1, source_target_pairs={{0,2},{1,3},{2,0},{3,1},{4,6},{5,7},{6,4},{7,5},{8,10},{9,11},{10,... | collective-permute-start | bytes 73736 | tf_op jit(solution)/shard_map/ppermute | solution.py:1254
  371.3 10.7 %collective-permute-start.44 = (bf16[256,1024]{1,0:T(8,128)(2,1)S(1)}, bf16[256,1024]{1,0:T(8,128)(2,1)S(1)}, u32[]{:S(2)}, u32[]{:S(2)}) collective-permute-start(bf16[256,1024]{1,0:T(8,128)(2,1)S(1)} %collective-permute-done.38.rest_0_), channel_id=1, source_target_pairs={{0,1},{1,2},{2,3},{4,5},{5,6},{6,7},{8,9},{9,10},{10,11},{12,13},{... | collective-permute-start | bytes 1572872 | tf_op jit(solution)/shard_map/ppermute | solution.py:1252
  372.8 13.3 %collective-permute-start.45 = (bf16[256,1024]{1,0:T(8,128)(2,1)S(1)}, bf16[256,1024]{1,0:T(8,128)(2,1)}, u32[]{:S(2)}, u32[]{:S(2)}) collective-permute-start(bf16[256,1024]{1,0:T(8,128)(2,1)S(1)} %collective-permute-done.39.rest_3_), channel_id=1, source_target_pairs={{1,0},{2,1},{3,2},{5,4},{6,5},{7,6},{9,8},{10,9},{11,10},{13,12},{... | collective-permute-start | bytes 1572872 | tf_op jit(solution)/shard_map/ppermute | solution.py:1253
  382.1 13.2 %copy-start.10 = (bf16[256,1024]{1,0:T(8,128)(2,1)}, bf16[256,1024]{1,0:T(8,128)(2,1)S(1)}, u32[]{:S(2)}) copy-start(bf16[256,1024]{1,0:T(8,128)(2,1)S(1)} %collective-permute-done.44.rest_1_) | copy-start | bytes 1572868
  386.1 11.1 %collective-permute-start.46 = (bf16[256,1024]{1,0:T(8,128)(2,1)S(1)}, bf16[256,1024]{1,0:T(8,128)(2,1)S(1)}, u32[]{:S(2)}, u32[]{:S(2)}) collective-permute-start(bf16[256,1024]{1,0:T(8,128)(2,1)S(1)} %collective-permute-done.44.rest_1_), channel_id=1, source_target_pairs={{0,1},{1,2},{2,3},{4,5},{5,6},{6,7},{8,9},{9,10},{10,11},{12,13},{... | collective-permute-start | bytes 1572872 | tf_op jit(solution)/shard_map/ppermute | solution.py:1291
  389.5 12.0 %collective-permute-start.47 = (bf16[256,1024]{1,0:T(8,128)(2,1)}, bf16[256,1024]{1,0:T(8,128)(2,1)S(1)}, u32[]{:S(2)}, u32[]{:S(2)}) collective-permute-start(bf16[256,1024]{1,0:T(8,128)(2,1)} %collective-permute-done.45.rest_4_), channel_id=1, source_target_pairs={{1,0},{2,1},{3,2},{5,4},{6,5},{7,6},{9,8},{10,9},{11,10},{13,12},{... | collective-permute-start | bytes 1572872 | tf_op jit(solution)/shard_map/ppermute | solution.py:1292
  (21 other events, 106.2 us)
Sparse Core Ops, SparseCore 0:
  63.1 34.9 all-gather.2
  140.7 30.0 all-gather.4
